TPU v7x, 128 devices: a whole 4x4x4 slice. The times are simulated.
128 devices in a mesh: seq: 32 (over x, z_lo, y), grp: 4 (over z_hi, core).
Axes of the slice: x: 4, y: 4, z: 4 (z_hi: 2, z_lo: 2; z = z_hi * 2 + z_lo), core: 2. Of those that a mesh axis runs over, the one named last changes fastest.
Arguments:
- query: bfloat16 [196608, 512], P('seq', 'grp'), may hold values from -6 to 6
- pos_emb: bfloat16 [196608, 512], P('seq', 'grp'), may hold values from -5 to 5
- pos_ids: int32 [196608], P('seq'), may hold values from 0 to 1048575
- lengths: int32 [32, 32], P('seq'), may hold values from 1 to 192, 2048 in all within a row
- negatives: bfloat16 [2048, 512], P(('seq', 'grp')), may hold values from -100 to 100
- neg_ids: int32 [2048], P(('seq', 'grp')), may hold values from 0 to 1048575
Outputs:
- grad_query: bfloat16 [196608, 512], P('seq', 'grp')
- grad_items: float32 [2048, 512], P(('seq', 'grp'))
Inputs may be any that keep to these rules, and one draw needn't show every extreme that they name: Each row of 32 lengths sums to 2048, and every row holds one length of exactly 192.
All inputs are finite; a program needn't handle non-finite values.
Results may differ from a plain program's by a relative error of at most 0.0037.
Values may be sent and summed in bfloat16 or wider, within the bound.
No kernel may reach another device: no remote copies, remote signals or barrier semaphores. Data moves between devices by JAX's collectives and lax.ppermute only.
A program may use at most 64 MiB of HBM per device.

v0:
```python
from functools import partial

import jax
import jax.numpy as jnp
from jax import lax
from jax.sharding import PartitionSpec as P

HIST_DEV = 8
MEANLEN = 64
MAXLEN = 192


def history_table(length_row):
    hist_ends = jnp.cumsum(length_row)
    hist_starts = hist_ends - length_row
    return (hist_ends, hist_starts)


def slot_targets(length_row, slot_rows):
    hist_ends, hist_starts = history_table(length_row)
    slot_index = jnp.arange(slot_rows, dtype=jnp.int32)
    history = slot_index // MAXLEN
    offset = slot_index - history * MAXLEN
    picked = history[:, None] == jnp.arange(length_row.shape[0], dtype=jnp.int32)[None, :]
    first_row = jnp.sum(jnp.where(picked, hist_starts[None, :], 0), axis=1)
    hist_size = jnp.sum(jnp.where(picked, length_row[None, :], 0), axis=1)
    return (first_row + offset, offset < hist_size)


def block_grads(item_pool, item_ids, inputs):
    rows_q, rows_p, rows_id, live_rows = inputs
    scores = lax.dot_general(
        rows_q, item_pool, (((1,), (1,)), ((), ())), preferred_element_type=jnp.float32
    )
    positive = jnp.sum(rows_q.astype(jnp.float32) * rows_p.astype(jnp.float32), axis=1)
    collide = rows_id[:, None] == item_ids[None, :]
    masked = jnp.where(collide, -jnp.inf, scores)
    row_top = jnp.maximum(jnp.max(masked, axis=1), positive)
    denominator = jnp.exp(positive - row_top) + jnp.sum(jnp.exp(masked - row_top[:, None]), axis=1)
    log_total = row_top + jnp.log(denominator)
    kept_mask = live_rows[:, None] & jnp.logical_not(collide)
    weights = jnp.where(kept_mask, jnp.exp(scores - log_total[:, None]), 0.0).astype(jnp.bfloat16)
    own_term = jnp.where(live_rows, jnp.exp(positive - log_total) - 1.0, 0.0)
    grad_rows = jnp.dot(weights, item_pool, preferred_element_type=jnp.float32) + own_term[
        :, None
    ] * rows_p.astype(jnp.float32)
    return (weights, grad_rows.astype(jnp.bfloat16))


def shards(query, pos_emb, pos_ids, lengths, negatives, neg_ids):
    groups = lax.axis_size("grp")
    member = lax.axis_index("grp")
    lengths_row = lengths[0]
    slot_rows = query.shape[0]
    rows_q, rows_p = (
        lax.all_to_all(query, "grp", split_axis=0, concat_axis=1, tiled=True),
        lax.all_to_all(pos_emb, "grp", split_axis=0, concat_axis=1, tiled=True),
    )
    capacity = slot_rows // groups
    rows_id = lax.dynamic_slice_in_dim(pos_ids, member * capacity, capacity)
    unused_at, live_all = slot_targets(lengths_row, slot_rows)
    live_rows = lax.dynamic_slice_in_dim(live_all, member * capacity, capacity)
    item_pool, item_ids = (
        lax.all_gather(negatives, ("seq", "grp"), axis=0, tiled=True),
        lax.all_gather(neg_ids, ("seq", "grp"), axis=0, tiled=True),
    )
    block_rows = HIST_DEV * MEANLEN
    block_count = rows_q.shape[0] // block_rows
    stacked = (
        rows_q.reshape(block_count, block_rows, rows_q.shape[1]),
        rows_p.reshape(block_count, block_rows, rows_p.shape[1]),
        rows_id.reshape(block_count, block_rows),
        live_rows.reshape(block_count, block_rows),
    )
    weights, grad_rows = lax.map(partial(block_grads, item_pool, item_ids), stacked)
    weights = weights.reshape(block_count * block_rows, weights.shape[2])
    grad_rows = grad_rows.reshape(block_count * block_rows, grad_rows.shape[2])
    grad_items = lax.psum_scatter(
        lax.dot_general(
            weights, rows_q, (((0,), (0,)), ((), ())), preferred_element_type=jnp.float32
        ),
        ("seq", "grp"),
        scatter_dimension=0,
        tiled=True,
    )
    grad_query = lax.all_to_all(grad_rows, "grp", split_axis=1, concat_axis=0, tiled=True)
    return (grad_query, grad_items)


def solution(mesh):
    return jax.shard_map(
        shards,
        mesh=mesh,
        in_specs=(
            P("seq", "grp"),
            P("seq", "grp"),
            P("seq"),
            P("seq", None),
            P(("seq", "grp"), None),
            P(("seq", "grp")),
        ),
        out_specs=(P("seq", "grp"), P(("seq", "grp"), None)),
        check_vma=False,
    )
```

profile of v0, /device:TPU:0, one launch (start us, length us, event | category | flops | bytes accessed | tf_op | source)
XLA Modules:
  0.0 918.1 jit_solution(1053459192295733919)
XLA Ops:
  7.9 27.4 %all_to_all.54 = bf16[4,1536,128]{2,1,0:T(8,128)(2,1)S(1)} all-to-all(bf16[4,1536,128]{2,1,0:T(8,128)(2,1)} %bitcast.53), channel_id=1, replica_groups=mesh['seq'=32,'grp'=4] {'grp'}, dimensions={0} | all-to-all | bytes 3145728 | tf_op jit(solution)/shard_map/all_to_all | solution.py:56
  35.4 4.4 all-to-all-start.1
  41.3 76.4 %all-reduce = s32[2048]{0:T(1024)S(1)} all-reduce(s32[2048]{0:T(1024)S(1)} %dynamic-update-slice), channel_id=1, replica_groups=mesh['seq'=32,'grp'=4] {'seq','grp'}, use_global_device_ids=true, to_apply=%add | all-reduce | flops 2048 | bytes 16384
  117.6 8.2 copy.17
  125.8 2.5 reshape.95
  128.3 8.5 copy.18
  136.9 3.6 reshape.96
  140.5 1.6 copy.16
  142.1 83.7 %all-gather.2.cloned.1.call-done = bf16[2048,512]{1,0:T(8,128)(2,1)} async-done(((bf16[16,512]{1,0:T(8,128)(2,1)}), bf16[2048,512]{1,0:T(8,128)(2,1)}) %all-gather.2.cloned.1.call-update) | async-done | bytes 2097168 | tf_op jit(solution)/shard_map/all_gather | solution.py:64
  225.8 32.7 %while.14 = (s32[]{:T(128)}, bf16[3,512,2048]{2,1,0:T(8,128)(2,1)}, bf16[3,512,512]{2,1,0:T(8,128)(2,1)}, pred[3,512]{1,0:T(4,128)(4,1)S(1)}, s32[3,512]{1,0:T(4...) while((s32[]{:T(128)}, bf16[3,512,2048]{2,1,0:T(8,128)(2,1)}, ...), condition=%wide.region_5.6_spmd, body=%wide.region_1.5_spmd.sunk | while | flops 2169505792 | bytes 53032168 | solution.py:75
  225.8 3.1 fusion.25
  231.0 2.0 fusion.27
  234.1 2.6 bitcast_dynamic-update-slice_fusion.2
  236.7 3.1 fusion.25
  241.9 2.0 fusion.27
  245.0 2.5 bitcast_dynamic-update-slice_fusion.2
  247.6 3.1 fusion.25
  252.8 2.0 fusion.27
  255.9 2.6 bitcast_dynamic-update-slice_fusion.2
  258.5 8.1 fusion.13
  266.6 1.4 copy-done.4
  268.6 26.1 %all_to_all.55 = bf16[1536,4,128]{2,0,1:T(8,128)(2,1)S(1)} all-to-all(bf16[1536,4,128]{2,0,1:T(8,128)(2,1)S(1)} %copy.19), channel_id=1, replica_groups=mesh['seq'=32,'grp'=4] {'grp'}, dimensions={1} | all-to-all | bytes 3145728 | tf_op jit(solution)/shard_map/all_to_all | solution.py:86
  294.7 615.4 %reduce-scatter.2.cloned.1.call-done = f32[16,512]{1,0:T(8,128)} async-done(((f32[2048,512]{1,0:T(8,128)}), f32[16,512]{1,0:T(8,128)}) %reduce-scatter.2.cloned.1.call-update) | async-done | bytes 32784 | tf_op jit(solution)/shard_map/reduce_scatter | solution.py:78
  910.1 1.1 copy.36
  (66 shorter events, 12.4 us)
Async XLA Ops:
  7.2 32.7 %copy-start.5 = (s32[1,32]{1,0:T(1,128)S(1)}, s32[1,32]{1,0:T(1,128)}, u32[]{:S(2)}) copy-start(s32[1,32]{1,0:T(1,128)} %param.11) | copy-start | bytes 388
  7.2 33.8 %copy-start.7 = (s32[16]{0:T(128)S(1)}, s32[16]{0:T(128)}, u32[]{:S(2)}) copy-start(s32[16]{0:T(128)} %param.13) | copy-start | bytes 196
  7.2 218.6 %all-gather.2.cloned.1.call-start = ((), (), s32[]{:S(2)}) async-start(), calls=%async_computation.4 | async-start | bytes 2113536 | tf_op jit(solution)/shard_map/all_gather | solution.py:64
  35.4 93.0 %all-to-all-start.1 = ((bf16[4,1536,128]{2,1,0:T(8,128)(2,1)}), bf16[4,1536,128]{2,1,0:T(8,128)(2,1)}, u32[]{:S(2)}, u32[]{:S(2)}) async-start(bf16[4,1536,128]{2,1,0:T(8,128)(2,1)} %bitcast.54), calls=%async_computation.1 | async-start | bytes 3145728 | tf_op jit(solution)/shard_map/all_to_all | solution.py:57
  39.8 870.4 %reduce-scatter.2.cloned.1.call-start = ((), (), s32[]{:S(2)}) async-start(), calls=%async_computation.5 | async-start | bytes 4227072 | tf_op jit(solution)/shard_map/reduce_scatter | solution.py:78
  225.8 32.7 %copy-start.1 = (bf16[4,1536,128]{1,2,0:T(8,128)(2,1)S(1)}, bf16[4,1536,128]{1,2,0:T(8,128)(2,1)}, u32[]{:S(2)}) copy-start(bf16[4,1536,128]{1,2,0:T(8,128)(2,1)} %copy.16) | copy-start | bytes 4718596
  225.8 3.2 copy-start
  228.9 1.4 copy-start.2
  228.9 2.1 copy-start.6
  233.0 1.1 copy-start.3
  236.7 3.1 copy-start
  239.8 1.4 copy-start.2
  239.8 2.1 copy-start.6
  243.9 1.1 copy-start.3
  247.6 3.1 copy-start
  250.7 1.4 copy-start.2
  250.7 2.1 copy-start.6
  254.7 1.1 copy-start.3
  266.5 1.4 copy-start.4
Sparse Core Ops, SparseCore 0:
  9.7 215.9 all-gather.1
  266.7 643.4 reduce-scatter.1
where the time goes:
time: 919 us; the launch traced here: 918 us
  waiting for transfers between devices  700 us (76%)
  blocking collectives  130 us (14%)
  local copies, waits for them, and re-layouts  34.6 us (4%)
  matrix products  23.4 us (3%)
  between operations  14.1 us (2%)
  other arithmetic  11.6 us (1%)
    reduce_scatter x1, waiting for transfers between devices, shards(): lax.psum_scatter(lax.dot_general(weights, rows_q, (((0,), (0,)), ((), ())...  615 us
    all_gather x1, waiting for transfers between devices, shards(): lax.all_gather(negatives, ('seq', 'grp'), axis=0, tiled=True)  83.7 us
    unnamed x1, blocking collectives  76.4 us
    all_to_all x1, blocking collectives, shards(): lax.all_to_all(query, 'grp', split_axis=0, concat_axis=1, tiled=True)  27.4 us
    all_to_all x1, blocking collectives, shards(): lax.all_to_all(grad_rows, 'grp', split_axis=1, concat_axis=0, tiled=True)  26.1 us
  transfers between devices with their start and end apart: 3, of which 2 were waited for; matrix products, arithmetic and copies ran while one was open for 3% of the time, Pallas kernels for 0%

commit v1 on v0

v1 whole, which is shorter than its diff:
```python
from functools import partial

import jax
import jax.numpy as jnp
from jax import lax
from jax.experimental import pallas as pl
from jax.experimental.pallas import tpu as pltpu
from jax.sharding import PartitionSpec as P

MAXLEN = 192
LANES = 128
CHUNK = 64
FLOOR = -1e30
MASKED = -3e38
F32 = jnp.float32
BF16 = jnp.bfloat16
VMEM_BYTES = 56 * 1024 * 1024


def params():
    return pltpu.CompilerParams(vmem_limit_bytes=VMEM_BYTES)


def whole():
    return pl.BlockSpec(memory_space=pltpu.VMEM)


def small():
    return pl.BlockSpec(memory_space=pltpu.SMEM)


def dot(a, b, da, db):
    return lax.dot_general(a, b, (((da,), (db,)), ((), ())), preferred_element_type=F32)


def copy_rows(len_ref, src_ref, packed):
    start = jnp.int32(0)
    for h in range(len_ref.shape[1]):
        size = len_ref[0, h]
        for c in range(0, MAXLEN, CHUNK):

            @pl.when(size > c)
            def _():
                packed[pl.ds(start + c, CHUNK), :] = src_ref[h * MAXLEN + c : h * MAXLEN + c + CHUNK, :].astype(F32)

        start = start + size


def pack_query(len_ref, q_ref, qp_ref, packed):
    copy_rows(len_ref, q_ref, packed)
    qp_ref[...] = packed[: qp_ref.shape[0], :].astype(BF16)


def pack_positive(len_ref, p_ref, id_ref, qp_ref, pp_ref, part_ref, idp_ref, packed, ids):
    rows = pp_ref.shape[0]
    copy_rows(len_ref, p_ref, packed)
    held = packed[:rows, :]
    pp_ref[...] = held.astype(BF16)
    product = held * qp_ref[...].astype(F32)
    high = product.astype(BF16)
    low = (product - high.astype(F32)).astype(BF16)
    ones = jnp.ones((16, LANES), BF16)
    part_ref[...] = (dot(ones, high, 1, 1) + dot(ones, low, 1, 1))[:1, :]
    lane = lax.broadcasted_iota(jnp.int32, (1, LANES), 1)
    start = jnp.int32(0)
    for h in range(len_ref.shape[1]):
        row, off = divmod(h * MAXLEN, LANES)
        at = start + (LANES - off)
        target = at // LANES
        shift = at - target * LANES
        first = pltpu.roll(id_ref[row : row + 1, :], shift, 1)
        second = pltpu.roll(id_ref[row + 1 : row + 2, :], shift, 1)
        kept0 = ids[pl.ds(target, 1), :]
        kept1 = ids[pl.ds(target + 1, 1), :]
        ids[pl.ds(target, 1), :] = jnp.where(lane >= shift + off, first, kept0)
        ids[pl.ds(target + 1, 1), :] = jnp.where(
            lane + LANES >= shift + off, jnp.where(lane >= shift, second, first), kept1
        )
        ids[pl.ds(target + 2, 1), :] = second
        start = start + len_ref[0, h]
    for k in range(rows // LANES):
        idp_ref[:, k * LANES : (k + 1) * LANES] = ids[k + 1 : k + 2, :].astype(F32)


def block_of(order, step):
    return pl.ds(pl.multiple_of((order ^ step) * LANES, LANES), LANES)


def scores_kernel(neg_ref, q0_ref, q1_ref, q2_ref, q3_ref, idp_ref, part_ref, qfull_ref, e_ref, stat_ref, negid):
    member = lax.axis_index("grp")
    width = 4 * LANES

    @pl.when(pl.program_id(0) == 0)
    def _():
        lane = lax.broadcasted_iota(jnp.int32, (1, LANES), 1)
        place = jnp.where(lane == 0, 65536.0, jnp.where(lane == 1, 256.0, jnp.where(lane == 2, 1.0, 0.0)))
        value = jnp.sum(neg_ref[:, width : width + LANES].astype(F32) * place, axis=1, keepdims=True)
        negid[...] = jnp.broadcast_to(value, negid.shape)

    for k, ref in enumerate((q0_ref, q1_ref, q2_ref, q3_ref)):
        qfull_ref[:, block_of(member, k)] = ref[...]
    scores = dot(neg_ref[:, :width], qfull_ref[...], 1, 1)
    for k in range(scores.shape[1] // LANES):
        at = slice(k * LANES, (k + 1) * LANES)
        part = jnp.where(negid[...] == idp_ref[:, at], MASKED, scores[:, at])
        top = jnp.maximum(jnp.max(part, axis=0, keepdims=True), FLOOR)
        e = jnp.exp(part - top)
        e_ref[:, at] = e
        stat_ref[0:1, at] = top
        stat_ref[1:2, at] = jnp.sum(e, axis=0, keepdims=True)
        stat_ref[2:3, at] = part_ref[:, at]
        stat_ref[3:4, at] = part_ref[:, at]


def rows_kernel(neg_ref, e_ref, keep_ref, send_ref, turned):
    member = lax.axis_index("grp")
    half = 2 * LANES

    @pl.when(pl.program_id(0) == 0)
    def _():
        for k, step in enumerate((0, 2, 1, 3)):
            turned[k * LANES : (k + 1) * LANES, :] = neg_ref[:, block_of(member, step)].T

    out = dot(turned[...], e_ref[...].astype(BF16), 1, 0)
    keep_ref[...] = out[:half, :]
    send_ref[...] = out[half:, :].astype(BF16)


def totals(refs):
    positive = refs[0][2:3, :] + refs[1][2:3, :] + refs[2][2:3, :] + refs[3][2:3, :]
    top = positive
    for ref in refs:
        top = jnp.maximum(top, ref[0:1, :])
    total = jnp.exp(positive - top)
    for ref in refs:
        total = total + ref[1:2, :] * jnp.exp(ref[0:1, :] - top)
    return positive, top + jnp.log(total)


def combine_kernel(s0, s1, s2, s3, keep_ref, recv_ref, own_ref, send_ref, term_ref):
    positive, log_total = totals((s0, s1, s2, s3))
    mine = jnp.exp(s0[0:1, :] - log_total)
    other = jnp.exp(s1[0:1, :] - log_total)
    own_ref[...] = keep_ref[:LANES, :] * mine + recv_ref[:LANES, :].astype(F32) * other
    send_ref[...] = (keep_ref[LANES:, :] * mine + recv_ref[LANES:, :].astype(F32) * other).astype(BF16)
    term_ref[...] = jnp.exp(positive - log_total) - 1.0


def items_kernel(s0, s1, s2, s3, e_ref, q_ref, out_ref, acc):
    step = pl.program_id(0)
    _, log_total = totals((s0, s1, s2, s3))
    weights = (e_ref[...] * jnp.exp(s0[0:1, :] - log_total)).astype(BF16)
    part = dot(weights, q_ref[...], 1, 0)

    @pl.when(step == 0)
    def _():
        acc[...] = part

    @pl.when(step > 0)
    def _():
        acc[...] += part

    @pl.when(step == pl.num_programs(0) - 1)
    def _():
        out_ref[...] = acc[...].astype(BF16)


def unpack_kernel(len_ref, own_ref, recv_ref, term_ref, pp_ref, out_ref, packed):
    rows = own_ref.shape[1]
    for k in range(rows // LANES):
        at = slice(k * LANES, (k + 1) * LANES)
        block = (own_ref[:, at] + recv_ref[:, at].astype(F32)).T
        term = jnp.broadcast_to(term_ref[:, at], (LANES, LANES)).T
        packed[at, :] = block + term * pp_ref[at, :].astype(F32)
    index = lax.broadcasted_iota(jnp.int32, (CHUNK, LANES), 0)
    start = jnp.int32(0)
    for h in range(len_ref.shape[1]):
        size = len_ref[0, h]
        for c in range(0, MAXLEN, CHUNK):
            at = slice(h * MAXLEN + c, h * MAXLEN + c + CHUNK)

            @pl.when(size > c)
            def _():
                out_ref[at, :] = jnp.where(index < size - c, packed[pl.ds(start + c, CHUNK), :], 0.0).astype(BF16)

            @pl.when(size <= c)
            def _():
                out_ref[at, :] = jnp.zeros((CHUNK, LANES), BF16)

        start = start + size


def swap(value, step, groups):
    return lax.ppermute(value, "grp", [(g, g ^ step) for g in range(groups)])


def shards(live, query, pos_emb, pos_ids, lengths, negatives, neg_ids):
    groups = lax.axis_size("grp")
    seqs = lax.axis_size("seq")
    own_neg, width = negatives.shape
    slots = query.shape[0]
    negs = own_neg * seqs
    sds = jax.ShapeDtypeStruct
    tile = min(512, live)
    steps = live // tile

    digits = jnp.stack([neg_ids // 65536, (neg_ids // 256) % 256, neg_ids % 256], axis=1).astype(BF16)
    row = jnp.concatenate([negatives, jnp.pad(digits, ((0, 0), (0, LANES - 3)))], axis=1)

    qp = pl.pallas_call(
        pack_query,
        out_shape=sds((live, LANES), BF16),
        in_specs=[small(), whole()],
        out_specs=whole(),
        scratch_shapes=[pltpu.VMEM((live + MAXLEN, LANES), F32)],
        compiler_params=params(),
        name="pack_query",
    )(lengths, query)
    q2 = swap(qp, 2, groups)
    q1 = swap(qp, 1, groups)
    q3 = swap(q2, 1, groups)

    pp, part, idp = pl.pallas_call(
        pack_positive,
        out_shape=(sds((live, LANES), BF16), sds((1, live), F32), sds((1, live), F32)),
        in_specs=[small(), whole(), whole(), whole()],
        out_specs=(whole(), whole(), whole()),
        scratch_shapes=[
            pltpu.VMEM((live + MAXLEN, LANES), F32),
            pltpu.VMEM((live // LANES + 8, LANES), jnp.int32),
        ],
        compiler_params=params(),
        name="pack_positive",
    )(lengths, pos_emb, pos_ids.reshape(slots // LANES, LANES), qp)

    pool = lax.all_to_all(jnp.tile(row, (seqs, 1)), "seq", split_axis=0, concat_axis=0, tiled=True)

    tall = pl.BlockSpec((tile, LANES), lambda i: (i, 0))
    line = pl.BlockSpec((1, tile), lambda i: (0, i))
    e_spec = pl.BlockSpec((negs, tile), lambda i: (0, i))
    stat_spec = pl.BlockSpec((4, tile), lambda i: (0, i))
    pool_spec = pl.BlockSpec((negs, width + LANES), lambda i: (0, 0))
    qfull, e, stat = pl.pallas_call(
        scores_kernel,
        grid=(steps,),
        out_shape=(sds((live, width), BF16), sds((negs, live), F32), sds((4, live), F32)),
        in_specs=[pool_spec, tall, tall, tall, tall, line, line],
        out_specs=(pl.BlockSpec((tile, width), lambda i: (i, 0)), e_spec, stat_spec),
        scratch_shapes=[pltpu.VMEM((negs, LANES), F32)],
        compiler_params=params(),
        name="scores",
    )(pool, qp, q1, q2, q3, idp, part)

    stats = (stat, swap(stat, 1, groups), swap(stat, 2, groups), swap(stat, 3, groups))

    keep, send = pl.pallas_call(
        rows_kernel,
        grid=(steps,),
        out_shape=(sds((2 * LANES, live), F32), sds((2 * LANES, live), BF16)),
        in_specs=[pool_spec, e_spec],
        out_specs=(pl.BlockSpec((2 * LANES, tile), lambda i: (0, i)), pl.BlockSpec((2 * LANES, tile), lambda i: (0, i))),
        scratch_shapes=[pltpu.VMEM((width, negs), BF16)],
        compiler_params=params(),
        name="row_products",
    )(pool, e)
    recv = swap(send, 1, groups)

    own, onward, term = pl.pallas_call(
        combine_kernel,
        out_shape=(sds((LANES, live), F32), sds((LANES, live), BF16), sds((1, live), F32)),
        in_specs=[whole()] * 6,
        out_specs=(whole(), whole(), whole()),
        compiler_params=params(),
        name="combine",
    )(*stats, keep, recv)
    recv2 = swap(onward, 2, groups)

    items = pl.pallas_call(
        items_kernel,
        grid=(steps,),
        out_shape=sds((negs, width), BF16),
        in_specs=[stat_spec] * 4 + [e_spec, pl.BlockSpec((tile, width), lambda i: (i, 0))],
        out_specs=pl.BlockSpec((negs, width), lambda i: (0, 0)),
        scratch_shapes=[pltpu.VMEM((negs, width), F32)],
        compiler_params=params(),
        name="item_products",
    )(*stats, e, qfull)
    shares = lax.all_to_all(items, "seq", split_axis=0, concat_axis=0, tiled=True)
    grad_items = jnp.sum(shares.reshape(seqs, own_neg, width).astype(F32), axis=0)

    grad_query = pl.pallas_call(
        unpack_kernel,
        out_shape=sds((slots, LANES), BF16),
        in_specs=[small()] + [whole()] * 4,
        out_specs=whole(),
        scratch_shapes=[pltpu.VMEM((live + MAXLEN, LANES), F32)],
        compiler_params=params(),
        name="unpack",
    )(lengths, own, recv2, term, pp)
    return grad_query, grad_items


def solution(mesh, live=2048):
    return jax.shard_map(
        partial(shards, live),
        mesh=mesh,
        in_specs=(
            P("seq", "grp"),
            P("seq", "grp"),
            P("seq"),
            P("seq", None),
            P(("seq", "grp"), None),
            P(("seq", "grp")),
        ),
        out_specs=(P("seq", "grp"), P(("seq", "grp"), None)),
        check_vma=False,
    )
```

time: 919 us -> 92.6 us (0.10)
  waiting for transfers between devices: 700 us -> 28.5 us
  blocking collectives: 130 us -> 0 us
  Pallas kernels: 0 us -> 31.7 us
  local copies, waits for them, and re-layouts: 34.6 us -> 4.4 us
  matrix products: 23.4 us -> 0 us
  starting transfers between devices: 4.47 us -> 25.9 us
  between operations: 14.1 us -> 0.74 us
  other arithmetic: 11.6 us -> 0.74 us
    reduce_scatter x1 -> x0, waiting for transfers between devices: 615 us -> none  [shards(): lax.psum_scatter(lax.dot_general(weights, rows_q, (((0,), (0,)), ((), ())...]
    all_gather x1 -> x0, waiting for transfers between devices: 83.7 us -> none  [shards(): lax.all_gather(negatives, ('seq', 'grp'), axis=0, tiled=True)]
    unnamed x1 -> x0, blocking collectives: 76.4 us -> none
    all_to_all x2 -> x0, blocking collectives: 53.6 us -> none  [the longest x1 27.4 us: shards(): lax.all_to_all(query, 'grp', split_axis=0, concat_axis=1, tiled=True)]
    pallas_call x0 -> x7, Pallas kernels: none -> 31.7 us  [the longest x1 6.6 us: shards(): pl.pallas_call(scores_kernel, grid=(steps,), out_shape=(sds((live, width)...]
    dot_general x7 -> x0, matrix products: 23.4 us -> none  [the longest x3 9.34 us: block_grads(): lax.dot_general(rows_q, item_pool, (((1,), (1,)), ((), ())), preferred_el...]
    ppermute x0 -> x8, waiting for transfers between devices: none -> 21.9 us  [swap(): return lax.ppermute(value, 'grp', [(g, g ^ step) for g in range(groups)])]
    all_to_all x5 -> x0, local copies, waits for them, and re-layouts: 18.9 us -> none  [the longest x2 9.76 us: shards(): lax.all_to_all(query, 'grp', split_axis=0, concat_axis=1, tiled=True)]
  transfers between devices with their start and end apart: 3 -> 10, of which waited for: 2 -> 6; matrix products, arithmetic and copies ran while one was open for 3% -> 2% of each run, Pallas kernels for 0% -> 13%
where the time goes in v1:
time: 92.6 us; the launch traced here: 91.9 us
  Pallas kernels  31.7 us (34%)
  waiting for transfers between devices  28.5 us (31%)
  starting transfers between devices  25.9 us (28%)
  local copies, waits for them, and re-layouts  4.4 us (5%)
    ppermute x8, waiting for transfers between devices, swap(): return lax.ppermute(value, 'grp', [(g, g ^ step) for g in range(groups)])  21.9 us
    all_to_all x1, starting transfers between devices, shards(): lax.all_to_all(items, 'seq', split_axis=0, concat_axis=0, tiled=True)  9.11 us
    ppermute x8, starting transfers between devices, swap(): return lax.ppermute(value, 'grp', [(g, g ^ step) for g in range(groups)])  8.99 us
    all_to_all x1, starting transfers between devices, shards(): lax.all_to_all(jnp.tile(row, (seqs, 1)), 'seq', split_axis=0, concat_axis...  7.77 us
    pallas_call x1, Pallas kernels, shards(): pl.pallas_call(scores_kernel, grid=(steps,), out_shape=(sds((live, width)...  6.6 us
    pallas_call x1, Pallas kernels, shards(): pl.pallas_call(items_kernel, grid=(steps,), out_shape=sds((negs, width),...  5.53 us
    pallas_call x1, Pallas kernels, shards(): pl.pallas_call(rows_kernel, grid=(steps,), out_shape=(sds((2 * LANES, liv...  5.51 us
    all_to_all x1, waiting for transfers between devices, shards(): lax.all_to_all(items, 'seq', split_axis=0, concat_axis=0, tiled=True)  5.46 us
  transfers between devices with their start and end apart: 10, of which 6 were waited for; matrix products, arithmetic and copies ran while one was open for 2% of the time, Pallas kernels for 13%

profile of v1, /device:TPU:0, one launch (start us, length us, event | category | flops | bytes accessed | tf_op | source)
XLA Modules:
  0.0 91.9 jit_solution(2945367605696095893)
XLA Ops:
  0.7 2.9 %pack_query.1.qp_ref.q0_ref = bf16[2048,128]{1,0:T(8,128)(2,1)} custom-call(s32[1,32]{1,0:T(1,128)} %len_ref.5, bf16[6144,128]{1,0:T(8,128)(2,1)} %q_ref.1), custom_call_target="tpu_custom_call" | custom-call | tf_op jit(solution)/shard_map/pack_query/pallas_call | solution.py:210
  3.5 4.0 %collective-permute-start.1 = (bf16[2048,128]{1,0:T(8,128)(2,1)}, bf16[2048,128]{1,0:T(8,128)(2,1)S(1)}, u32[]{:S(2)}, u32[]{:S(2)}) collective-permute-start(bf16[2048,128]{1,0:T(8,128)(2,1)} %pack_query.1.qp_ref.q0_ref), channel_id=1, source_target_pairs={{0,2},{1,3},{2,0},{3,1},{4,6},{5,7},{6,4},{7,5},{8,10},{9,11},{10,... | collective-permute-start | bytes 1572872 | tf_op jit(solution)/shard_map/ppermute | solution.py:194
  7.6 0.9 tile.2
  8.5 7.8 %all-to-all-start = ((bf16[32,16,640]{2,1,0:T(8,128)(2,1)}), bf16[32,16,640]{2,1,0:T(8,128)(2,1)S(1)}, u32[]{:S(2)}, u32[]{:S(2)}) async-start(bf16[32,16,640]{2,1,0:T(8,128)(2,1)} %tile.2), calls=%async_computation | async-start | bytes 1310720 | tf_op jit(solution)/shard_map/all_to_all | solution.py:236
  16.4 7.9 %collective-permute-done.1.q2_ref = bf16[2048,128]{1,0:T(8,128)(2,1)S(1)} collective-permute-done((bf16[2048,128]{1,0:T(8,128)(2,1)}, bf16[2048,128]{1,0:T(8,128)(2,1)S(1)}, u32[]{:S(2)}, u32[]{:S(2)}) %collective-permute-start.1) | collective-permute-done | bytes 524320 | tf_op jit(solution)/shard_map/ppermute | solution.py:194
  24.3 3.5 %pack_positive.1 = (bf16[2048,128]{1,0:T(8,128)(2,1)}, f32[1,2048]{1,0:T(1,128)}, f32[1,2048]{1,0:T(1,128)}) custom-call(s32[1,32]{1,0:T(1,128)} %len_ref.5, bf16[6144,128]{1,0:T(8,128)(2,1)} %p_ref.1, s32[48,128]{1,0:T(8,128)} %bitcast.12, bf16[2048,128]{1,0:T(8,128)(2,1)} %pack_query.1.qp_ref.q0_ref), custom_call_target="tpu_custom_call" | custom-call | tf_op jit(solution)/shard_map/pack_positive/pallas_call | solution.py:223
  27.8 1.2 %all-to-all-done = bf16[32,16,640]{2,1,0:T(8,128)(2,1)S(1)} async-done(((bf16[32,16,640]{2,1,0:T(8,128)(2,1)}), bf16[32,16,640]{2,1,0:T(8,128)(2,1)S(1)}, u32[]{:S(2)}, u32[]{:S(2)}) %all-to-all-start) | async-done | bytes 655392 | tf_op jit(solution)/shard_map/all_to_all | solution.py:236
  29.0 0.9 copy-done
  29.9 6.6 %scores.1 = (bf16[2048,512]{1,0:T(8,128)(2,1)}, f32[512,2048]{1,0:T(8,128)}, f32[4,2048]{1,0:T(4,128)}) custom-call(bf16[512,640]{1,0:T(8,128)(2,1)} %bitcast.9, bf16[2048,128]{1,0:T(8,128)(2,1)} %pack_query.1.qp_ref.q0_ref, bf16[2048,128]{1,0:T(8,128)(2,1)} %copy-done.3, bf16[2048,128]{1,0:T(8,128)(2,1)} %copy-done.2, bf16[2048,128]{1,0:T(8,128)(2,1)} %copy-done.4, ...), custom_call_target="tpu_custom_call" | custom-call | tf_op jit(solution)/shard_map/scores/pallas_call | solution.py:243
  36.5 5.5 %row_products.1 = (f32[256,2048]{1,0:T(8,128)}, bf16[256,2048]{1,0:T(8,128)(2,1)}) custom-call(bf16[512,640]{1,0:T(8,128)(2,1)} %bitcast.10, f32[512,2048]{1,0:T(8,128)} %get-tuple-element.16.e_ref), custom_call_target="tpu_custom_call" | custom-call | tf_op jit(solution)/shard_map/row_products/pallas_call | solution.py:256
  42.1 3.2 %collective-permute-start.5 = (f32[4,2048]{1,0:T(4,128)S(1)}, f32[4,2048]{1,0:T(4,128)S(1)}, u32[]{:S(2)}, u32[]{:S(2)}) collective-permute-start(f32[4,2048]{1,0:T(4,128)S(1)} %copy-done.6), channel_id=1, source_target_pairs={{0,3},{1,2},{2,1},{3,0},{4,7},{5,6},{6,5},{7,4},{8,11},{9,10},{10,... | collective-permute-start | bytes 98312 | tf_op jit(solution)/shard_map/ppermute | solution.py:194
  45.7 1.3 %collective-permute-done.5.s3 = f32[4,2048]{1,0:T(4,128)S(1)} collective-permute-done((f32[4,2048]{1,0:T(4,128)S(1)}, f32[4,2048]{1,0:T(4,128)S(1)}, u32[]{:S(2)}, u32[]{:S(2)}) %collective-permute-start.5) | collective-permute-done | bytes 32800 | tf_op jit(solution)/shard_map/ppermute | solution.py:194
  47.0 3.7 %collective-permute-done.4.s2 = f32[4,2048]{1,0:T(4,128)S(1)} collective-permute-done((f32[4,2048]{1,0:T(4,128)S(1)}, f32[4,2048]{1,0:T(4,128)S(1)}, u32[]{:S(2)}, u32[]{:S(2)}) %collective-permute-start.4) | collective-permute-done | bytes 32800 | tf_op jit(solution)/shard_map/ppermute | solution.py:194
  50.7 0.6 copy-done.8
  51.3 5.5 %item_products.1 = bf16[512,512]{1,0:T(8,128)(2,1)} custom-call(f32[4,2048]{1,0:T(4,128)} %get-tuple-element.15.s0, f32[4,2048]{1,0:T(4,128)} %copy-done.9, f32[4,2048]{1,0:T(4,128)} %copy-done.8, f32[4,2048]{1,0:T(4,128)} %copy-done.7, f32[512,2048]{1,0:T(8,128)} %get-tuple-element.16.e_ref, bf16[2048,512]{1,0:T(8,128)(2,1)} %get-tuple-element.23.q_ref), custom_call_target="tpu_custom_call" | custom-call | tf_op jit(solution)/shard_map/item_products/pallas_call | solution.py:278
  56.8 9.1 %all-to-all-start.1 = ((bf16[32,16,512]{2,1,0:T(8,128)(2,1)}), bf16[32,16,512]{2,1,0:T(8,128)(2,1)S(1)}, u32[]{:S(2)}, u32[]{:S(2)}) async-start(bf16[32,16,512]{2,1,0:T(8,128)(2,1)} %bitcast.11), calls=%async_computation.1 | async-start | bytes 1048576 | tf_op jit(solution)/shard_map/all_to_all | solution.py:288
  66.0 1.0 %copy-done.1 = bf16[256,2048]{1,0:T(8,128)(2,1)} copy-done((bf16[256,2048]{1,0:T(8,128)(2,1)}, bf16[256,2048]{1,0:T(8,128)(2,1)S(1)}, u32[]{:S(2)}) %copy-start.1) | copy-done | bytes 1048600
  66.9 3.3 %combine.1 = (f32[128,2048]{1,0:T(8,128)}, bf16[128,2048]{1,0:T(8,128)(2,1)}, f32[1,2048]{1,0:T(1,128)}) custom-call(f32[4,2048]{1,0:T(4,128)} %get-tuple-element.15.s0, f32[4,2048]{1,0:T(4,128)} %copy-done.9, f32[4,2048]{1,0:T(4,128)} %copy-done.8, f32[4,2048]{1,0:T(4,128)} %copy-done.7, f32[256,2048]{1,0:T(8,128)} %get-tuple-element.17.keep_ref, ...), custom_call_target="tpu_custom_call" | custom-call | tf_op jit(solution)/shard_map/combine/pallas_call | solution.py:268
  70.3 1.3 %collective-permute-start.7 = (bf16[128,2048]{1,0:T(8,128)(2,1)}, bf16[128,2048]{1,0:T(8,128)(2,1)S(1)}, u32[]{:S(2)}, u32[]{:S(2)}) collective-permute-start(bf16[128,2048]{1,0:T(8,128)(2,1)} %get-tuple-element.20), channel_id=1, source_target_pairs={{0,2},{1,3},{2,0},{3,1},{4,6},{5,7},{6,4},{7,5},{8,10},{9,11},{10,... | collective-permute-start | bytes 1572872 | tf_op jit(solution)/shard_map/ppermute | solution.py:194
  71.5 5.5 %all-to-all-done.1 = bf16[32,16,512]{2,1,0:T(8,128)(2,1)S(1)} async-done(((bf16[32,16,512]{2,1,0:T(8,128)(2,1)}), bf16[32,16,512]{2,1,0:T(8,128)(2,1)S(1)}, u32[]{:S(2)}, u32[]{:S(2)}) %all-to-all-start.1) | async-done | bytes 524320 | tf_op jit(solution)/shard_map/all_to_all | solution.py:288
  77.0 0.7 convert_reduce_fusion
  77.7 9.0 %collective-permute-done.7.recv_ref = bf16[128,2048]{1,0:T(8,128)(2,1)S(1)} collective-permute-done((bf16[128,2048]{1,0:T(8,128)(2,1)}, bf16[128,2048]{1,0:T(8,128)(2,1)S(1)}, u32[]{:S(2)}, u32[]{:S(2)}) %collective-permute-start.7) | collective-permute-done | bytes 524320 | tf_op jit(solution)/shard_map/ppermute | solution.py:194
  86.7 0.8 copy-done.5
  87.5 4.3 %unpack.1 = bf16[6144,128]{1,0:T(8,128)(2,1)} custom-call(s32[1,32]{1,0:T(1,128)} %len_ref.5, f32[128,2048]{1,0:T(8,128)} %get-tuple-element.19.own_ref, bf16[128,2048]{1,0:T(8,128)(2,1)} %copy-done.5, f32[1,2048]{1,0:T(1,128)} %get-tuple-element.21.term_ref, bf16[2048,128]{1,0:T(8,128)(2,1)} %get-tuple-element.22.pp_ref), custom_call_target="tpu_custom_call" | custom-call | tf_op jit(solution)/shard_map/unpack/pallas_call | solution.py:291
  (33 shorter events, 0.9 us)
Async XLA Ops:
  0.6 6.9 %copy-start.11 = (s32[16]{0:T(128)S(1)}, s32[16]{0:T(128)}, u32[]{:S(2)}) copy-start(s32[16]{0:T(128)} %param.11) | copy-start | bytes 196
  0.6 7.0 %copy-start.10 = (bf16[16,512]{1,0:T(8,128)(2,1)S(1)}, bf16[16,512]{1,0:T(8,128)(2,1)}, u32[]{:S(2)}) copy-start(bf16[16,512]{1,0:T(8,128)(2,1)} %param.10) | copy-start | bytes 49156
  3.5 20.8 %collective-permute-start.1 = (bf16[2048,128]{1,0:T(8,128)(2,1)}, bf16[2048,128]{1,0:T(8,128)(2,1)S(1)}, u32[]{:S(2)}, u32[]{:S(2)}) collective-permute-start(bf16[2048,128]{1,0:T(8,128)(2,1)} %pack_query.1.qp_ref.q0_ref), channel_id=1, source_target_pairs={{0,2},{1,3},{2,0},{3,1},{4,6},{5,7},{6,4},{7,5},{8,10},{9,11},{10,... | collective-permute-start | bytes 1572872 | tf_op jit(solution)/shard_map/ppermute | solution.py:194
  8.5 20.4 %all-to-all-start = ((bf16[32,16,640]{2,1,0:T(8,128)(2,1)}), bf16[32,16,640]{2,1,0:T(8,128)(2,1)S(1)}, u32[]{:S(2)}, u32[]{:S(2)}) async-start(bf16[32,16,640]{2,1,0:T(8,128)(2,1)} %tile.2), calls=%async_computation | async-start | bytes 1310720 | tf_op jit(solution)/shard_map/all_to_all | solution.py:236
  16.3 11.5 %collective-permute-start = (bf16[2048,128]{1,0:T(8,128)(2,1)}, bf16[2048,128]{1,0:T(8,128)(2,1)S(1)}, u32[]{:S(2)}, u32[]{:S(2)}) collective-permute-start(bf16[2048,128]{1,0:T(8,128)(2,1)} %pack_query.1.qp_ref.q0_ref), channel_id=1, source_target_pairs={{0,1},{1,0},{2,3},{3,2},{4,5},{5,4},{6,7},{7,6},{8,9},{9,8},{10,11... | collective-permute-start | bytes 1572872 | tf_op jit(solution)/shard_map/ppermute | solution.py:194
  24.3 4.6 %copy-start.2 = (bf16[2048,128]{1,0:T(8,128)(2,1)}, bf16[2048,128]{1,0:T(8,128)(2,1)S(1)}, u32[]{:S(2)}) copy-start(bf16[2048,128]{1,0:T(8,128)(2,1)S(1)} %collective-permute-done.1.q2_ref) | copy-start | bytes 1572868
  24.3 4.6 %collective-permute-start.2 = (bf16[2048,128]{1,0:T(8,128)(2,1)S(1)}, bf16[2048,128]{1,0:T(8,128)(2,1)S(1)}, u32[]{:S(2)}, u32[]{:S(2)}) collective-permute-start(bf16[2048,128]{1,0:T(8,128)(2,1)S(1)} %collective-permute-done.1.q2_ref), channel_id=1, source_target_pairs={{0,1},{1,0},{2,3},{3,2},{4,5},{5,4},{6,7},{7,6},{8,9},{9,8},{10,11... | collective-permute-start | bytes 1572872 | tf_op jit(solution)/shard_map/ppermute | solution.py:194
  27.8 1.2 %copy-start.3 = (bf16[2048,128]{1,0:T(8,128)(2,1)}, bf16[2048,128]{1,0:T(8,128)(2,1)S(1)}, u32[]{:S(2)}) copy-start(bf16[2048,128]{1,0:T(8,128)(2,1)S(1)} %collective-permute-done.q1_ref) | copy-start | bytes 1572868
  28.9 0.9 %copy-start = (bf16[32,16,640]{2,1,0:T(8,128)(2,1)}, bf16[32,16,640]{2,1,0:T(8,128)(2,1)S(1)}, u32[]{:S(2)}) copy-start(bf16[32,16,640]{2,1,0:T(8,128)(2,1)S(1)} %all-to-all-done) | copy-start | bytes 1966084
  28.9 1.0 %copy-start.4 = (bf16[2048,128]{1,0:T(8,128)(2,1)}, bf16[2048,128]{1,0:T(8,128)(2,1)S(1)}, u32[]{:S(2)}) copy-start(bf16[2048,128]{1,0:T(8,128)(2,1)S(1)} %collective-permute-done.2.q3_ref) | copy-start | bytes 1572868
  36.5 5.5 %copy-start.6 = (f32[4,2048]{1,0:T(4,128)S(1)}, f32[4,2048]{1,0:T(4,128)}, u32[]{:S(2)}) copy-start(f32[4,2048]{1,0:T(4,128)} %get-tuple-element.15.s0) | copy-start | bytes 98308
  42.1 23.9 %collective-permute-start.6 = (bf16[256,2048]{1,0:T(8,128)(2,1)}, bf16[256,2048]{1,0:T(8,128)(2,1)S(1)}, u32[]{:S(2)}, u32[]{:S(2)}) collective-permute-start(bf16[256,2048]{1,0:T(8,128)(2,1)} %get-tuple-element.18), channel_id=1, source_target_pairs={{0,1},{1,0},{2,3},{3,2},{4,5},{5,4},{6,7},{7,6},{8,9},{9,8},{10,11... | collective-permute-start | bytes 3145736 | tf_op jit(solution)/shard_map/ppermute | solution.py:194
  42.1 4.9 %collective-permute-start.5 = (f32[4,2048]{1,0:T(4,128)S(1)}, f32[4,2048]{1,0:T(4,128)S(1)}, u32[]{:S(2)}, u32[]{:S(2)}) collective-permute-start(f32[4,2048]{1,0:T(4,128)S(1)} %copy-done.6), channel_id=1, source_target_pairs={{0,3},{1,2},{2,1},{3,0},{4,7},{5,6},{6,5},{7,4},{8,11},{9,10},{10,... | collective-permute-start | bytes 98312 | tf_op jit(solution)/shard_map/ppermute | solution.py:194
  45.2 5.4 %collective-permute-start.4 = (f32[4,2048]{1,0:T(4,128)S(1)}, f32[4,2048]{1,0:T(4,128)S(1)}, u32[]{:S(2)}, u32[]{:S(2)}) collective-permute-start(f32[4,2048]{1,0:T(4,128)S(1)} %copy-done.6), channel_id=1, source_target_pairs={{0,2},{1,3},{2,0},{3,1},{4,6},{5,7},{6,4},{7,5},{8,10},{9,11},{10,... | collective-permute-start | bytes 98312 | tf_op jit(solution)/shard_map/ppermute | solution.py:194
  45.7 4.9 %collective-permute-start.3 = (f32[4,2048]{1,0:T(4,128)S(1)}, f32[4,2048]{1,0:T(4,128)S(1)}, u32[]{:S(2)}, u32[]{:S(2)}) collective-permute-start(f32[4,2048]{1,0:T(4,128)S(1)} %copy-done.6), channel_id=1, source_target_pairs={{0,1},{1,0},{2,3},{3,2},{4,5},{5,4},{6,7},{7,6},{8,9},{9,8},{10,11... | collective-permute-start | bytes 98312 | tf_op jit(solution)/shard_map/ppermute | solution.py:194
  47.0 3.7 %copy-start.7 = (f32[4,2048]{1,0:T(4,128)}, f32[4,2048]{1,0:T(4,128)S(1)}, u32[]{:S(2)}) copy-start(f32[4,2048]{1,0:T(4,128)S(1)} %collective-permute-done.5.s3) | copy-start | bytes 98308
  50.7 0.6 copy-start.8
  50.7 0.6 copy-start.9
  56.8 20.2 %all-to-all-start.1 = ((bf16[32,16,512]{2,1,0:T(8,128)(2,1)}), bf16[32,16,512]{2,1,0:T(8,128)(2,1)S(1)}, u32[]{:S(2)}, u32[]{:S(2)}) async-start(bf16[32,16,512]{2,1,0:T(8,128)(2,1)} %bitcast.11), calls=%async_computation.1 | async-start | bytes 1048576 | tf_op jit(solution)/shard_map/all_to_all | solution.py:288
  65.9 1.0 %copy-start.1 = (bf16[256,2048]{1,0:T(8,128)(2,1)}, bf16[256,2048]{1,0:T(8,128)(2,1)S(1)}, u32[]{:S(2)}) copy-start(bf16[256,2048]{1,0:T(8,128)(2,1)S(1)} %collective-permute-done.6.recv_ref) | copy-start | bytes 3145732
  70.3 16.5 %collective-permute-start.7 = (bf16[128,2048]{1,0:T(8,128)(2,1)}, bf16[128,2048]{1,0:T(8,128)(2,1)S(1)}, u32[]{:S(2)}, u32[]{:S(2)}) collective-permute-start(bf16[128,2048]{1,0:T(8,128)(2,1)} %get-tuple-element.20), channel_id=1, source_target_pairs={{0,2},{1,3},{2,0},{3,1},{4,6},{5,7},{6,4},{7,5},{8,10},{9,11},{10,... | collective-permute-start | bytes 1572872 | tf_op jit(solution)/shard_map/ppermute | solution.py:194
  86.7 0.8 copy-start.5

commit v2 on v1

v2 whole, which is shorter than its diff:
```python
from functools import partial

import jax
import jax.numpy as jnp
from jax import lax
from jax.experimental import pallas as pl
from jax.experimental.pallas import tpu as pltpu
from jax.sharding import Mesh
from jax.sharding import PartitionSpec as P

MAXLEN = 192
LANES = 128
CHUNK = 64
TILE = 512
FLOOR = -1e30
MASKED = -3e38
SEQ = ("x", "zl", "y")
F32 = jnp.float32
BF16 = jnp.bfloat16
VMEM_BYTES = 14 * 1024 * 1024


def params():
    return pltpu.CompilerParams(vmem_limit_bytes=VMEM_BYTES)


def whole():
    return pl.BlockSpec(memory_space=pltpu.VMEM)


def small():
    return pl.BlockSpec(memory_space=pltpu.SMEM)


def dot(a, b, da, db):
    return lax.dot_general(a, b, (((da,), (db,)), ((), ())), preferred_element_type=F32)


def copy_rows(len_ref, src_ref, packed):
    start = jnp.int32(0)
    for h in range(len_ref.shape[1]):
        size = len_ref[0, h]
        for c in range(0, MAXLEN, CHUNK):

            @pl.when(size > c)
            def _():
                packed[pl.ds(start + c, CHUNK), :] = src_ref[h * MAXLEN + c : h * MAXLEN + c + CHUNK, :].astype(F32)

        start = start + size


def pass_on(value_ref, after_ref, out_ref):
    pass


def copies_kernel(row_ref, other_ref, out_ref):
    first = lax.axis_index("zl") == 0
    size = row_ref.shape[0]
    row, other = row_ref[...], other_ref[...]
    pair = (jnp.where(first, row, other), jnp.where(first, other, row))
    for i in range(out_ref.shape[0] // size):
        out_ref[i * size : (i + 1) * size, :] = pair[i % 2]


def sum_kernel(share_ref, after_ref, out_ref):
    size = out_ref.shape[0]
    total = share_ref[:size, :].astype(F32)
    for i in range(1, share_ref.shape[0] // size):
        total = total + share_ref[i * size : (i + 1) * size, :].astype(F32)
    out_ref[...] = total


def pack_query(len_ref, q_ref, qp_ref, packed):
    copy_rows(len_ref, q_ref, packed)
    qp_ref[...] = packed[: qp_ref.shape[0], :].astype(BF16)


def pack_positive(len_ref, p_ref, id_ref, qp_ref, pt_ref, part_ref, idp_ref, packed, ids):
    rows = qp_ref.shape[0]
    copy_rows(len_ref, p_ref, packed)
    ones = jnp.ones((16, LANES), BF16)
    for k in range(rows // LANES):
        at = slice(k * LANES, (k + 1) * LANES)
        held = packed[at, :]
        pt_ref[:, at] = held.T.astype(BF16)
        product = held * qp_ref[at, :].astype(F32)
        high = product.astype(BF16)
        low = (product - high.astype(F32)).astype(BF16)
        part_ref[:, at] = (dot(ones, high, 1, 1) + dot(ones, low, 1, 1))[:1, :]
    lane = lax.broadcasted_iota(jnp.int32, (1, LANES), 1)
    start = jnp.int32(0)
    for h in range(len_ref.shape[1]):
        row, off = divmod(h * MAXLEN, LANES)
        at = start + (LANES - off)
        target = at // LANES
        shift = at - target * LANES
        first = pltpu.roll(id_ref[row : row + 1, :], shift, 1)
        second = pltpu.roll(id_ref[row + 1 : row + 2, :], shift, 1)
        kept0 = ids[pl.ds(target, 1), :]
        kept1 = ids[pl.ds(target + 1, 1), :]
        ids[pl.ds(target, 1), :] = jnp.where(lane >= shift + off, first, kept0)
        ids[pl.ds(target + 1, 1), :] = jnp.where(
            lane + LANES >= shift + off, jnp.where(lane >= shift, second, first), kept1
        )
        ids[pl.ds(target + 2, 1), :] = second
        start = start + len_ref[0, h]
    for k in range(rows // LANES):
        idp_ref[:, k * LANES : (k + 1) * LANES] = ids[k + 1 : k + 2, :].astype(F32)


def block_of(order, step):
    return pl.ds(pl.multiple_of((order ^ step) * LANES, LANES), LANES)


def scores_kernel(neg_ref, q0_ref, q1_ref, q2_ref, q3_ref, idp_ref, part_ref, qfull_ref, e_ref, stat_ref, negid):
    member = lax.axis_index("grp")
    width = 4 * LANES
    lane = lax.broadcasted_iota(jnp.int32, (1, LANES), 1)
    place = jnp.where(lane == 0, 65536.0, jnp.where(lane == 1, 256.0, jnp.where(lane == 2, 1.0, 0.0)))
    value = jnp.sum(neg_ref[:, width : width + LANES].astype(F32) * place, axis=1, keepdims=True)
    negid[...] = jnp.broadcast_to(value, negid.shape)
    for t in range(0, qfull_ref.shape[0], TILE):
        rows = slice(t, t + TILE)
        for k, ref in enumerate((q0_ref, q1_ref, q2_ref, q3_ref)):
            qfull_ref[rows, block_of(member, k)] = ref[rows, :]
        scores = dot(neg_ref[:, :width], qfull_ref[rows, :], 1, 1)
        for k in range(TILE // LANES):
            at = slice(t + k * LANES, t + (k + 1) * LANES)
            part = jnp.where(negid[...] == idp_ref[:, at], MASKED, scores[:, k * LANES : (k + 1) * LANES])
            top = jnp.maximum(jnp.max(part, axis=0, keepdims=True), FLOOR)
            e = jnp.exp(part - top)
            e_ref[:, at] = e
            stat_ref[0:1, at] = top
            stat_ref[1:2, at] = jnp.sum(e, axis=0, keepdims=True)
    stat_ref[2:3, :] = part_ref[...]
    stat_ref[3:4, :] = part_ref[...]


def rows_kernel(neg_ref, e_ref, keep_ref, send_ref, turned):
    member = lax.axis_index("grp")
    half = 2 * LANES
    for k, step in enumerate((0, 2, 1, 3)):
        turned[k * LANES : (k + 1) * LANES, :] = neg_ref[:, block_of(member, step)].T
    for t in range(0, e_ref.shape[1], TILE):
        at = slice(t, t + TILE)
        out = dot(turned[...], e_ref[:, at].astype(BF16), 1, 0)
        keep_ref[:, at] = out[:half, :]
        send_ref[:, at] = out[half:, :].astype(BF16)


def combine_kernel(s0, s1, s2, s3, keep_ref, recv_ref, own_ref, send_ref, term_ref, scale_ref):
    refs = (s0, s1, s2, s3)
    positive = s0[2:3, :] + s1[2:3, :] + s2[2:3, :] + s3[2:3, :]
    top = positive
    for ref in refs:
        top = jnp.maximum(top, ref[0:1, :])
    total = jnp.exp(positive - top)
    for ref in refs:
        total = total + ref[1:2, :] * jnp.exp(ref[0:1, :] - top)
    log_total = top + jnp.log(total)
    mine = jnp.exp(s0[0:1, :] - log_total)
    other = jnp.exp(s1[0:1, :] - log_total)
    scale_ref[...] = mine
    term_ref[...] = jnp.exp(positive - log_total) - 1.0
    send_ref[...] = (keep_ref[LANES:, :] * mine + recv_ref[LANES:, :].astype(F32) * other).astype(BF16)
    own_ref[...] = keep_ref[:LANES, :] * mine + recv_ref[:LANES, :].astype(F32) * other


def items_kernel(scale_ref, e_ref, q_ref, out_ref):
    total = None
    for t in range(0, e_ref.shape[1], TILE):
        at = slice(t, t + TILE)
        weights = (e_ref[:, at] * scale_ref[:, at]).astype(BF16)
        part = dot(weights, q_ref[at, :], 1, 0)
        total = part if total is None else total + part
    x, y, z = lax.axis_size("x"), lax.axis_size("y"), lax.axis_size("zl")
    size = out_ref.shape[0] // (x * y * z)
    for i in range(x * y * z):
        src = ((i // (y * z)) * y + i % y) * z + (i // y) % z
        out_ref[i * size : (i + 1) * size, :] = total[src * size : (src + 1) * size, :].astype(BF16)


def unpack_kernel(len_ref, own_ref, recv_ref, term_ref, pt_ref, out_ref, packed):
    rows = own_ref.shape[1]
    for k in range(rows // LANES):
        at = slice(k * LANES, (k + 1) * LANES)
        packed[at, :] = (own_ref[:, at] + recv_ref[:, at].astype(F32) + term_ref[:, at] * pt_ref[:, at].astype(F32)).T
    index = lax.broadcasted_iota(jnp.int32, (CHUNK, LANES), 0)
    start = jnp.int32(0)
    for h in range(len_ref.shape[1]):
        size = len_ref[0, h]
        for c in range(0, MAXLEN, CHUNK):
            at = slice(h * MAXLEN + c, h * MAXLEN + c + CHUNK)

            @pl.when(size > c)
            def _():
                out_ref[at, :] = jnp.where(index < size - c, packed[pl.ds(start + c, CHUNK), :], 0.0).astype(BF16)

            @pl.when(size <= c)
            def _():
                out_ref[at, :] = jnp.zeros((CHUNK, LANES), BF16)

        start = start + size


def held(value):
    return pltpu.with_memory_space_constraint(value, pltpu.VMEM)


def after(value, other):
    any_place = pl.BlockSpec(memory_space=pl.ANY)
    return pl.pallas_call(
        pass_on,
        out_shape=pltpu.VMEM(value.shape, value.dtype),
        in_specs=[any_place, any_place],
        out_specs=any_place,
        input_output_aliases={0: 0},
        compiler_params=params(),
        name="after",
    )(held(value), other)


def swap(value, step, groups):
    return lax.ppermute(value, "grp", [(g, g ^ step) for g in range(groups)])


def shards(live, query, pos_emb, pos_ids, lengths, negatives, neg_ids):
    groups = lax.axis_size("grp")
    seqs = lax.axis_size(SEQ)
    near = lax.axis_size("zl")
    own_neg, width = negatives.shape
    slots = query.shape[0]
    negs = own_neg * seqs
    half = 2 * LANES
    vmem = pltpu.VMEM

    digits = jnp.stack([neg_ids // 65536, (neg_ids // 256) % 256, neg_ids % 256], axis=1).astype(BF16)
    row = jnp.concatenate([negatives, jnp.pad(digits, ((0, 0), (0, LANES - 3)))], axis=1)

    other = lax.ppermute(row, "zl", [(i, near - 1 - i) for i in range(near)])
    qp = pl.pallas_call(
        pack_query,
        out_shape=vmem((live, LANES), BF16),
        in_specs=[small(), whole()],
        out_specs=whole(),
        scratch_shapes=[vmem((live + MAXLEN, LANES), F32)],
        compiler_params=params(),
        name="pack_query",
    )(lengths, query)
    qp = after(qp, other)
    q2 = swap(qp, 2, groups)
    q1 = swap(qp, 1, groups)
    q3 = swap(q2, 1, groups)

    pt, part, idp = pl.pallas_call(
        pack_positive,
        out_shape=(vmem((LANES, live), BF16), vmem((1, live), F32), vmem((1, live), F32)),
        in_specs=[small(), whole(), whole(), whole()],
        out_specs=(whole(), whole(), whole()),
        scratch_shapes=[vmem((live + MAXLEN, LANES), F32), vmem((live // LANES + 8, LANES), jnp.int32)],
        compiler_params=params(),
        name="pack_positive",
    )(lengths, pos_emb, pos_ids.reshape(slots // LANES, LANES), held(qp))

    copies = pl.pallas_call(
        copies_kernel,
        out_shape=vmem((negs, width + LANES), BF16),
        in_specs=[whole()] * 2,
        out_specs=whole(),
        compiler_params=params(),
        name="copies",
    )(held(row), held(other))
    pool = lax.all_to_all(copies, ("x", "y"), split_axis=0, concat_axis=0, tiled=True)
    pool = held(pool)

    qfull, e, stat = pl.pallas_call(
        scores_kernel,
        out_shape=(vmem((live, width), BF16), vmem((negs, live), F32), vmem((4, live), F32)),
        in_specs=[whole()] * 7,
        out_specs=(whole(), whole(), whole()),
        scratch_shapes=[vmem((negs, LANES), F32)],
        compiler_params=params(),
        name="scores",
    )(pool, held(qp), held(q1), held(q2), held(q3), held(idp), held(part))
    stat2 = swap(stat, 2, groups)
    stats = [held(s) for s in (stat, swap(stat, 1, groups), stat2, swap(stat2, 1, groups))]

    keep, send = pl.pallas_call(
        rows_kernel,
        out_shape=(vmem((half, live), F32), vmem((half, live), BF16)),
        in_specs=[whole()] * 2,
        out_specs=(whole(), whole()),
        scratch_shapes=[vmem((width, negs), BF16)],
        compiler_params=params(),
        name="row_products",
    )(pool, held(e))
    recv = swap(send, 1, groups)

    own, onward, term, scale = pl.pallas_call(
        combine_kernel,
        out_shape=(vmem((LANES, live), F32), vmem((LANES, live), BF16), vmem((1, live), F32), vmem((1, live), F32)),
        in_specs=[whole()] * 6,
        out_specs=(whole(), whole(), whole(), whole()),
        compiler_params=params(),
        name="combine",
    )(*stats, held(keep), held(recv))
    recv2 = swap(onward, 2, groups)

    items = pl.pallas_call(
        items_kernel,
        out_shape=vmem((negs, width), BF16),
        in_specs=[whole()] * 3,
        out_specs=whole(),
        compiler_params=params(),
        name="item_products",
    )(held(scale), held(e), held(qfull))
    shares = lax.all_to_all(items, SEQ, split_axis=0, concat_axis=0, tiled=True)
    last = swap(recv2[:16, :LANES], 1, groups)
    grad_items = pl.pallas_call(
        sum_kernel,
        out_shape=jax.ShapeDtypeStruct((own_neg, width), F32),
        in_specs=[whole(), pl.BlockSpec(memory_space=pl.ANY)],
        out_specs=whole(),
        compiler_params=params(),
        name="sum_shares",
    )(shares, last)

    grad_query = pl.pallas_call(
        unpack_kernel,
        out_shape=jax.ShapeDtypeStruct((slots, LANES), BF16),
        in_specs=[small()] + [whole()] * 4,
        out_specs=whole(),
        scratch_shapes=[vmem((live + MAXLEN, LANES), F32)],
        compiler_params=params(),
        name="unpack",
    )(lengths, held(own), held(recv2), held(term), held(pt))
    return grad_query, grad_items


def solution(mesh, live=2048):
    split = Mesh(mesh.devices.reshape(4, 2, 4, mesh.shape["grp"]), SEQ + ("grp",))
    return jax.shard_map(
        partial(shards, live),
        mesh=split,
        in_specs=(
            P(SEQ, "grp"),
            P(SEQ, "grp"),
            P(SEQ),
            P(SEQ, None),
            P(SEQ + ("grp",), None),
            P(SEQ + ("grp",)),
        ),
        out_specs=(P(SEQ, "grp"), P(SEQ + ("grp",), None)),
        check_vma=False,
    )
```

time: 92.6 us -> 71 us (0.77)
  the two profiles are of different devices: /device:TPU:0 before, /device:TPU:1 now
where the time goes in v2:
time: 71 us; the launch traced here: 70.6 us
  starting transfers between devices  25.8 us (36%)
  waiting for transfers between devices  23.8 us (34%)
  Pallas kernels  14.9 us (21%)
  local copies, waits for them, and re-layouts  4.02 us (6%)
  other arithmetic  1.41 us (2%)
  between operations  0.72 us (1%)
    ppermute x9, waiting for transfers between devices, swap(): return lax.ppermute(value, 'grp', [(g, g ^ step) for g in range(groups)])  20.3 us
    ppermute x9, starting transfers between devices, swap(): return lax.ppermute(value, 'grp', [(g, g ^ step) for g in range(groups)])  12 us
    all_to_all x1, starting transfers between devices, shards(): lax.all_to_all(copies, ('x', 'y'), split_axis=0, concat_axis=0, tiled=True)  6.75 us
    all_to_all x1, starting transfers between devices, shards(): shares = lax.all_to_all(items, SEQ, split_axis=0, concat_axis=0, tiled=True)  4.58 us
    unnamed x14, local copies, waits for them, and re-layouts  3.93 us
    all_to_all x1, waiting for transfers between devices, shards(): lax.all_to_all(copies, ('x', 'y'), split_axis=0, concat_axis=0, tiled=True)  3.52 us
    pallas_call x1, Pallas kernels, shards(): pl.pallas_call(scores_kernel, out_shape=(vmem((live, width), BF16), vmem(...  3.5 us
    pallas_call x1, Pallas kernels, shards(): pl.pallas_call(unpack_kernel, out_shape=jax.ShapeDtypeStruct((slots, LANE...  3.04 us
  transfers between devices with their start and end apart: 12, of which 5 were waited for; matrix products, arithmetic and copies ran while one was open for 0% of the time, Pallas kernels for 13%

profile of v2, /device:TPU:1, one launch (start us, length us, event | category | flops | bytes accessed | tf_op | source)
XLA Modules:
  0.0 70.6 jit_solution(18247017101179362352)
XLA Ops:
  2.1 2.5 %collective-permute-start = (bf16[16,640]{1,0:T(8,128)(2,1)S(1)}, bf16[16,640]{1,0:T(8,128)(2,1)S(1)}, u32[]{:S(2)}, u32[]{:S(2)}) collective-permute-start(bf16[16,640]{1,0:T(8,128)(2,1)S(1)} %fusion.1.row_ref), channel_id=1, source_target_pairs={{0,16},{16,0},{1,17},{17,1},{2,18},{18,2},{3,19},{19,3},{4,20},{20... | collective-permute-start | bytes 61448 | tf_op jit(solution)/shard_map/ppermute | solution.py:240
  4.6 1.4 %copy-done = bf16[6144,128]{1,0:T(8,128)(2,1)S(1)} copy-done((bf16[6144,128]{1,0:T(8,128)(2,1)S(1)}, bf16[6144,128]{1,0:T(8,128)(2,1)}, u32[]{:S(2)}) %copy-start) | copy-done | bytes 1572888
  6.7 1.2 %pack_query.1.value_ref = bf16[2048,128]{1,0:T(8,128)(2,1)S(1)} custom-call(s32[1,32]{1,0:T(1,128)S(1)} %copy-done.5, bf16[6144,128]{1,0:T(8,128)(2,1)S(1)} %copy-done), custom_call_target="tpu_custom_call" | custom-call | tf_op jit(solution)/shard_map/pack_query/pallas_call | solution.py:241
  7.9 3.4 %collective-permute-start.2 = (bf16[2048,128]{1,0:T(8,128)(2,1)S(1)}, bf16[2048,128]{1,0:T(8,128)(2,1)}, u32[]{:S(2)}, u32[]{:S(2)}) collective-permute-start(bf16[2048,128]{1,0:T(8,128)(2,1)S(1)} %after.1.qp_ref.q0_ref), channel_id=1, source_target_pairs={{0,2},{1,3},{2,0},{3,1},{4,6},{5,7},{6,4},{7,5},{8,10},{9,11},{10,... | collective-permute-start | bytes 1572872 | tf_op jit(solution)/shard_map/ppermute | solution.py:224
  11.3 0.9 %copies.1 = bf16[512,640]{1,0:T(8,128)(2,1)} custom-call(bf16[16,640]{1,0:T(8,128)(2,1)S(1)} %fusion.1.row_ref, bf16[16,640]{1,0:T(8,128)(2,1)S(1)} %collective-permute-done.other_ref.after_ref), custom_call_target="tpu_custom_call" | custom-call | tf_op jit(solution)/shard_map/copies/pallas_call | solution.py:265
  12.2 6.8 %all-to-all-start = ((bf16[16,32,640]{2,1,0:T(8,128)(2,1)}), bf16[16,32,640]{2,1,0:T(8,128)(2,1)S(1)}, u32[]{:S(2)}, u32[]{:S(2)}) async-start(bf16[16,32,640]{2,1,0:T(8,128)(2,1)} %bitcast.3), calls=%async_computation | async-start | bytes 1310720 | tf_op jit(solution)/shard_map/all_to_all | solution.py:273
  18.9 1.6 %collective-permute-start.1 = (bf16[2048,128]{1,0:T(8,128)(2,1)S(1)}, bf16[2048,128]{1,0:T(8,128)(2,1)S(1)}, u32[]{:S(2)}, u32[]{:S(2)}) collective-permute-start(bf16[2048,128]{1,0:T(8,128)(2,1)S(1)} %after.1.qp_ref.q0_ref), channel_id=1, source_target_pairs={{0,1},{1,0},{2,3},{3,2},{4,5},{5,4},{6,7},{7,6},{8,9},{9,8},{10,11... | collective-permute-start | bytes 1572872 | tf_op jit(solution)/shard_map/ppermute | solution.py:224
  20.5 2.2 %collective-permute-done.2.q2_ref = bf16[2048,128]{1,0:T(8,128)(2,1)} collective-permute-done((bf16[2048,128]{1,0:T(8,128)(2,1)S(1)}, bf16[2048,128]{1,0:T(8,128)(2,1)}, u32[]{:S(2)}, u32[]{:S(2)}) %collective-permute-start.2) | collective-permute-done | bytes 524320 | tf_op jit(solution)/shard_map/ppermute | solution.py:224
  22.7 1.5 %collective-permute-start.3 = (bf16[2048,128]{1,0:T(8,128)(2,1)}, bf16[2048,128]{1,0:T(8,128)(2,1)}, u32[]{:S(2)}, u32[]{:S(2)}) collective-permute-start(bf16[2048,128]{1,0:T(8,128)(2,1)} %collective-permute-done.2.q2_ref), channel_id=1, source_target_pairs={{0,1},{1,0},{2,3},{3,2},{4,5},{5,4},{6,7},{7,6},{8,9},{9,8},{10,11... | collective-permute-start | bytes 1572872 | tf_op jit(solution)/shard_map/ppermute | solution.py:224
  24.3 1.8 %pack_positive.1 = (bf16[128,2048]{1,0:T(8,128)(2,1)S(1)}, f32[1,2048]{1,0:T(1,128)S(1)}, f32[1,2048]{1,0:T(1,128)S(1)}) custom-call(s32[1,32]{1,0:T(1,128)S(1)} %copy-done.6, bf16[6144,128]{1,0:T(8,128)(2,1)S(1)} %copy-done.1, s32[48,128]{1,0:T(8,128)S(1)} %bitcast.14, bf16[2048,128]{1,0:T(8,128)(2,1)S(1)} %after.1.qp_ref.q0_ref), custom_call_target="tpu_custom_call" | custom-call | tf_op jit(solution)/shard_map/pack_positive/pallas_call | solution.py:255
  26.1 0.8 %copy-done.2 = bf16[2048,128]{1,0:T(8,128)(2,1)} copy-done((bf16[2048,128]{1,0:T(8,128)(2,1)}, bf16[2048,128]{1,0:T(8,128)(2,1)S(1)}, u32[]{:S(2)}) %copy-start.2) | copy-done | bytes 524312
  26.9 3.5 %all-to-all-done = bf16[16,32,640]{2,1,0:T(8,128)(2,1)S(1)} async-done(((bf16[16,32,640]{2,1,0:T(8,128)(2,1)}), bf16[16,32,640]{2,1,0:T(8,128)(2,1)S(1)}, u32[]{:S(2)}, u32[]{:S(2)}) %all-to-all-start) | async-done | bytes 655392 | tf_op jit(solution)/shard_map/all_to_all | solution.py:273
  30.5 1.0 %copy-done.3 = bf16[2048,128]{1,0:T(8,128)(2,1)S(1)} copy-done((bf16[2048,128]{1,0:T(8,128)(2,1)S(1)}, bf16[2048,128]{1,0:T(8,128)(2,1)}, u32[]{:S(2)}) %copy-start.3) | copy-done | bytes 524312
  31.5 3.5 %scores.1 = (bf16[2048,512]{1,0:T(8,128)(2,1)S(1)}, f32[512,2048]{1,0:T(8,128)S(1)}, f32[4,2048]{1,0:T(4,128)S(1)}) custom-call(bf16[512,640]{1,0:T(8,128)(2,1)S(1)} %bitcast.11, bf16[2048,128]{1,0:T(8,128)(2,1)S(1)} %after.1.qp_ref.q0_ref, bf16[2048,128]{1,0:T(8,128)(2,1)S(1)} %copy-done.3, bf16[2048,128]{1,0:T(8,128)(2,1)} %collective-permute-done.2.q2_ref, ...), custom_call_target="tpu_custom_call" | custom-call | tf_op jit(solution)/shard_map/scores/pallas_call | solution.py:276
  35.0 1.3 %row_products.1 = (f32[256,2048]{1,0:T(8,128)S(1)}, bf16[256,2048]{1,0:T(8,128)(2,1)S(1)}) custom-call(bf16[512,640]{1,0:T(8,128)(2,1)S(1)} %bitcast.12, f32[512,2048]{1,0:T(8,128)S(1)} %get-tuple-element.17.e_ref), custom_call_target="tpu_custom_call" | custom-call | tf_op jit(solution)/shard_map/row_products/pallas_call | solution.py:288
  36.3 2.4 %collective-permute-start.7 = (bf16[256,2048]{1,0:T(8,128)(2,1)S(1)}, bf16[256,2048]{1,0:T(8,128)(2,1)S(1)}, u32[]{:S(2)}, u32[]{:S(2)}) collective-permute-start(bf16[256,2048]{1,0:T(8,128)(2,1)S(1)} %get-tuple-element.19), channel_id=1, source_target_pairs={{0,1},{1,0},{2,3},{3,2},{4,5},{5,4},{6,7},{7,6},{8,9},{9,8},{10,11... | collective-permute-start | bytes 3145736 | tf_op jit(solution)/shard_map/ppermute | solution.py:224
  38.9 4.1 %collective-permute-done.5.s2 = f32[4,2048]{1,0:T(4,128)S(1)} collective-permute-done((f32[4,2048]{1,0:T(4,128)S(1)}, f32[4,2048]{1,0:T(4,128)S(1)}, u32[]{:S(2)}, u32[]{:S(2)}) %collective-permute-start.5) | collective-permute-done | bytes 32800 | tf_op jit(solution)/shard_map/ppermute | solution.py:224
  43.0 1.2 %collective-permute-start.6 = (f32[4,2048]{1,0:T(4,128)S(1)}, f32[4,2048]{1,0:T(4,128)S(1)}, u32[]{:S(2)}, u32[]{:S(2)}) collective-permute-start(f32[4,2048]{1,0:T(4,128)S(1)} %collective-permute-done.5.s2), channel_id=1, source_target_pairs={{0,1},{1,0},{2,3},{3,2},{4,5},{5,4},{6,7},{7,6},{8,9},{9,8},{10,11... | collective-permute-start | bytes 98312 | tf_op jit(solution)/shard_map/ppermute | solution.py:224
  44.2 0.9 %collective-permute-done.6.s3 = f32[4,2048]{1,0:T(4,128)S(1)} collective-permute-done((f32[4,2048]{1,0:T(4,128)S(1)}, f32[4,2048]{1,0:T(4,128)S(1)}, u32[]{:S(2)}, u32[]{:S(2)}) %collective-permute-start.6) | collective-permute-done | bytes 32800 | tf_op jit(solution)/shard_map/ppermute | solution.py:224
  45.5 2.1 %item_products.1 = bf16[512,512]{1,0:T(8,128)(2,1)} custom-call(f32[1,2048]{1,0:T(1,128)S(1)} %get-tuple-element.24.scale_ref, f32[512,2048]{1,0:T(8,128)S(1)} %get-tuple-element.17.e_ref, bf16[2048,512]{1,0:T(8,128)(2,1)S(1)} %get-tuple-element.25.q_ref), custom_call_target="tpu_custom_call" | custom-call | tf_op jit(solution)/shard_map/item_products/pallas_call | solution.py:309
  47.6 4.6 %all-to-all-start.1 = ((bf16[32,16,512]{2,1,0:T(8,128)(2,1)}), bf16[32,16,512]{2,1,0:T(8,128)(2,1)S(1)}, u32[]{:S(2)}, u32[]{:S(2)}) async-start(bf16[32,16,512]{2,1,0:T(8,128)(2,1)} %bitcast.6), calls=%async_computation.1 | async-start | bytes 1048576 | tf_op jit(solution)/shard_map/all_to_all | solution.py:317
  52.2 13.1 %collective-permute-done.8.recv_ref = bf16[128,2048]{1,0:T(8,128)(2,1)S(1)} collective-permute-done((bf16[128,2048]{1,0:T(8,128)(2,1)S(1)}, bf16[128,2048]{1,0:T(8,128)(2,1)S(1)}, u32[]{:S(2)}, u32[]{:S(2)}) %collective-permute-start.8) | collective-permute-done | bytes 524320 | tf_op jit(solution)/shard_map/ppermute | solution.py:224
  65.3 1.5 %collective-permute-start.9 = (bf16[16,128]{1,0:T(8,128)(2,1)S(1)}, bf16[16,128]{1,0:T(8,128)(2,1)S(1)}, u32[]{:S(2)}, u32[]{:S(2)}) collective-permute-start(bf16[16,128]{1,0:T(8,128)(2,1)S(1)} %slice.4), channel_id=1, source_target_pairs={{0,1},{1,0},{2,3},{3,2},{4,5},{5,4},{6,7},{7,6},{8,9},{9,8},{10,11... | collective-permute-start | bytes 12296 | tf_op jit(solution)/shard_map/ppermute | solution.py:224
  66.8 3.0 %unpack.1 = bf16[6144,128]{1,0:T(8,128)(2,1)} custom-call(s32[1,32]{1,0:T(1,128)S(1)} %copy-done.6, f32[128,2048]{1,0:T(8,128)S(1)} %get-tuple-element.20.own_ref, bf16[128,2048]{1,0:T(8,128)(2,1)S(1)} %collective-permute-done.8.recv_ref, f32[1,2048]{1,0:T(1,128)S(1)} %get-tuple-element.22.term_ref, bf16[128,2048]{1,0:T(8,128)(2,1)S(1)} %get-tuple-element.23.pt_ref), custom_call_target="tpu_custom_call" | custom-call | tf_op jit(solution)/shard_map/unpack/pallas_call | solution.py:328
  (29 shorter events, 3.5 us)
Async XLA Ops:
  2.1 5.7 %collective-permute-start = (bf16[16,640]{1,0:T(8,128)(2,1)S(1)}, bf16[16,640]{1,0:T(8,128)(2,1)S(1)}, u32[]{:S(2)}, u32[]{:S(2)}) collective-permute-start(bf16[16,640]{1,0:T(8,128)(2,1)S(1)} %fusion.1.row_ref), channel_id=1, source_target_pairs={{0,16},{16,0},{1,17},{17,1},{2,18},{18,2},{3,19},{19,3},{4,20},{20... | collective-permute-start | bytes 61448 | tf_op jit(solution)/shard_map/ppermute | solution.py:240
  4.6 1.4 %copy-start = (bf16[6144,128]{1,0:T(8,128)(2,1)S(1)}, bf16[6144,128]{1,0:T(8,128)(2,1)}, u32[]{:S(2)}) copy-start(bf16[6144,128]{1,0:T(8,128)(2,1)} %q_ref.1) | copy-start | bytes 4718596
  6.0 0.7 copy-start.5
  6.7 17.6 %copy-start.1 = (bf16[6144,128]{1,0:T(8,128)(2,1)S(1)}, bf16[6144,128]{1,0:T(8,128)(2,1)}, u32[]{:S(2)}) copy-start(bf16[6144,128]{1,0:T(8,128)(2,1)} %p_ref.1) | copy-start | bytes 4718596
  6.7 17.6 %copy-start.4 = (s32[6144]{0:T(1024)S(1)}, s32[6144]{0:T(1024)}, u32[]{:S(2)}) copy-start(s32[6144]{0:T(1024)} %param.8) | copy-start | bytes 73732
  6.7 17.6 %copy-start.6 = (s32[1,32]{1,0:T(1,128)S(1)}, s32[1,32]{1,0:T(1,128)}, u32[]{:S(2)}) copy-start(s32[1,32]{1,0:T(1,128)} %len_ref.5) | copy-start | bytes 388
  7.9 14.8 %collective-permute-start.2 = (bf16[2048,128]{1,0:T(8,128)(2,1)S(1)}, bf16[2048,128]{1,0:T(8,128)(2,1)}, u32[]{:S(2)}, u32[]{:S(2)}) collective-permute-start(bf16[2048,128]{1,0:T(8,128)(2,1)S(1)} %after.1.qp_ref.q0_ref), channel_id=1, source_target_pairs={{0,2},{1,3},{2,0},{3,1},{4,6},{5,7},{6,4},{7,5},{8,10},{9,11},{10,... | collective-permute-start | bytes 1572872 | tf_op jit(solution)/shard_map/ppermute | solution.py:224
  12.2 18.3 %all-to-all-start = ((bf16[16,32,640]{2,1,0:T(8,128)(2,1)}), bf16[16,32,640]{2,1,0:T(8,128)(2,1)S(1)}, u32[]{:S(2)}, u32[]{:S(2)}) async-start(bf16[16,32,640]{2,1,0:T(8,128)(2,1)} %bitcast.3), calls=%async_computation | async-start | bytes 1310720 | tf_op jit(solution)/shard_map/all_to_all | solution.py:273
  18.9 7.2 %collective-permute-start.1 = (bf16[2048,128]{1,0:T(8,128)(2,1)S(1)}, bf16[2048,128]{1,0:T(8,128)(2,1)S(1)}, u32[]{:S(2)}, u32[]{:S(2)}) collective-permute-start(bf16[2048,128]{1,0:T(8,128)(2,1)S(1)} %after.1.qp_ref.q0_ref), channel_id=1, source_target_pairs={{0,1},{1,0},{2,3},{3,2},{4,5},{5,4},{6,7},{7,6},{8,9},{9,8},{10,11... | collective-permute-start | bytes 1572872 | tf_op jit(solution)/shard_map/ppermute | solution.py:224
  22.7 7.7 %collective-permute-start.3 = (bf16[2048,128]{1,0:T(8,128)(2,1)}, bf16[2048,128]{1,0:T(8,128)(2,1)}, u32[]{:S(2)}, u32[]{:S(2)}) collective-permute-start(bf16[2048,128]{1,0:T(8,128)(2,1)} %collective-permute-done.2.q2_ref), channel_id=1, source_target_pairs={{0,1},{1,0},{2,3},{3,2},{4,5},{5,4},{6,7},{7,6},{8,9},{9,8},{10,11... | collective-permute-start | bytes 1572872 | tf_op jit(solution)/shard_map/ppermute | solution.py:224
  26.1 0.8 %copy-start.2 = (bf16[2048,128]{1,0:T(8,128)(2,1)}, bf16[2048,128]{1,0:T(8,128)(2,1)S(1)}, u32[]{:S(2)}) copy-start(bf16[2048,128]{1,0:T(8,128)(2,1)S(1)} %collective-permute-done.1.q1_ref) | copy-start | bytes 1572868
  30.5 1.0 %copy-start.3 = (bf16[2048,128]{1,0:T(8,128)(2,1)S(1)}, bf16[2048,128]{1,0:T(8,128)(2,1)}, u32[]{:S(2)}) copy-start(bf16[2048,128]{1,0:T(8,128)(2,1)} %copy-done.2) | copy-start | bytes 1572868
  36.3 8.8 %collective-permute-start.7 = (bf16[256,2048]{1,0:T(8,128)(2,1)S(1)}, bf16[256,2048]{1,0:T(8,128)(2,1)S(1)}, u32[]{:S(2)}, u32[]{:S(2)}) collective-permute-start(bf16[256,2048]{1,0:T(8,128)(2,1)S(1)} %get-tuple-element.19), channel_id=1, source_target_pairs={{0,1},{1,0},{2,3},{3,2},{4,5},{5,4},{6,7},{7,6},{8,9},{9,8},{10,11... | collective-permute-start | bytes 3145736 | tf_op jit(solution)/shard_map/ppermute | solution.py:224
  38.7 4.3 %collective-permute-start.5 = (f32[4,2048]{1,0:T(4,128)S(1)}, f32[4,2048]{1,0:T(4,128)S(1)}, u32[]{:S(2)}, u32[]{:S(2)}) collective-permute-start(f32[4,2048]{1,0:T(4,128)S(1)} %get-tuple-element.16.s0), channel_id=1, source_target_pairs={{0,2},{1,3},{2,0},{3,1},{4,6},{5,7},{6,4},{7,5},{8,10},{9,11},{10,... | collective-permute-start | bytes 98312 | tf_op jit(solution)/shard_map/ppermute | solution.py:224
  38.7 5.5 %collective-permute-start.4 = (f32[4,2048]{1,0:T(4,128)S(1)}, f32[4,2048]{1,0:T(4,128)S(1)}, u32[]{:S(2)}, u32[]{:S(2)}) collective-permute-start(f32[4,2048]{1,0:T(4,128)S(1)} %get-tuple-element.16.s0), channel_id=1, source_target_pairs={{0,1},{1,0},{2,3},{3,2},{4,5},{5,4},{6,7},{7,6},{8,9},{9,8},{10,11... | collective-permute-start | bytes 98312 | tf_op jit(solution)/shard_map/ppermute | solution.py:224
  43.0 2.1 %collective-permute-start.6 = (f32[4,2048]{1,0:T(4,128)S(1)}, f32[4,2048]{1,0:T(4,128)S(1)}, u32[]{:S(2)}, u32[]{:S(2)}) collective-permute-start(f32[4,2048]{1,0:T(4,128)S(1)} %collective-permute-done.5.s2), channel_id=1, source_target_pairs={{0,1},{1,0},{2,3},{3,2},{4,5},{5,4},{6,7},{7,6},{8,9},{9,8},{10,11... | collective-permute-start | bytes 98312 | tf_op jit(solution)/shard_map/ppermute | solution.py:224
  45.4 19.8 %collective-permute-start.8 = (bf16[128,2048]{1,0:T(8,128)(2,1)S(1)}, bf16[128,2048]{1,0:T(8,128)(2,1)S(1)}, u32[]{:S(2)}, u32[]{:S(2)}) collective-permute-start(bf16[128,2048]{1,0:T(8,128)(2,1)S(1)} %get-tuple-element.21), channel_id=1, source_target_pairs={{0,2},{1,3},{2,0},{3,1},{4,6},{5,7},{6,4},{7,5},{8,10},{9,11},{10,... | collective-permute-start | bytes 1572872 | tf_op jit(solution)/shard_map/ppermute | solution.py:224
  47.6 22.3 %all-to-all-start.1 = ((bf16[32,16,512]{2,1,0:T(8,128)(2,1)}), bf16[32,16,512]{2,1,0:T(8,128)(2,1)S(1)}, u32[]{:S(2)}, u32[]{:S(2)}) async-start(bf16[32,16,512]{2,1,0:T(8,128)(2,1)} %bitcast.6), calls=%async_computation.1 | async-start | bytes 1048576 | tf_op jit(solution)/shard_map/all_to_all | solution.py:317
  65.3 4.6 %collective-permute-start.9 = (bf16[16,128]{1,0:T(8,128)(2,1)S(1)}, bf16[16,128]{1,0:T(8,128)(2,1)S(1)}, u32[]{:S(2)}, u32[]{:S(2)}) collective-permute-start(bf16[16,128]{1,0:T(8,128)(2,1)S(1)} %slice.4), channel_id=1, source_target_pairs={{0,1},{1,0},{2,3},{3,2},{4,5},{5,4},{6,7},{7,6},{8,9},{9,8},{10,11... | collective-permute-start | bytes 12296 | tf_op jit(solution)/shard_map/ppermute | solution.py:224

commit v3 on v2

--- a/solution.py
+++ b/solution.py
@@ -12,6 +12,7 @@
 LANES = 128
 CHUNK = 64
 TILE = 512
+PARTS = 4
 FLOOR = -1e30
 MASKED = -3e38
 SEQ = ("x", "zl", "y")
@@ -28,6 +29,10 @@
     return pl.BlockSpec(memory_space=pltpu.VMEM)
 
 
+def anywhere():
+    return pl.BlockSpec(memory_space=pl.ANY)
+
+
 def small():
     return pl.BlockSpec(memory_space=pltpu.SMEM)
 
@@ -36,9 +41,8 @@
     return lax.dot_general(a, b, (((da,), (db,)), ((), ())), preferred_element_type=F32)
 
 
-def copy_rows(len_ref, src_ref, packed):
-    start = jnp.int32(0)
-    for h in range(len_ref.shape[1]):
+def copy_rows(len_ref, src_ref, packed, first, last, start):
+    for h in range(first, last):
         size = len_ref[0, h]
         for c in range(0, MAXLEN, CHUNK):
 
@@ -47,6 +51,7 @@
                 packed[pl.ds(start + c, CHUNK), :] = src_ref[h * MAXLEN + c : h * MAXLEN + c + CHUNK, :].astype(F32)
 
         start = start + size
+    return start
 
 
 def pass_on(value_ref, after_ref, out_ref):
@@ -62,22 +67,65 @@
         out_ref[i * size : (i + 1) * size, :] = pair[i % 2]
 
 
-def sum_kernel(share_ref, after_ref, out_ref):
-    size = out_ref.shape[0]
-    total = share_ref[:size, :].astype(F32)
-    for i in range(1, share_ref.shape[0] // size):
-        total = total + share_ref[i * size : (i + 1) * size, :].astype(F32)
-    out_ref[...] = total
-
-
-def pack_query(len_ref, q_ref, qp_ref, packed):
-    copy_rows(len_ref, q_ref, packed)
+def sum_kernel(share_ref, own_ref, other_ref):
+    first = lax.axis_index("zl") == 0
+    size = own_ref.shape[0]
+    totals = []
+    for k in range(2):
+        parts = [
+            share_ref[i + k * size : i + (k + 1) * size, :].astype(F32)
+            for i in range(0, share_ref.shape[0], 2 * size)
+        ]
+        while len(parts) > 1:
+            parts = [a + b for a, b in zip(parts[::2], parts[1::2])]
+        totals.append(parts[0])
+    own_ref[...] = jnp.where(first, totals[0], totals[1])
+    other_ref[...] = jnp.where(first, totals[1], totals[0])
+
+
+def add_kernel(own_ref, recv_ref, out_ref):
+    out_ref[...] = own_ref[...] + recv_ref[...]
+
+
+def row_kernel(neg_ref, id_ref, out_ref, held_id, sems):
+    rows, width = neg_ref.shape
+    load_id = pltpu.make_async_copy(id_ref, held_id, sems.at[0])
+    load = pltpu.make_async_copy(neg_ref, out_ref.at[:, pl.ds(0, width)], sems.at[1])
+    load_id.start()
+    load.start()
+    load_id.wait()
+    shape = (rows, LANES)
+    lane = lax.broadcasted_iota(jnp.int32, shape, 1)
+    ids = jnp.concatenate([held_id[...], jnp.zeros((1, LANES - rows), jnp.int32)], axis=1)
+    own = lane == lax.broadcasted_iota(jnp.int32, shape, 0)
+    value = jnp.sum(jnp.where(own, jnp.broadcast_to(ids, shape), 0), axis=1, keepdims=True)
+    value = jnp.broadcast_to(value, shape)
+    digit = jnp.where(lane == 0, value >> 16, jnp.where(lane == 1, (value >> 8) & 255, value & 255))
+    out_ref[:, width:] = jnp.where(lane < 3, digit, 0).astype(F32).astype(BF16)
+    load.wait()
+
+
+def pack_query(len_ref, q_ref, qp_ref, held_q, held_len, packed, sems):
+    parts = sems.shape[0] - 1
+    size = q_ref.shape[0] // parts
+    rows = [slice(i * size, (i + 1) * size) for i in range(parts)]
+    loads = [pltpu.make_async_copy(q_ref.at[at], held_q.at[at], sems.at[i]) for i, at in enumerate(rows)]
+    lengths = pltpu.make_async_copy(len_ref, held_len, sems.at[parts])
+    lengths.start()
+    for load in loads:
+        load.start()
+    lengths.wait()
+    start = jnp.int32(0)
+    per = size // MAXLEN
+    for i, load in enumerate(loads):
+        load.wait()
+        start = copy_rows(held_len, held_q, packed, i * per, (i + 1) * per, start)
     qp_ref[...] = packed[: qp_ref.shape[0], :].astype(BF16)
 
 
 def pack_positive(len_ref, p_ref, id_ref, qp_ref, pt_ref, part_ref, idp_ref, packed, ids):
     rows = qp_ref.shape[0]
-    copy_rows(len_ref, p_ref, packed)
+    copy_rows(len_ref, p_ref, packed, 0, len_ref.shape[1], jnp.int32(0))
     ones = jnp.ones((16, LANES), BF16)
     for k in range(rows // LANES):
         at = slice(k * LANES, (k + 1) * LANES)
@@ -119,19 +167,17 @@
     place = jnp.where(lane == 0, 65536.0, jnp.where(lane == 1, 256.0, jnp.where(lane == 2, 1.0, 0.0)))
     value = jnp.sum(neg_ref[:, width : width + LANES].astype(F32) * place, axis=1, keepdims=True)
     negid[...] = jnp.broadcast_to(value, negid.shape)
-    for t in range(0, qfull_ref.shape[0], TILE):
-        rows = slice(t, t + TILE)
-        for k, ref in enumerate((q0_ref, q1_ref, q2_ref, q3_ref)):
-            qfull_ref[rows, block_of(member, k)] = ref[rows, :]
-        scores = dot(neg_ref[:, :width], qfull_ref[rows, :], 1, 1)
-        for k in range(TILE // LANES):
-            at = slice(t + k * LANES, t + (k + 1) * LANES)
-            part = jnp.where(negid[...] == idp_ref[:, at], MASKED, scores[:, k * LANES : (k + 1) * LANES])
-            top = jnp.maximum(jnp.max(part, axis=0, keepdims=True), FLOOR)
-            e = jnp.exp(part - top)
-            e_ref[:, at] = e
-            stat_ref[0:1, at] = top
-            stat_ref[1:2, at] = jnp.sum(e, axis=0, keepdims=True)
+    for k, ref in enumerate((q0_ref, q1_ref, q2_ref, q3_ref)):
+        qfull_ref[:, block_of(member, k)] = ref[...]
+    e_ref[...] = dot(neg_ref[:, :width], qfull_ref[...], 1, 1)
+    for k in range(e_ref.shape[1] // LANES):
+        at = slice(k * LANES, (k + 1) * LANES)
+        part = jnp.where(negid[...] == idp_ref[:, at], MASKED, e_ref[:, at])
+        top = jnp.maximum(jnp.max(part, axis=0, keepdims=True), FLOOR)
+        e = jnp.exp(part - top)
+        e_ref[:, at] = e
+        stat_ref[0:1, at] = top
+        stat_ref[1:2, at] = jnp.sum(e, axis=0, keepdims=True)
     stat_ref[2:3, :] = part_ref[...]
     stat_ref[3:4, :] = part_ref[...]
 
@@ -173,47 +219,56 @@
         weights = (e_ref[:, at] * scale_ref[:, at]).astype(BF16)
         part = dot(weights, q_ref[at, :], 1, 0)
         total = part if total is None else total + part
-    x, y, z = lax.axis_size("x"), lax.axis_size("y"), lax.axis_size("zl")
-    size = out_ref.shape[0] // (x * y * z)
-    for i in range(x * y * z):
-        src = ((i // (y * z)) * y + i % y) * z + (i // y) % z
-        out_ref[i * size : (i + 1) * size, :] = total[src * size : (src + 1) * size, :].astype(BF16)
-
-
-def unpack_kernel(len_ref, own_ref, recv_ref, term_ref, pt_ref, out_ref, packed):
+    out_ref[...] = total.astype(BF16)
+
+
+def unpack_kernel(len_ref, own_ref, recv_ref, term_ref, pt_ref, out_ref, packed, staged, sems):
     rows = own_ref.shape[1]
     for k in range(rows // LANES):
         at = slice(k * LANES, (k + 1) * LANES)
         packed[at, :] = (own_ref[:, at] + recv_ref[:, at].astype(F32) + term_ref[:, at] * pt_ref[:, at].astype(F32)).T
     index = lax.broadcasted_iota(jnp.int32, (CHUNK, LANES), 0)
     start = jnp.int32(0)
-    for h in range(len_ref.shape[1]):
-        size = len_ref[0, h]
-        for c in range(0, MAXLEN, CHUNK):
-            at = slice(h * MAXLEN + c, h * MAXLEN + c + CHUNK)
-
-            @pl.when(size > c)
-            def _():
-                out_ref[at, :] = jnp.where(index < size - c, packed[pl.ds(start + c, CHUNK), :], 0.0).astype(BF16)
-
-            @pl.when(size <= c)
-            def _():
-                out_ref[at, :] = jnp.zeros((CHUNK, LANES), BF16)
-
-        start = start + size
+    parts = sems.shape[0]
+    size = out_ref.shape[0] // parts
+    stores = []
+    for i in range(parts):
+        for h in range(i * size // MAXLEN, (i + 1) * size // MAXLEN):
+            count = len_ref[0, h]
+            for c in range(0, MAXLEN, CHUNK):
+                at = slice(h * MAXLEN + c, h * MAXLEN + c + CHUNK)
+
+                @pl.when(count > c)
+                def _():
+                    live = jnp.where(index < count - c, packed[pl.ds(start + c, CHUNK), :], 0.0)
+                    staged[at, :] = live.astype(BF16)
+
+                @pl.when(count <= c)
+                def _():
+                    staged[at, :] = jnp.zeros((CHUNK, LANES), BF16)
+
+            start = start + count
+        at = slice(i * size, (i + 1) * size)
+        stores.append(pltpu.make_async_copy(staged.at[at], out_ref.at[at], sems.at[i]))
+        stores[-1].start()
+    for store in stores:
+        store.wait()
 
 
 def held(value):
     return pltpu.with_memory_space_constraint(value, pltpu.VMEM)
 
 
+def in_hbm(value):
+    return pltpu.with_memory_space_constraint(value, pltpu.HBM)
+
+
 def after(value, other):
-    any_place = pl.BlockSpec(memory_space=pl.ANY)
     return pl.pallas_call(
         pass_on,
         out_shape=pltpu.VMEM(value.shape, value.dtype),
-        in_specs=[any_place, any_place],
-        out_specs=any_place,
+        in_specs=[anywhere()] * 2,
+        out_specs=anywhere(),
         input_output_aliases={0: 0},
         compiler_params=params(),
         name="after",
@@ -234,33 +289,47 @@
     half = 2 * LANES
     vmem = pltpu.VMEM
 
-    digits = jnp.stack([neg_ids // 65536, (neg_ids // 256) % 256, neg_ids % 256], axis=1).astype(BF16)
-    row = jnp.concatenate([negatives, jnp.pad(digits, ((0, 0), (0, LANES - 3)))], axis=1)
+    row = pl.pallas_call(
+        row_kernel,
+        out_shape=vmem((own_neg, width + LANES), BF16),
+        in_specs=[anywhere()] * 2,
+        out_specs=whole(),
+        scratch_shapes=[vmem((1, own_neg), jnp.int32), pltpu.SemaphoreType.DMA((2,))],
+        compiler_params=params(),
+        name="negative_rows",
+    )(in_hbm(negatives), in_hbm(neg_ids.reshape(1, own_neg)))
 
     other = lax.ppermute(row, "zl", [(i, near - 1 - i) for i in range(near)])
     qp = pl.pallas_call(
         pack_query,
         out_shape=vmem((live, LANES), BF16),
-        in_specs=[small(), whole()],
+        in_specs=[anywhere()] * 2,
         out_specs=whole(),
-        scratch_shapes=[vmem((live + MAXLEN, LANES), F32)],
+        scratch_shapes=[
+            vmem((slots, LANES), BF16),
+            pltpu.SMEM(lengths.shape, jnp.int32),
+            vmem((live + MAXLEN, LANES), F32),
+            pltpu.SemaphoreType.DMA((PARTS + 1,)),
+        ],
         compiler_params=params(),
         name="pack_query",
-    )(lengths, query)
+    )(in_hbm(lengths), in_hbm(query))
     qp = after(qp, other)
     q2 = swap(qp, 2, groups)
-    q1 = swap(qp, 1, groups)
-    q3 = swap(q2, 1, groups)
-
     pt, part, idp = pl.pallas_call(
         pack_positive,
-        out_shape=(vmem((LANES, live), BF16), vmem((1, live), F32), vmem((1, live), F32)),
+        out_shape=(jax.ShapeDtypeStruct((LANES, live), BF16), vmem((1, live), F32), vmem((1, live), F32)),
         in_specs=[small(), whole(), whole(), whole()],
         out_specs=(whole(), whole(), whole()),
         scratch_shapes=[vmem((live + MAXLEN, LANES), F32), vmem((live // LANES + 8, LANES), jnp.int32)],
         compiler_params=params(),
         name="pack_positive",
     )(lengths, pos_emb, pos_ids.reshape(slots // LANES, LANES), held(qp))
+
+    q2 = after(q2, part)
+    qp = after(qp, q2)
+    q1 = swap(qp, 1, groups)
+    q3 = swap(q2, 1, groups)
 
     copies = pl.pallas_call(
         copies_kernel,
@@ -314,23 +383,36 @@
         compiler_params=params(),
         name="item_products",
     )(held(scale), held(e), held(qfull))
-    shares = lax.all_to_all(items, SEQ, split_axis=0, concat_axis=0, tiled=True)
-    last = swap(recv2[:16, :LANES], 1, groups)
+    shares = lax.all_to_all(items, ("x", "y"), split_axis=0, concat_axis=0, tiled=True)
+    own_sum, other_sum = pl.pallas_call(
+        sum_kernel,
+        out_shape=(vmem((own_neg, width), F32), vmem((own_neg, width), F32)),
+        in_specs=[whole()],
+        out_specs=(whole(), whole()),
+        compiler_params=params(),
+        name="sum_shares",
+    )(held(shares))
+    other_sum = after(other_sum, recv2)
+    recv_sum = lax.ppermute(other_sum, "zl", [(i, near - 1 - i) for i in range(near)])
     grad_items = pl.pallas_call(
-        sum_kernel,
+        add_kernel,
         out_shape=jax.ShapeDtypeStruct((own_neg, width), F32),
-        in_specs=[whole(), pl.BlockSpec(memory_space=pl.ANY)],
+        in_specs=[whole(), whole()],
         out_specs=whole(),
         compiler_params=params(),
-        name="sum_shares",
-    )(shares, last)
+        name="add_neighbour",
+    )(held(own_sum), held(recv_sum))
 
     grad_query = pl.pallas_call(
         unpack_kernel,
         out_shape=jax.ShapeDtypeStruct((slots, LANES), BF16),
         in_specs=[small()] + [whole()] * 4,
-        out_specs=whole(),
-        scratch_shapes=[vmem((live + MAXLEN, LANES), F32)],
+        out_specs=anywhere(),
+        scratch_shapes=[
+            vmem((live + MAXLEN, LANES), F32),
+            vmem((slots, LANES), BF16),
+            pltpu.SemaphoreType.DMA((PARTS,)),
+        ],
         compiler_params=params(),
         name="unpack",
     )(lengths, held(own), held(recv2), held(term), held(pt))

time: 71 us -> 62.3 us (0.88)
  the two profiles are of different devices: /device:TPU:1 before, /device:TPU:0 now
where the time goes in v3:
time: 62.3 us; the launch traced here: 62 us
  waiting for transfers between devices  16.6 us (27%)
  blocking collectives  15.6 us (25%)
  starting transfers between devices  15.1 us (24%)
  Pallas kernels  13.9 us (22%)
  between operations  0.78 us (1%)
    all_to_all x1, blocking collectives, shards(): lax.all_to_all(items, ('x', 'y'), split_axis=0, concat_axis=0, tiled=True)  15.6 us
    all_to_all x1, waiting for transfers between devices, shards(): lax.all_to_all(copies, ('x', 'y'), split_axis=0, concat_axis=0, tiled=True)  8.11 us
    ppermute x8, waiting for transfers between devices, swap(): return lax.ppermute(value, 'grp', [(g, g ^ step) for g in range(groups)])  7.65 us
    all_to_all x1, starting transfers between devices, shards(): lax.all_to_all(copies, ('x', 'y'), split_axis=0, concat_axis=0, tiled=True)  7.03 us
    ppermute x8, starting transfers between devices, swap(): return lax.ppermute(value, 'grp', [(g, g ^ step) for g in range(groups)])  5.44 us
    pallas_call x1, Pallas kernels, shards(): pl.pallas_call(unpack_kernel, out_shape=jax.ShapeDtypeStruct((slots, LANE...  2.7 us
    pallas_call x1, Pallas kernels, shards(): pl.pallas_call(scores_kernel, out_shape=(vmem((live, width), BF16), vmem(...  2.42 us
    ppermute x1, starting transfers between devices, shards(): other = lax.ppermute(row, 'zl', [(i, near - 1 - i) for i in range(near)])  2.08 us
  transfers between devices with their start and end apart: 11, of which 6 were waited for; matrix products, arithmetic and copies ran while one was open for 0% of the time, Pallas kernels for 14%

profile of v3, /device:TPU:0, one launch (start us, length us, event | category | flops | bytes accessed | tf_op | source)
XLA Modules:
  0.0 62.0 jit_solution(8892711032380089689)
XLA Ops:
  0.6 0.8 %negative_rows.1.row_ref = bf16[16,640]{1,0:T(8,128)(2,1)S(1)} custom-call(bf16[16,512]{1,0:T(8,128)(2,1)} %neg_ref.1, s32[1,16]{1,0:T(1,128)} %bitcast.11), custom_call_target="tpu_custom_call" | custom-call | tf_op jit(solution)/shard_map/negative_rows/pallas_call | solution.py:292
  1.4 2.1 %collective-permute-start = (bf16[16,640]{1,0:T(8,128)(2,1)S(1)}, bf16[16,640]{1,0:T(8,128)(2,1)S(1)}, u32[]{:S(2)}, u32[]{:S(2)}) collective-permute-start(bf16[16,640]{1,0:T(8,128)(2,1)S(1)} %negative_rows.1.row_ref), channel_id=1, source_target_pairs={{0,16},{16,0},{1,17},{17,1},{2,18},{18,2},{3,19},{19,3},{4,20},{20... | collective-permute-start | bytes 61448 | tf_op jit(solution)/shard_map/ppermute | solution.py:302
  3.5 1.7 %pack_query.1.value_ref = bf16[2048,128]{1,0:T(8,128)(2,1)S(1)} custom-call(s32[1,32]{1,0:T(1,128)} %len_ref.5, bf16[6144,128]{1,0:T(8,128)(2,1)} %q_ref.1), custom_call_target="tpu_custom_call" | custom-call | tf_op jit(solution)/shard_map/pack_query/pallas_call | solution.py:303
  5.3 4.0 %collective-permute-start.1 = (bf16[2048,128]{1,0:T(8,128)(2,1)S(1)}, bf16[2048,128]{1,0:T(8,128)(2,1)S(1)}, u32[]{:S(2)}, u32[]{:S(2)}) collective-permute-start(bf16[2048,128]{1,0:T(8,128)(2,1)S(1)} %after.4.qp_ref.value_ref), channel_id=1, source_target_pairs={{0,2},{1,3},{2,0},{3,1},{4,6},{5,7},{6,4},{7,5},{8,10},{9,11},{10,... | collective-permute-start | bytes 1572872 | tf_op jit(solution)/shard_map/ppermute | solution.py:279
  9.3 0.9 %copies.1 = bf16[512,640]{1,0:T(8,128)(2,1)} custom-call(bf16[16,640]{1,0:T(8,128)(2,1)S(1)} %negative_rows.1.row_ref, bf16[16,640]{1,0:T(8,128)(2,1)S(1)} %collective-permute-done.other_ref.after_ref), custom_call_target="tpu_custom_call" | custom-call | tf_op jit(solution)/shard_map/copies/pallas_call | solution.py:334
  10.2 7.0 %all-to-all-start = ((bf16[16,32,640]{2,1,0:T(8,128)(2,1)}), bf16[16,32,640]{2,1,0:T(8,128)(2,1)S(1)}, u32[]{:S(2)}, u32[]{:S(2)}) async-start(bf16[16,32,640]{2,1,0:T(8,128)(2,1)} %bitcast.1), calls=%async_computation | async-start | bytes 1310720 | tf_op jit(solution)/shard_map/all_to_all | solution.py:342
  17.2 1.8 %pack_positive.1 = (bf16[128,2048]{1,0:T(8,128)(2,1)S(1)}, f32[1,2048]{1,0:T(1,128)S(1)}, f32[1,2048]{1,0:T(1,128)S(1)}) custom-call(s32[1,32]{1,0:T(1,128)S(1)} %copy-done.4, bf16[6144,128]{1,0:T(8,128)(2,1)S(1)} %copy-done, s32[48,128]{1,0:T(8,128)S(1)} %bitcast.10, bf16[2048,128]{1,0:T(8,128)(2,1)S(1)} %after.4.qp_ref.value_ref), custom_call_target="tpu_custom_call" | custom-call | tf_op jit(solution)/shard_map/pack_positive/pallas_call | solution.py:319
  19.1 1.5 %collective-permute-done.1.value_ref = bf16[2048,128]{1,0:T(8,128)(2,1)S(1)} collective-permute-done((bf16[2048,128]{1,0:T(8,128)(2,1)S(1)}, bf16[2048,128]{1,0:T(8,128)(2,1)S(1)}, u32[]{:S(2)}, u32[]{:S(2)}) %collective-permute-start.1) | collective-permute-done | bytes 524320 | tf_op jit(solution)/shard_map/ppermute | solution.py:279
  20.5 0.5 collective-permute-start.3
  21.0 8.1 %all-to-all-done = bf16[16,32,640]{2,1,0:T(8,128)(2,1)S(1)} async-done(((bf16[16,32,640]{2,1,0:T(8,128)(2,1)}), bf16[16,32,640]{2,1,0:T(8,128)(2,1)S(1)}, u32[]{:S(2)}, u32[]{:S(2)}) %all-to-all-start) | async-done | bytes 655392 | tf_op jit(solution)/shard_map/all_to_all | solution.py:342
  29.2 2.4 %scores.1 = (bf16[2048,512]{1,0:T(8,128)(2,1)S(1)}, f32[512,2048]{1,0:T(8,128)S(1)}, f32[4,2048]{1,0:T(4,128)S(1)}) custom-call(bf16[512,640]{1,0:T(8,128)(2,1)S(1)} %bitcast.6, bf16[2048,128]{1,0:T(8,128)(2,1)S(1)} %after.6.q0_ref, bf16[2048,128]{1,0:T(8,128)(2,1)S(1)} %collective-permute-done.2.q1_ref, bf16[2048,128]{1,0:T(8,128)(2,1)S(1)} %after.5.after_ref.q2_ref, ...), custom_call_target="tpu_custom_call" | custom-call | tf_op jit(solution)/shard_map/scores/pallas_call | solution.py:345
  31.6 1.3 %row_products.1 = (f32[256,2048]{1,0:T(8,128)S(1)}, bf16[256,2048]{1,0:T(8,128)(2,1)S(1)}) custom-call(bf16[512,640]{1,0:T(8,128)(2,1)S(1)} %bitcast.7, f32[512,2048]{1,0:T(8,128)S(1)} %get-tuple-element.19.e_ref), custom_call_target="tpu_custom_call" | custom-call | tf_op jit(solution)/shard_map/row_products/pallas_call | solution.py:357
  33.0 0.4 collective-permute-start.5
  33.4 0.2 collective-permute-start.4
  33.5 5.0 %collective-permute-done.5.s2 = f32[4,2048]{1,0:T(4,128)S(1)} collective-permute-done((f32[4,2048]{1,0:T(4,128)S(1)}, f32[4,2048]{1,0:T(4,128)S(1)}, u32[]{:S(2)}, u32[]{:S(2)}) %collective-permute-start.5) | collective-permute-done | bytes 32800 | tf_op jit(solution)/shard_map/ppermute | solution.py:279
  38.5 1.2 %collective-permute-done.6.s3 = f32[4,2048]{1,0:T(4,128)S(1)} collective-permute-done((f32[4,2048]{1,0:T(4,128)S(1)}, f32[4,2048]{1,0:T(4,128)S(1)}, u32[]{:S(2)}, u32[]{:S(2)}) %collective-permute-start.6) | collective-permute-done | bytes 32800 | tf_op jit(solution)/shard_map/ppermute | solution.py:279
  39.7 0.3 combine.1
  40.0 0.4 collective-permute-start.8
  40.4 1.2 %item_products.1 = bf16[512,512]{1,0:T(8,128)(2,1)S(1)} custom-call(f32[1,2048]{1,0:T(1,128)S(1)} %get-tuple-element.26.scale_ref, f32[512,2048]{1,0:T(8,128)S(1)} %get-tuple-element.19.e_ref, bf16[2048,512]{1,0:T(8,128)(2,1)S(1)} %get-tuple-element.27.q_ref), custom_call_target="tpu_custom_call" | custom-call | tf_op jit(solution)/shard_map/item_products/pallas_call | solution.py:378
  41.7 15.6 %all_to_all.22 = bf16[16,32,512]{2,1,0:T(8,128)(2,1)S(1)} all-to-all(bf16[16,32,512]{2,1,0:T(8,128)(2,1)S(1)} %bitcast.9), channel_id=1, replica_groups=mesh['x'=4,'zl'=2,'y'=4,'grp'=4] {'x','y'}, dimensions={0} | all-to-all | bytes 1048576 | tf_op jit(solution)/shard_map/all_to_all | solution.py:386
  57.3 0.6 collective-permute-start.9
  57.9 2.7 %unpack.1 = bf16[6144,128]{1,0:T(8,128)(2,1)} custom-call(s32[1,32]{1,0:T(1,128)S(1)} %copy-done.4, f32[128,2048]{1,0:T(8,128)S(1)} %get-tuple-element.22.own_ref, bf16[128,2048]{1,0:T(8,128)(2,1)S(1)} %collective-permute-done.8.recv_ref.after_ref, f32[1,2048]{1,0:T(1,128)S(1)} %get-tuple-element.24.term_ref, bf16[128,2048]{1,0:T(8,128)(2,1)S(1)} %copy-done.2), custom_call_target="tpu_custom_call" | custom-call | tf_op jit(solution)/shard_map/unpack/pallas_call | solution.py:406
  60.6 0.7 %collective-permute-done.9.recv_ref = f32[16,512]{1,0:T(8,128)S(1)} collective-permute-done((f32[16,512]{1,0:T(8,128)S(1)}, f32[16,512]{1,0:T(8,128)S(1)}, u32[]{:S(2)}, u32[]{:S(2)}) %collective-permute-start.9) | collective-permute-done | bytes 32800 | tf_op jit(solution)/shard_map/ppermute | solution.py:396
  61.3 0.6 add_neighbour.1
  (24 shorter events, 0.3 us)
Async XLA Ops:
  1.4 15.8 %copy-start = (bf16[6144,128]{1,0:T(8,128)(2,1)S(1)}, bf16[6144,128]{1,0:T(8,128)(2,1)}, u32[]{:S(2)}) copy-start(bf16[6144,128]{1,0:T(8,128)(2,1)} %p_ref.1) | copy-start | bytes 4718596
  1.4 15.8 %copy-start.3 = (s32[6144]{0:T(1024)S(1)}, s32[6144]{0:T(1024)}, u32[]{:S(2)}) copy-start(s32[6144]{0:T(1024)} %param.8) | copy-start | bytes 73732
  1.4 15.8 %copy-start.4 = (s32[1,32]{1,0:T(1,128)S(1)}, s32[1,32]{1,0:T(1,128)}, u32[]{:S(2)}) copy-start(s32[1,32]{1,0:T(1,128)} %len_ref.5) | copy-start | bytes 388
  1.4 3.9 %collective-permute-start = (bf16[16,640]{1,0:T(8,128)(2,1)S(1)}, bf16[16,640]{1,0:T(8,128)(2,1)S(1)}, u32[]{:S(2)}, u32[]{:S(2)}) collective-permute-start(bf16[16,640]{1,0:T(8,128)(2,1)S(1)} %negative_rows.1.row_ref), channel_id=1, source_target_pairs={{0,16},{16,0},{1,17},{17,1},{2,18},{18,2},{3,19},{19,3},{4,20},{20... | collective-permute-start | bytes 61448 | tf_op jit(solution)/shard_map/ppermute | solution.py:302
  5.3 15.2 %collective-permute-start.1 = (bf16[2048,128]{1,0:T(8,128)(2,1)S(1)}, bf16[2048,128]{1,0:T(8,128)(2,1)S(1)}, u32[]{:S(2)}, u32[]{:S(2)}) collective-permute-start(bf16[2048,128]{1,0:T(8,128)(2,1)S(1)} %after.4.qp_ref.value_ref), channel_id=1, source_target_pairs={{0,2},{1,3},{2,0},{3,1},{4,6},{5,7},{6,4},{7,5},{8,10},{9,11},{10,... | collective-permute-start | bytes 1572872 | tf_op jit(solution)/shard_map/ppermute | solution.py:279
  10.2 19.0 %all-to-all-start = ((bf16[16,32,640]{2,1,0:T(8,128)(2,1)}), bf16[16,32,640]{2,1,0:T(8,128)(2,1)S(1)}, u32[]{:S(2)}, u32[]{:S(2)}) async-start(bf16[16,32,640]{2,1,0:T(8,128)(2,1)} %bitcast.1), calls=%async_computation | async-start | bytes 1310720 | tf_op jit(solution)/shard_map/all_to_all | solution.py:342
  19.1 1.5 %copy-start.1 = (bf16[128,2048]{1,0:T(8,128)(2,1)}, bf16[128,2048]{1,0:T(8,128)(2,1)S(1)}, u32[]{:S(2)}) copy-start(bf16[128,2048]{1,0:T(8,128)(2,1)S(1)} %get-tuple-element.25.pt_ref) | copy-start | bytes 1572868
  20.5 8.6 %collective-permute-start.2 = (bf16[2048,128]{1,0:T(8,128)(2,1)S(1)}, bf16[2048,128]{1,0:T(8,128)(2,1)S(1)}, u32[]{:S(2)}, u32[]{:S(2)}) collective-permute-start(bf16[2048,128]{1,0:T(8,128)(2,1)S(1)} %after.6.q0_ref), channel_id=1, source_target_pairs={{0,1},{1,0},{2,3},{3,2},{4,5},{5,4},{6,7},{7,6},{8,9},{9,8},{10,11... | collective-permute-start | bytes 1572872 | tf_op jit(solution)/shard_map/ppermute | solution.py:279
  20.5 8.6 %collective-permute-start.3 = (bf16[2048,128]{1,0:T(8,128)(2,1)S(1)}, bf16[2048,128]{1,0:T(8,128)(2,1)S(1)}, u32[]{:S(2)}, u32[]{:S(2)}) collective-permute-start(bf16[2048,128]{1,0:T(8,128)(2,1)S(1)} %after.5.after_ref.q2_ref), channel_id=1, source_target_pairs={{0,1},{1,0},{2,3},{3,2},{4,5},{5,4},{6,7},{7,6},{8,9},{9,8},{10,11... | collective-permute-start | bytes 1572872 | tf_op jit(solution)/shard_map/ppermute | solution.py:279
  32.9 6.8 %collective-permute-start.7 = (bf16[256,2048]{1,0:T(8,128)(2,1)S(1)}, bf16[256,2048]{1,0:T(8,128)(2,1)S(1)}, u32[]{:S(2)}, u32[]{:S(2)}) collective-permute-start(bf16[256,2048]{1,0:T(8,128)(2,1)S(1)} %get-tuple-element.21), channel_id=1, source_target_pairs={{0,1},{1,0},{2,3},{3,2},{4,5},{5,4},{6,7},{7,6},{8,9},{9,8},{10,11... | collective-permute-start | bytes 3145736 | tf_op jit(solution)/shard_map/ppermute | solution.py:279
  33.0 5.5 %collective-permute-start.5 = (f32[4,2048]{1,0:T(4,128)S(1)}, f32[4,2048]{1,0:T(4,128)S(1)}, u32[]{:S(2)}, u32[]{:S(2)}) collective-permute-start(f32[4,2048]{1,0:T(4,128)S(1)} %get-tuple-element.18.s0), channel_id=1, source_target_pairs={{0,2},{1,3},{2,0},{3,1},{4,6},{5,7},{6,4},{7,5},{8,10},{9,11},{10,... | collective-permute-start | bytes 98312 | tf_op jit(solution)/shard_map/ppermute | solution.py:279
  33.4 5.1 %collective-permute-start.4 = (f32[4,2048]{1,0:T(4,128)S(1)}, f32[4,2048]{1,0:T(4,128)S(1)}, u32[]{:S(2)}, u32[]{:S(2)}) collective-permute-start(f32[4,2048]{1,0:T(4,128)S(1)} %get-tuple-element.18.s0), channel_id=1, source_target_pairs={{0,1},{1,0},{2,3},{3,2},{4,5},{5,4},{6,7},{7,6},{8,9},{9,8},{10,11... | collective-permute-start | bytes 98312 | tf_op jit(solution)/shard_map/ppermute | solution.py:279
  38.5 1.2 %collective-permute-start.6 = (f32[4,2048]{1,0:T(4,128)S(1)}, f32[4,2048]{1,0:T(4,128)S(1)}, u32[]{:S(2)}, u32[]{:S(2)}) collective-permute-start(f32[4,2048]{1,0:T(4,128)S(1)} %collective-permute-done.5.s2), channel_id=1, source_target_pairs={{0,1},{1,0},{2,3},{3,2},{4,5},{5,4},{6,7},{7,6},{8,9},{9,8},{10,11... | collective-permute-start | bytes 98312 | tf_op jit(solution)/shard_map/ppermute | solution.py:279
  40.0 17.3 %collective-permute-start.8 = (bf16[128,2048]{1,0:T(8,128)(2,1)S(1)}, bf16[128,2048]{1,0:T(8,128)(2,1)S(1)}, u32[]{:S(2)}, u32[]{:S(2)}) collective-permute-start(bf16[128,2048]{1,0:T(8,128)(2,1)S(1)} %get-tuple-element.23), channel_id=1, source_target_pairs={{0,2},{1,3},{2,0},{3,1},{4,6},{5,7},{6,4},{7,5},{8,10},{9,11},{10,... | collective-permute-start | bytes 1572872 | tf_op jit(solution)/shard_map/ppermute | solution.py:279
  41.7 16.3 %copy-start.2 = (bf16[128,2048]{1,0:T(8,128)(2,1)S(1)}, bf16[128,2048]{1,0:T(8,128)(2,1)}, u32[]{:S(2)}) copy-start(bf16[128,2048]{1,0:T(8,128)(2,1)} %copy-done.1) | copy-start | bytes 1572868
  57.3 4.0 %collective-permute-start.9 = (f32[16,512]{1,0:T(8,128)S(1)}, f32[16,512]{1,0:T(8,128)S(1)}, u32[]{:S(2)}, u32[]{:S(2)}) collective-permute-start(f32[16,512]{1,0:T(8,128)S(1)} %after.7), channel_id=1, source_target_pairs={{0,16},{16,0},{1,17},{17,1},{2,18},{18,2},{3,19},{19,3},{4,20},{20... | collective-permute-start | bytes 98312 | tf_op jit(solution)/shard_map/ppermute | solution.py:396

commit v4 on v3

--- a/solution.py
+++ b/solution.py
@@ -23,6 +23,10 @@
 
 def params():
     return pltpu.CompilerParams(vmem_limit_bytes=VMEM_BYTES)
+
+
+def weight(micros):
+    return pl.CostEstimate(flops=int(micros * 1e9), transcendentals=0, bytes_accessed=0)
 
 
 def whole():
@@ -160,15 +164,18 @@
     return pl.ds(pl.multiple_of((order ^ step) * LANES, LANES), LANES)
 
 
-def scores_kernel(neg_ref, q0_ref, q1_ref, q2_ref, q3_ref, idp_ref, part_ref, qfull_ref, e_ref, stat_ref, negid):
+def place_kernel(steps, *refs):
     member = lax.axis_index("grp")
+    for step, ref in zip(steps, refs[:2]):
+        refs[-1][:, block_of(member, step)] = ref[...]
+
+
+def scores_kernel(neg_ref, qfull_ref, idp_ref, part_ref, e_ref, stat_ref, negid):
     width = 4 * LANES
     lane = lax.broadcasted_iota(jnp.int32, (1, LANES), 1)
     place = jnp.where(lane == 0, 65536.0, jnp.where(lane == 1, 256.0, jnp.where(lane == 2, 1.0, 0.0)))
     value = jnp.sum(neg_ref[:, width : width + LANES].astype(F32) * place, axis=1, keepdims=True)
     negid[...] = jnp.broadcast_to(value, negid.shape)
-    for k, ref in enumerate((q0_ref, q1_ref, q2_ref, q3_ref)):
-        qfull_ref[:, block_of(member, k)] = ref[...]
     e_ref[...] = dot(neg_ref[:, :width], qfull_ref[...], 1, 1)
     for k in range(e_ref.shape[1] // LANES):
         at = slice(k * LANES, (k + 1) * LANES)
@@ -194,7 +201,7 @@
         send_ref[:, at] = out[half:, :].astype(BF16)
 
 
-def combine_kernel(s0, s1, s2, s3, keep_ref, recv_ref, own_ref, send_ref, term_ref, scale_ref):
+def norm_kernel(s0, s1, s2, s3, after_ref, scale_ref, other_ref, term_ref):
     refs = (s0, s1, s2, s3)
     positive = s0[2:3, :] + s1[2:3, :] + s2[2:3, :] + s3[2:3, :]
     top = positive
@@ -204,10 +211,13 @@
     for ref in refs:
         total = total + ref[1:2, :] * jnp.exp(ref[0:1, :] - top)
     log_total = top + jnp.log(total)
-    mine = jnp.exp(s0[0:1, :] - log_total)
-    other = jnp.exp(s1[0:1, :] - log_total)
-    scale_ref[...] = mine
+    scale_ref[...] = jnp.exp(s0[0:1, :] - log_total)
+    other_ref[...] = jnp.exp(s1[0:1, :] - log_total)
     term_ref[...] = jnp.exp(positive - log_total) - 1.0
+
+
+def combine_kernel(scale_ref, other_ref, keep_ref, recv_ref, after_ref, own_ref, send_ref):
+    mine, other = scale_ref[...], other_ref[...]
     send_ref[...] = (keep_ref[LANES:, :] * mine + recv_ref[LANES:, :].astype(F32) * other).astype(BF16)
     own_ref[...] = keep_ref[:LANES, :] * mine + recv_ref[:LANES, :].astype(F32) * other
 
@@ -342,17 +352,34 @@
     pool = lax.all_to_all(copies, ("x", "y"), split_axis=0, concat_axis=0, tiled=True)
     pool = held(pool)
 
-    qfull, e, stat = pl.pallas_call(
+    qfull = pl.pallas_call(
+        partial(place_kernel, (0, 2)),
+        out_shape=vmem((live, width), BF16),
+        in_specs=[whole()] * 2,
+        out_specs=whole(),
+        compiler_params=params(),
+        name="place_own",
+    )(held(qp), held(q2))
+    qfull = pl.pallas_call(
+        partial(place_kernel, (1, 3)),
+        out_shape=vmem((live, width), BF16),
+        in_specs=[whole()] * 3,
+        out_specs=whole(),
+        input_output_aliases={2: 0},
+        compiler_params=params(),
+        name="place_near",
+    )(held(q1), held(q3), held(qfull))
+    qfull = held(qfull)
+    e, stat = pl.pallas_call(
         scores_kernel,
-        out_shape=(vmem((live, width), BF16), vmem((negs, live), F32), vmem((4, live), F32)),
-        in_specs=[whole()] * 7,
-        out_specs=(whole(), whole(), whole()),
+        out_shape=(vmem((negs, live), F32), vmem((4, live), F32)),
+        in_specs=[whole()] * 4,
+        out_specs=(whole(), whole()),
         scratch_shapes=[vmem((negs, LANES), F32)],
         compiler_params=params(),
         name="scores",
-    )(pool, held(qp), held(q1), held(q2), held(q3), held(idp), held(part))
-    stat2 = swap(stat, 2, groups)
-    stats = [held(s) for s in (stat, swap(stat, 1, groups), stat2, swap(stat2, 1, groups))]
+    )(pool, qfull, held(idp), held(part))
+    stats = [held(s) for s in (stat, swap(stat, 1, groups), swap(stat, 2, groups), swap(stat, 3, groups))]
 
     keep, send = pl.pallas_call(
         rows_kernel,
@@ -365,24 +392,33 @@
     )(pool, held(e))
     recv = swap(send, 1, groups)
 
-    own, onward, term, scale = pl.pallas_call(
-        combine_kernel,
-        out_shape=(vmem((LANES, live), F32), vmem((LANES, live), BF16), vmem((1, live), F32), vmem((1, live), F32)),
-        in_specs=[whole()] * 6,
-        out_specs=(whole(), whole(), whole(), whole()),
-        compiler_params=params(),
-        name="combine",
-    )(*stats, held(keep), held(recv))
-    recv2 = swap(onward, 2, groups)
-
+    scale, other_scale, term = pl.pallas_call(
+        norm_kernel,
+        out_shape=(vmem((1, live), F32),) * 3,
+        in_specs=[whole()] * 4 + [anywhere()],
+        out_specs=(whole(),) * 3,
+        compiler_params=params(),
+        name="norm",
+    )(*stats, keep)
     items = pl.pallas_call(
         items_kernel,
         out_shape=vmem((negs, width), BF16),
         in_specs=[whole()] * 3,
         out_specs=whole(),
+        cost_estimate=weight(50),
         compiler_params=params(),
         name="item_products",
-    )(held(scale), held(e), held(qfull))
+    )(held(scale), held(e), qfull)
+    own, onward = pl.pallas_call(
+        combine_kernel,
+        out_shape=(vmem((LANES, live), F32), vmem((LANES, live), BF16)),
+        in_specs=[whole()] * 4 + [anywhere()],
+        out_specs=(whole(), whole()),
+        compiler_params=params(),
+        name="combine",
+    )(held(scale), held(other_scale), held(keep), held(recv), items)
+    recv2 = swap(onward, 2, groups)
+
     shares = lax.all_to_all(items, ("x", "y"), split_axis=0, concat_axis=0, tiled=True)
     own_sum, other_sum = pl.pallas_call(
         sum_kernel,

time: 62.3 us -> 61.3 us (0.984)
  waiting for transfers between devices: 16.6 us -> 9.91 us
  starting transfers between devices: 15.1 us -> 20.5 us
  Pallas kernels: 13.9 us -> 14.9 us
  blocking collectives: 15.6 us -> 14.8 us
    ppermute x8, starting transfers between devices: 5.44 us -> 10.8 us  [swap(): return lax.ppermute(value, 'grp', [(g, g ^ step) for g in range(groups)])]
    ppermute x8, waiting for transfers between devices: 7.65 us -> 3.62 us  [swap(): return lax.ppermute(value, 'grp', [(g, g ^ step) for g in range(groups)])]
    all_to_all x1, waiting for transfers between devices: 8.11 us -> 5.46 us  [shards(): lax.all_to_all(copies, ('x', 'y'), split_axis=0, concat_axis=0, tiled=True)]
    pallas_call x1 -> x4, Pallas kernels: 2.42 us -> 3.45 us  [the longest x1 1.96 us: shards(): pl.pallas_call(scores_kernel, out_shape=(vmem((negs, live), F32), vmem((4...]
    all_to_all x1, blocking collectives: 15.6 us -> 14.8 us  [shards(): lax.all_to_all(items, ('x', 'y'), split_axis=0, concat_axis=0, tiled=True)]
  transfers between devices with their start and end apart: 11 -> 11, of which waited for: 6 -> 8; matrix products, arithmetic and copies ran while one was open for 0% -> 0% of each run, Pallas kernels for 14% -> 18%
where the time goes in v4:
time: 61.3 us; the launch traced here: 60.9 us
  starting transfers between devices  20.5 us (33%)
  Pallas kernels  14.9 us (24%)
  blocking collectives  14.8 us (24%)
  waiting for transfers between devices  9.91 us (16%)
  between operations  0.79 us (1%)
    all_to_all x1, blocking collectives, shards(): lax.all_to_all(items, ('x', 'y'), split_axis=0, concat_axis=0, tiled=True)  14.8 us
    ppermute x8, starting transfers between devices, swap(): return lax.ppermute(value, 'grp', [(g, g ^ step) for g in range(groups)])  10.8 us
    all_to_all x1, starting transfers between devices, shards(): lax.all_to_all(copies, ('x', 'y'), split_axis=0, concat_axis=0, tiled=True)  7.03 us
    all_to_all x1, waiting for transfers between devices, shards(): lax.all_to_all(copies, ('x', 'y'), split_axis=0, concat_axis=0, tiled=True)  5.46 us
    ppermute x8, waiting for transfers between devices, swap(): return lax.ppermute(value, 'grp', [(g, g ^ step) for g in range(groups)])  3.62 us
    pallas_call x1, Pallas kernels, shards(): pl.pallas_call(unpack_kernel, out_shape=jax.ShapeDtypeStruct((slots, LANE...  2.69 us
    ppermute x1, starting transfers between devices, shards(): other = lax.ppermute(row, 'zl', [(i, near - 1 - i) for i in range(near)])  2.08 us
    pallas_call x1, Pallas kernels, shards(): pl.pallas_call(scores_kernel, out_shape=(vmem((negs, live), F32), vmem((4...  1.96 us
  transfers between devices with their start and end apart: 11, of which 8 were waited for; matrix products, arithmetic and copies ran while one was open for 0% of the time, Pallas kernels for 18%

profile of v4, /device:TPU:0, one launch (start us, length us, event | category | flops | bytes accessed | tf_op | source)
XLA Modules:
  0.0 60.9 jit_solution(8541549636954488156)
XLA Ops:
  0.6 0.8 %negative_rows.1.row_ref = bf16[16,640]{1,0:T(8,128)(2,1)S(1)} custom-call(bf16[16,512]{1,0:T(8,128)(2,1)} %neg_ref.1, s32[1,16]{1,0:T(1,128)} %bitcast.11), custom_call_target="tpu_custom_call" | custom-call | tf_op jit(solution)/shard_map/negative_rows/pallas_call | solution.py:302
  1.4 2.1 %collective-permute-start = (bf16[16,640]{1,0:T(8,128)(2,1)S(1)}, bf16[16,640]{1,0:T(8,128)(2,1)S(1)}, u32[]{:S(2)}, u32[]{:S(2)}) collective-permute-start(bf16[16,640]{1,0:T(8,128)(2,1)S(1)} %negative_rows.1.row_ref), channel_id=1, source_target_pairs={{0,16},{16,0},{1,17},{17,1},{2,18},{18,2},{3,19},{19,3},{4,20},{20... | collective-permute-start | bytes 61448 | tf_op jit(solution)/shard_map/ppermute | solution.py:312
  3.5 1.7 %pack_query.1.value_ref = bf16[2048,128]{1,0:T(8,128)(2,1)S(1)} custom-call(s32[1,32]{1,0:T(1,128)} %len_ref.5, bf16[6144,128]{1,0:T(8,128)(2,1)} %q_ref.1), custom_call_target="tpu_custom_call" | custom-call | tf_op jit(solution)/shard_map/pack_query/pallas_call | solution.py:313
  5.3 4.0 %collective-permute-start.1 = (bf16[2048,128]{1,0:T(8,128)(2,1)S(1)}, bf16[2048,128]{1,0:T(8,128)(2,1)}, u32[]{:S(2)}, u32[]{:S(2)}) collective-permute-start(bf16[2048,128]{1,0:T(8,128)(2,1)S(1)} %after.4.qp_ref.value_ref), channel_id=1, source_target_pairs={{0,2},{1,3},{2,0},{3,1},{4,6},{5,7},{6,4},{7,5},{8,10},{9,11},{10,... | collective-permute-start | bytes 1572872 | tf_op jit(solution)/shard_map/ppermute | solution.py:289
  9.3 0.9 %copies.1 = bf16[512,640]{1,0:T(8,128)(2,1)} custom-call(bf16[16,640]{1,0:T(8,128)(2,1)S(1)} %negative_rows.1.row_ref, bf16[16,640]{1,0:T(8,128)(2,1)S(1)} %collective-permute-done.other_ref.after_ref), custom_call_target="tpu_custom_call" | custom-call | tf_op jit(solution)/shard_map/copies/pallas_call | solution.py:344
  10.2 7.0 %all-to-all-start = ((bf16[16,32,640]{2,1,0:T(8,128)(2,1)}), bf16[16,32,640]{2,1,0:T(8,128)(2,1)S(1)}, u32[]{:S(2)}, u32[]{:S(2)}) async-start(bf16[16,32,640]{2,1,0:T(8,128)(2,1)} %bitcast.1), calls=%async_computation | async-start | bytes 1310720 | tf_op jit(solution)/shard_map/all_to_all | solution.py:352
  17.2 1.8 %pack_positive.1 = (bf16[128,2048]{1,0:T(8,128)(2,1)S(1)}, f32[1,2048]{1,0:T(1,128)S(1)}, f32[1,2048]{1,0:T(1,128)S(1)}) custom-call(s32[1,32]{1,0:T(1,128)S(1)} %copy-done.4, bf16[6144,128]{1,0:T(8,128)(2,1)S(1)} %copy-done, s32[48,128]{1,0:T(8,128)S(1)} %bitcast.10, bf16[2048,128]{1,0:T(8,128)(2,1)S(1)} %after.4.qp_ref.value_ref), custom_call_target="tpu_custom_call" | custom-call | tf_op jit(solution)/shard_map/pack_positive/pallas_call | solution.py:329
  19.1 1.5 %collective-permute-done.1.value_ref = bf16[2048,128]{1,0:T(8,128)(2,1)} collective-permute-done((bf16[2048,128]{1,0:T(8,128)(2,1)S(1)}, bf16[2048,128]{1,0:T(8,128)(2,1)}, u32[]{:S(2)}, u32[]{:S(2)}) %collective-permute-start.1) | collective-permute-done | bytes 524320 | tf_op jit(solution)/shard_map/ppermute | solution.py:289
  20.6 0.5 collective-permute-start.3
  21.1 1.3 %place_own.1.refs_2_ = bf16[2048,512]{1,0:T(8,128)(2,1)S(1)} custom-call(bf16[2048,128]{1,0:T(8,128)(2,1)S(1)} %after.6.refs_0_, bf16[2048,128]{1,0:T(8,128)(2,1)} %after.5.after_ref.refs_1_), custom_call_target="tpu_custom_call" | custom-call | tf_op jit(solution)/shard_map/place_own/pallas_call | solution.py:355
  22.4 0.8 %collective-permute-done.2.refs_0_ = bf16[2048,128]{1,0:T(8,128)(2,1)S(1)} collective-permute-done((bf16[2048,128]{1,0:T(8,128)(2,1)S(1)}, bf16[2048,128]{1,0:T(8,128)(2,1)S(1)}, u32[]{:S(2)}, u32[]{:S(2)}) %collective-permute-start.2) | collective-permute-done | bytes 524320 | tf_op jit(solution)/shard_map/ppermute | solution.py:289
  23.7 5.5 %all-to-all-done = bf16[16,32,640]{2,1,0:T(8,128)(2,1)S(1)} async-done(((bf16[16,32,640]{2,1,0:T(8,128)(2,1)}), bf16[16,32,640]{2,1,0:T(8,128)(2,1)S(1)}, u32[]{:S(2)}, u32[]{:S(2)}) %all-to-all-start) | async-done | bytes 655392 | tf_op jit(solution)/shard_map/all_to_all | solution.py:352
  29.1 2.0 %scores.1 = (f32[512,2048]{1,0:T(8,128)S(1)}, f32[4,2048]{1,0:T(4,128)S(1)}) custom-call(bf16[512,640]{1,0:T(8,128)(2,1)S(1)} %bitcast.6, bf16[2048,512]{1,0:T(8,128)(2,1)S(1)} %place_near.1.qfull_ref.q_ref, f32[1,2048]{1,0:T(1,128)S(1)} %get-tuple-element.17.idp_ref, f32[1,2048]{1,0:T(1,128)S(1)} %get-tuple-element.16.after_ref.part_ref), custom_call_target="tpu_custom_call" | custom-call | tf_op jit(solution)/shard_map/scores/pallas_call | solution.py:373
  31.6 3.0 %collective-permute-start.6 = (f32[4,2048]{1,0:T(4,128)S(1)}, f32[4,2048]{1,0:T(4,128)S(1)}, u32[]{:S(2)}, u32[]{:S(2)}) collective-permute-start(f32[4,2048]{1,0:T(4,128)S(1)} %get-tuple-element.18.s0), channel_id=1, source_target_pairs={{0,3},{1,2},{2,1},{3,0},{4,7},{5,6},{6,5},{7,4},{8,11},{9,10},{10,... | collective-permute-start | bytes 98312 | tf_op jit(solution)/shard_map/ppermute | solution.py:289
  34.6 1.3 %row_products.1 = (f32[256,2048]{1,0:T(8,128)S(1)}, bf16[256,2048]{1,0:T(8,128)(2,1)S(1)}) custom-call(bf16[512,640]{1,0:T(8,128)(2,1)S(1)} %bitcast.7, f32[512,2048]{1,0:T(8,128)S(1)} %get-tuple-element.19.e_ref), custom_call_target="tpu_custom_call" | custom-call | tf_op jit(solution)/shard_map/row_products/pallas_call | solution.py:384
  36.3 0.5 collective-permute-done.5.s2
  36.9 1.2 %item_products.1.after_ref = bf16[512,512]{1,0:T(8,128)(2,1)S(1)} custom-call(f32[1,2048]{1,0:T(1,128)S(1)} %get-tuple-element.21.scale_ref, f32[512,2048]{1,0:T(8,128)S(1)} %get-tuple-element.19.e_ref, bf16[2048,512]{1,0:T(8,128)(2,1)S(1)} %place_near.1.qfull_ref.q_ref), custom_call_target="tpu_custom_call" | custom-call | flops 49999998976 | tf_op jit(solution)/shard_map/item_products/pallas_call | solution.py:403
  38.2 0.5 collective-permute-done.7.recv_ref
  38.9 2.5 %collective-permute-start.8 = (bf16[128,2048]{1,0:T(8,128)(2,1)S(1)}, bf16[128,2048]{1,0:T(8,128)(2,1)S(1)}, u32[]{:S(2)}, u32[]{:S(2)}) collective-permute-start(bf16[128,2048]{1,0:T(8,128)(2,1)S(1)} %get-tuple-element.25), channel_id=1, source_target_pairs={{0,2},{1,3},{2,0},{3,1},{4,6},{5,7},{6,4},{7,5},{8,10},{9,11},{10,... | collective-permute-start | bytes 1572872 | tf_op jit(solution)/shard_map/ppermute | solution.py:289
  41.4 14.8 %all_to_all.22 = bf16[16,32,512]{2,1,0:T(8,128)(2,1)S(1)} all-to-all(bf16[16,32,512]{2,1,0:T(8,128)(2,1)S(1)} %bitcast.8), channel_id=1, replica_groups=mesh['x'=4,'zl'=2,'y'=4,'grp'=4] {'x','y'}, dimensions={0} | all-to-all | bytes 1048576 | tf_op jit(solution)/shard_map/all_to_all | solution.py:422
  56.3 0.6 collective-permute-start.9
  56.9 2.7 %unpack.1 = bf16[6144,128]{1,0:T(8,128)(2,1)} custom-call(s32[1,32]{1,0:T(1,128)S(1)} %copy-done.4, f32[128,2048]{1,0:T(8,128)S(1)} %get-tuple-element.24.own_ref, bf16[128,2048]{1,0:T(8,128)(2,1)S(1)} %collective-permute-done.8.recv_ref.after_ref, f32[1,2048]{1,0:T(1,128)S(1)} %get-tuple-element.26.term_ref, bf16[128,2048]{1,0:T(8,128)(2,1)S(1)} %copy-done.2), custom_call_target="tpu_custom_call" | custom-call | tf_op jit(solution)/shard_map/unpack/pallas_call | solution.py:442
  59.6 0.7 %collective-permute-done.9.recv_ref = f32[16,512]{1,0:T(8,128)S(1)} collective-permute-done((f32[16,512]{1,0:T(8,128)S(1)}, f32[16,512]{1,0:T(8,128)S(1)}, u32[]{:S(2)}, u32[]{:S(2)}) %collective-permute-start.9) | collective-permute-done | bytes 32800 | tf_op jit(solution)/shard_map/ppermute | solution.py:432
  60.3 0.6 %add_neighbour.1 = f32[16,512]{1,0:T(8,128)} custom-call(f32[16,512]{1,0:T(8,128)S(1)} %get-tuple-element.28.own_ref, f32[16,512]{1,0:T(8,128)S(1)} %collective-permute-done.9.recv_ref), custom_call_target="tpu_custom_call" | custom-call | tf_op jit(solution)/shard_map/add_neighbour/pallas_call | solution.py:433
  (27 shorter events, 1.9 us)
Async XLA Ops:
  1.4 15.8 %copy-start = (bf16[6144,128]{1,0:T(8,128)(2,1)S(1)}, bf16[6144,128]{1,0:T(8,128)(2,1)}, u32[]{:S(2)}) copy-start(bf16[6144,128]{1,0:T(8,128)(2,1)} %p_ref.1) | copy-start | bytes 4718596
  1.4 15.8 %copy-start.3 = (s32[6144]{0:T(1024)S(1)}, s32[6144]{0:T(1024)}, u32[]{:S(2)}) copy-start(s32[6144]{0:T(1024)} %param.8) | copy-start | bytes 73732
  1.4 15.8 %copy-start.4 = (s32[1,32]{1,0:T(1,128)S(1)}, s32[1,32]{1,0:T(1,128)}, u32[]{:S(2)}) copy-start(s32[1,32]{1,0:T(1,128)} %len_ref.5) | copy-start | bytes 388
  1.4 3.9 %collective-permute-start = (bf16[16,640]{1,0:T(8,128)(2,1)S(1)}, bf16[16,640]{1,0:T(8,128)(2,1)S(1)}, u32[]{:S(2)}, u32[]{:S(2)}) collective-permute-start(bf16[16,640]{1,0:T(8,128)(2,1)S(1)} %negative_rows.1.row_ref), channel_id=1, source_target_pairs={{0,16},{16,0},{1,17},{17,1},{2,18},{18,2},{3,19},{19,3},{4,20},{20... | collective-permute-start | bytes 61448 | tf_op jit(solution)/shard_map/ppermute | solution.py:312
  5.3 15.3 %collective-permute-start.1 = (bf16[2048,128]{1,0:T(8,128)(2,1)S(1)}, bf16[2048,128]{1,0:T(8,128)(2,1)}, u32[]{:S(2)}, u32[]{:S(2)}) collective-permute-start(bf16[2048,128]{1,0:T(8,128)(2,1)S(1)} %after.4.qp_ref.value_ref), channel_id=1, source_target_pairs={{0,2},{1,3},{2,0},{3,1},{4,6},{5,7},{6,4},{7,5},{8,10},{9,11},{10,... | collective-permute-start | bytes 1572872 | tf_op jit(solution)/shard_map/ppermute | solution.py:289
  10.2 19.0 %all-to-all-start = ((bf16[16,32,640]{2,1,0:T(8,128)(2,1)}), bf16[16,32,640]{2,1,0:T(8,128)(2,1)S(1)}, u32[]{:S(2)}, u32[]{:S(2)}) async-start(bf16[16,32,640]{2,1,0:T(8,128)(2,1)} %bitcast.1), calls=%async_computation | async-start | bytes 1310720 | tf_op jit(solution)/shard_map/all_to_all | solution.py:352
  19.1 3.3 %copy-start.1 = (bf16[128,2048]{1,0:T(8,128)(2,1)}, bf16[128,2048]{1,0:T(8,128)(2,1)S(1)}, u32[]{:S(2)}) copy-start(bf16[128,2048]{1,0:T(8,128)(2,1)S(1)} %get-tuple-element.27.pt_ref) | copy-start | bytes 1572868
  20.6 2.6 %collective-permute-start.2 = (bf16[2048,128]{1,0:T(8,128)(2,1)S(1)}, bf16[2048,128]{1,0:T(8,128)(2,1)S(1)}, u32[]{:S(2)}, u32[]{:S(2)}) collective-permute-start(bf16[2048,128]{1,0:T(8,128)(2,1)S(1)} %after.6.refs_0_), channel_id=1, source_target_pairs={{0,1},{1,0},{2,3},{3,2},{4,5},{5,4},{6,7},{7,6},{8,9},{9,8},{10,11... | collective-permute-start | bytes 1572872 | tf_op jit(solution)/shard_map/ppermute | solution.py:289
  20.6 2.9 %collective-permute-start.3 = (bf16[2048,128]{1,0:T(8,128)(2,1)}, bf16[2048,128]{1,0:T(8,128)(2,1)S(1)}, u32[]{:S(2)}, u32[]{:S(2)}) collective-permute-start(bf16[2048,128]{1,0:T(8,128)(2,1)} %after.5.after_ref.refs_1_), channel_id=1, source_target_pairs={{0,1},{1,0},{2,3},{3,2},{4,5},{5,4},{6,7},{7,6},{8,9},{9,8},{10,11... | collective-permute-start | bytes 1572872 | tf_op jit(solution)/shard_map/ppermute | solution.py:289
  31.1 5.2 %collective-permute-start.4 = (f32[4,2048]{1,0:T(4,128)S(1)}, f32[4,2048]{1,0:T(4,128)S(1)}, u32[]{:S(2)}, u32[]{:S(2)}) collective-permute-start(f32[4,2048]{1,0:T(4,128)S(1)} %get-tuple-element.18.s0), channel_id=1, source_target_pairs={{0,1},{1,0},{2,3},{3,2},{4,5},{5,4},{6,7},{7,6},{8,9},{9,8},{10,11... | collective-permute-start | bytes 98312 | tf_op jit(solution)/shard_map/ppermute | solution.py:289
  31.2 5.7 %collective-permute-start.5 = (f32[4,2048]{1,0:T(4,128)S(1)}, f32[4,2048]{1,0:T(4,128)S(1)}, u32[]{:S(2)}, u32[]{:S(2)}) collective-permute-start(f32[4,2048]{1,0:T(4,128)S(1)} %get-tuple-element.18.s0), channel_id=1, source_target_pairs={{0,2},{1,3},{2,0},{3,1},{4,6},{5,7},{6,4},{7,5},{8,10},{9,11},{10,... | collective-permute-start | bytes 98312 | tf_op jit(solution)/shard_map/ppermute | solution.py:289
  31.6 5.3 %collective-permute-start.6 = (f32[4,2048]{1,0:T(4,128)S(1)}, f32[4,2048]{1,0:T(4,128)S(1)}, u32[]{:S(2)}, u32[]{:S(2)}) collective-permute-start(f32[4,2048]{1,0:T(4,128)S(1)} %get-tuple-element.18.s0), channel_id=1, source_target_pairs={{0,3},{1,2},{2,1},{3,0},{4,7},{5,6},{6,5},{7,4},{8,11},{9,10},{10,... | collective-permute-start | bytes 98312 | tf_op jit(solution)/shard_map/ppermute | solution.py:289
  35.9 2.7 %collective-permute-start.7 = (bf16[256,2048]{1,0:T(8,128)(2,1)S(1)}, bf16[256,2048]{1,0:T(8,128)(2,1)S(1)}, u32[]{:S(2)}, u32[]{:S(2)}) collective-permute-start(bf16[256,2048]{1,0:T(8,128)(2,1)S(1)} %get-tuple-element.23), channel_id=1, source_target_pairs={{0,1},{1,0},{2,3},{3,2},{4,5},{5,4},{6,7},{7,6},{8,9},{9,8},{10,11... | collective-permute-start | bytes 3145736 | tf_op jit(solution)/shard_map/ppermute | solution.py:289
  38.6 18.3 %copy-start.2 = (bf16[128,2048]{1,0:T(8,128)(2,1)S(1)}, bf16[128,2048]{1,0:T(8,128)(2,1)}, u32[]{:S(2)}) copy-start(bf16[128,2048]{1,0:T(8,128)(2,1)} %copy-done.1) | copy-start | bytes 1572868
  38.9 17.3 %collective-permute-start.8 = (bf16[128,2048]{1,0:T(8,128)(2,1)S(1)}, bf16[128,2048]{1,0:T(8,128)(2,1)S(1)}, u32[]{:S(2)}, u32[]{:S(2)}) collective-permute-start(bf16[128,2048]{1,0:T(8,128)(2,1)S(1)} %get-tuple-element.25), channel_id=1, source_target_pairs={{0,2},{1,3},{2,0},{3,1},{4,6},{5,7},{6,4},{7,5},{8,10},{9,11},{10,... | collective-permute-start | bytes 1572872 | tf_op jit(solution)/shard_map/ppermute | solution.py:289
  56.3 4.0 %collective-permute-start.9 = (f32[16,512]{1,0:T(8,128)S(1)}, f32[16,512]{1,0:T(8,128)S(1)}, u32[]{:S(2)}, u32[]{:S(2)}) collective-permute-start(f32[16,512]{1,0:T(8,128)S(1)} %after.7), channel_id=1, source_target_pairs={{0,16},{16,0},{1,17},{17,1},{2,18},{18,2},{3,19},{19,3},{4,20},{20... | collective-permute-start | bytes 98312 | tf_op jit(solution)/shard_map/ppermute | solution.py:432

commit v5 on v4

--- a/solution.py
+++ b/solution.py
@@ -201,14 +201,20 @@
         send_ref[:, at] = out[half:, :].astype(BF16)
 
 
-def norm_kernel(s0, s1, s2, s3, after_ref, scale_ref, other_ref, term_ref):
-    refs = (s0, s1, s2, s3)
-    positive = s0[2:3, :] + s1[2:3, :] + s2[2:3, :] + s3[2:3, :]
-    top = positive
-    for ref in refs:
-        top = jnp.maximum(top, ref[0:1, :])
+def merge_kernel(own_ref, other_ref, out_ref):
+    top = jnp.maximum(own_ref[0:1, :], other_ref[0:1, :])
+    total = own_ref[1:2, :] * jnp.exp(own_ref[0:1, :] - top) + other_ref[1:2, :] * jnp.exp(other_ref[0:1, :] - top)
+    out_ref[0:1, :] = top
+    out_ref[1:2, :] = total
+    out_ref[2:3, :] = own_ref[2:3, :] + other_ref[2:3, :]
+    out_ref[3:4, :] = total
+
+
+def norm_kernel(s0, s1, near, far, after_ref, scale_ref, other_ref, term_ref):
+    positive = near[2:3, :] + far[2:3, :]
+    top = jnp.maximum(jnp.maximum(near[0:1, :], far[0:1, :]), positive)
     total = jnp.exp(positive - top)
-    for ref in refs:
+    for ref in (near, far):
         total = total + ref[1:2, :] * jnp.exp(ref[0:1, :] - top)
     log_total = top + jnp.log(total)
     scale_ref[...] = jnp.exp(s0[0:1, :] - log_total)
@@ -379,7 +385,16 @@
         compiler_params=params(),
         name="scores",
     )(pool, qfull, held(idp), held(part))
-    stats = [held(s) for s in (stat, swap(stat, 1, groups), swap(stat, 2, groups), swap(stat, 3, groups))]
+    stat, stat1 = held(stat), held(swap(stat, 1, groups))
+    near_stat = pl.pallas_call(
+        merge_kernel,
+        out_shape=vmem((4, live), F32),
+        in_specs=[whole()] * 2,
+        out_specs=whole(),
+        compiler_params=params(),
+        name="merge_stats",
+    )(stat, stat1)
+    stats = (stat, stat1, held(near_stat), held(swap(near_stat, 2, groups)))
 
     keep, send = pl.pallas_call(
         rows_kernel,

time: 61.3 us -> 60.3 us (0.984)
  starting transfers between devices: 20.5 us -> 15.6 us
  waiting for transfers between devices: 9.91 us -> 13.8 us
    ppermute x8 -> x7, starting transfers between devices: 10.8 us -> 5.95 us  [swap(): return lax.ppermute(value, 'grp', [(g, g ^ step) for g in range(groups)])]
    ppermute x8 -> x7, waiting for transfers between devices: 3.62 us -> 7.55 us  [swap(): return lax.ppermute(value, 'grp', [(g, g ^ step) for g in range(groups)])]
  transfers between devices with their start and end apart: 11 -> 10, of which waited for: 8 -> 8; matrix products, arithmetic and copies ran while one was open for 0% -> 0% of each run, Pallas kernels for 18% -> 19%
where the time goes in v5:
time: 60.3 us; the launch traced here: 60 us
  starting transfers between devices  15.6 us (26%)
  Pallas kernels  14.9 us (25%)
  blocking collectives  14.8 us (25%)
  waiting for transfers between devices  13.8 us (23%)
  between operations  0.82 us (1%)
    all_to_all x1, blocking collectives, shards(): lax.all_to_all(items, ('x', 'y'), split_axis=0, concat_axis=0, tiled=True)  14.8 us
    ppermute x7, waiting for transfers between devices, swap(): return lax.ppermute(value, 'grp', [(g, g ^ step) for g in range(groups)])  7.55 us
    all_to_all x1, starting transfers between devices, shards(): lax.all_to_all(copies, ('x', 'y'), split_axis=0, concat_axis=0, tiled=True)  7.03 us
    ppermute x7, starting transfers between devices, swap(): return lax.ppermute(value, 'grp', [(g, g ^ step) for g in range(groups)])  5.95 us
    all_to_all x1, waiting for transfers between devices, shards(): lax.all_to_all(copies, ('x', 'y'), split_axis=0, concat_axis=0, tiled=True)  5.44 us
    pallas_call x1, Pallas kernels, shards(): pl.pallas_call(unpack_kernel, out_shape=jax.ShapeDtypeStruct((slots, LANE...  2.69 us
    ppermute x1, starting transfers between devices, shards(): other = lax.ppermute(row, 'zl', [(i, near - 1 - i) for i in range(near)])  2.08 us
    pallas_call x1, Pallas kernels, shards(): pl.pallas_call(scores_kernel, out_shape=(vmem((negs, live), F32), vmem((4...  1.96 us
  transfers between devices with their start and end apart: 10, of which 8 were waited for; matrix products, arithmetic and copies ran while one was open for 0% of the time, Pallas kernels for 19%

profile of v5, /device:TPU:0, one launch (start us, length us, event | category | flops | bytes accessed | tf_op | source)
XLA Modules:
  0.0 60.0 jit_solution(12500275055344218909)
XLA Ops:
  0.6 0.8 %negative_rows.1.row_ref = bf16[16,640]{1,0:T(8,128)(2,1)S(1)} custom-call(bf16[16,512]{1,0:T(8,128)(2,1)} %neg_ref.1, s32[1,16]{1,0:T(1,128)} %bitcast.11), custom_call_target="tpu_custom_call" | custom-call | tf_op jit(solution)/shard_map/negative_rows/pallas_call | solution.py:308
  1.4 2.1 %collective-permute-start = (bf16[16,640]{1,0:T(8,128)(2,1)S(1)}, bf16[16,640]{1,0:T(8,128)(2,1)S(1)}, u32[]{:S(2)}, u32[]{:S(2)}) collective-permute-start(bf16[16,640]{1,0:T(8,128)(2,1)S(1)} %negative_rows.1.row_ref), channel_id=1, source_target_pairs={{0,16},{16,0},{1,17},{17,1},{2,18},{18,2},{3,19},{19,3},{4,20},{20... | collective-permute-start | bytes 61448 | tf_op jit(solution)/shard_map/ppermute | solution.py:318
  3.5 1.7 %pack_query.1.value_ref = bf16[2048,128]{1,0:T(8,128)(2,1)S(1)} custom-call(s32[1,32]{1,0:T(1,128)} %len_ref.5, bf16[6144,128]{1,0:T(8,128)(2,1)} %q_ref.1), custom_call_target="tpu_custom_call" | custom-call | tf_op jit(solution)/shard_map/pack_query/pallas_call | solution.py:319
  5.3 4.0 %collective-permute-start.1 = (bf16[2048,128]{1,0:T(8,128)(2,1)S(1)}, bf16[2048,128]{1,0:T(8,128)(2,1)}, u32[]{:S(2)}, u32[]{:S(2)}) collective-permute-start(bf16[2048,128]{1,0:T(8,128)(2,1)S(1)} %after.4.qp_ref.value_ref), channel_id=1, source_target_pairs={{0,2},{1,3},{2,0},{3,1},{4,6},{5,7},{6,4},{7,5},{8,10},{9,11},{10,... | collective-permute-start | bytes 1572872 | tf_op jit(solution)/shard_map/ppermute | solution.py:295
  9.3 0.9 %copies.1 = bf16[512,640]{1,0:T(8,128)(2,1)} custom-call(bf16[16,640]{1,0:T(8,128)(2,1)S(1)} %negative_rows.1.row_ref, bf16[16,640]{1,0:T(8,128)(2,1)S(1)} %collective-permute-done.other_ref.after_ref), custom_call_target="tpu_custom_call" | custom-call | tf_op jit(solution)/shard_map/copies/pallas_call | solution.py:350
  10.2 7.0 %all-to-all-start = ((bf16[16,32,640]{2,1,0:T(8,128)(2,1)}), bf16[16,32,640]{2,1,0:T(8,128)(2,1)S(1)}, u32[]{:S(2)}, u32[]{:S(2)}) async-start(bf16[16,32,640]{2,1,0:T(8,128)(2,1)} %bitcast.1), calls=%async_computation | async-start | bytes 1310720 | tf_op jit(solution)/shard_map/all_to_all | solution.py:358
  17.2 1.8 %pack_positive.1 = (bf16[128,2048]{1,0:T(8,128)(2,1)S(1)}, f32[1,2048]{1,0:T(1,128)S(1)}, f32[1,2048]{1,0:T(1,128)S(1)}) custom-call(s32[1,32]{1,0:T(1,128)S(1)} %copy-done.4, bf16[6144,128]{1,0:T(8,128)(2,1)S(1)} %copy-done, s32[48,128]{1,0:T(8,128)S(1)} %bitcast.10, bf16[2048,128]{1,0:T(8,128)(2,1)S(1)} %after.4.qp_ref.value_ref), custom_call_target="tpu_custom_call" | custom-call | tf_op jit(solution)/shard_map/pack_positive/pallas_call | solution.py:335
  19.1 1.6 %collective-permute-done.1.value_ref = bf16[2048,128]{1,0:T(8,128)(2,1)} collective-permute-done((bf16[2048,128]{1,0:T(8,128)(2,1)S(1)}, bf16[2048,128]{1,0:T(8,128)(2,1)}, u32[]{:S(2)}, u32[]{:S(2)}) %collective-permute-start.1) | collective-permute-done | bytes 524320 | tf_op jit(solution)/shard_map/ppermute | solution.py:295
  20.6 0.5 collective-permute-start.3
  21.2 1.3 %place_own.1.refs_2_ = bf16[2048,512]{1,0:T(8,128)(2,1)S(1)} custom-call(bf16[2048,128]{1,0:T(8,128)(2,1)S(1)} %after.6.refs_0_, bf16[2048,128]{1,0:T(8,128)(2,1)} %after.5.after_ref.refs_1_), custom_call_target="tpu_custom_call" | custom-call | tf_op jit(solution)/shard_map/place_own/pallas_call | solution.py:361
  22.4 0.8 %collective-permute-done.2.refs_0_ = bf16[2048,128]{1,0:T(8,128)(2,1)S(1)} collective-permute-done((bf16[2048,128]{1,0:T(8,128)(2,1)S(1)}, bf16[2048,128]{1,0:T(8,128)(2,1)S(1)}, u32[]{:S(2)}, u32[]{:S(2)}) %collective-permute-start.2) | collective-permute-done | bytes 524320 | tf_op jit(solution)/shard_map/ppermute | solution.py:295
  23.7 5.4 %all-to-all-done = bf16[16,32,640]{2,1,0:T(8,128)(2,1)S(1)} async-done(((bf16[16,32,640]{2,1,0:T(8,128)(2,1)}), bf16[16,32,640]{2,1,0:T(8,128)(2,1)S(1)}, u32[]{:S(2)}, u32[]{:S(2)}) %all-to-all-start) | async-done | bytes 655392 | tf_op jit(solution)/shard_map/all_to_all | solution.py:358
  29.1 2.0 %scores.1 = (f32[512,2048]{1,0:T(8,128)S(1)}, f32[4,2048]{1,0:T(4,128)S(1)}) custom-call(bf16[512,640]{1,0:T(8,128)(2,1)S(1)} %bitcast.6, bf16[2048,512]{1,0:T(8,128)(2,1)S(1)} %place_near.1.qfull_ref.q_ref, f32[1,2048]{1,0:T(1,128)S(1)} %get-tuple-element.17.idp_ref, f32[1,2048]{1,0:T(1,128)S(1)} %get-tuple-element.16.after_ref.part_ref), custom_call_target="tpu_custom_call" | custom-call | tf_op jit(solution)/shard_map/scores/pallas_call | solution.py:379
  31.2 1.2 %collective-permute-done.4.other_ref.s1 = f32[4,2048]{1,0:T(4,128)S(1)} collective-permute-done((f32[4,2048]{1,0:T(4,128)S(1)}, f32[4,2048]{1,0:T(4,128)S(1)}, u32[]{:S(2)}, u32[]{:S(2)}) %collective-permute-start.4) | collective-permute-done | bytes 32800 | tf_op jit(solution)/shard_map/ppermute | solution.py:295
  32.4 0.4 collective-permute-start.5
  32.8 1.3 %row_products.1 = (f32[256,2048]{1,0:T(8,128)S(1)}, bf16[256,2048]{1,0:T(8,128)(2,1)S(1)}) custom-call(bf16[512,640]{1,0:T(8,128)(2,1)S(1)} %bitcast.7, f32[512,2048]{1,0:T(8,128)S(1)} %get-tuple-element.19.e_ref), custom_call_target="tpu_custom_call" | custom-call | tf_op jit(solution)/shard_map/row_products/pallas_call | solution.py:399
  34.2 3.7 %collective-permute-done.5.far = f32[4,2048]{1,0:T(4,128)S(1)} collective-permute-done((f32[4,2048]{1,0:T(4,128)S(1)}, f32[4,2048]{1,0:T(4,128)S(1)}, u32[]{:S(2)}, u32[]{:S(2)}) %collective-permute-start.5) | collective-permute-done | bytes 32800 | tf_op jit(solution)/shard_map/ppermute | solution.py:295
  37.9 1.2 %item_products.1.after_ref = bf16[512,512]{1,0:T(8,128)(2,1)S(1)} custom-call(f32[1,2048]{1,0:T(1,128)S(1)} %get-tuple-element.21.scale_ref, f32[512,2048]{1,0:T(8,128)S(1)} %get-tuple-element.19.e_ref, bf16[2048,512]{1,0:T(8,128)(2,1)S(1)} %place_near.1.qfull_ref.q_ref), custom_call_target="tpu_custom_call" | custom-call | flops 49999998976 | tf_op jit(solution)/shard_map/item_products/pallas_call | solution.py:418
  39.5 0.9 %collective-permute-start.7 = (bf16[128,2048]{1,0:T(8,128)(2,1)S(1)}, bf16[128,2048]{1,0:T(8,128)(2,1)S(1)}, u32[]{:S(2)}, u32[]{:S(2)}) collective-permute-start(bf16[128,2048]{1,0:T(8,128)(2,1)S(1)} %get-tuple-element.25), channel_id=1, source_target_pairs={{0,2},{1,3},{2,0},{3,1},{4,6},{5,7},{6,4},{7,5},{8,10},{9,11},{10,... | collective-permute-start | bytes 1572872 | tf_op jit(solution)/shard_map/ppermute | solution.py:295
  40.5 14.8 %all_to_all.22 = bf16[16,32,512]{2,1,0:T(8,128)(2,1)S(1)} all-to-all(bf16[16,32,512]{2,1,0:T(8,128)(2,1)S(1)} %bitcast.8), channel_id=1, replica_groups=mesh['x'=4,'zl'=2,'y'=4,'grp'=4] {'x','y'}, dimensions={0} | all-to-all | bytes 1048576 | tf_op jit(solution)/shard_map/all_to_all | solution.py:437
  55.4 0.6 collective-permute-start.8
  55.9 2.7 %unpack.1 = bf16[6144,128]{1,0:T(8,128)(2,1)} custom-call(s32[1,32]{1,0:T(1,128)S(1)} %copy-done.4, f32[128,2048]{1,0:T(8,128)S(1)} %get-tuple-element.24.own_ref, bf16[128,2048]{1,0:T(8,128)(2,1)S(1)} %collective-permute-done.7.recv_ref.after_ref, f32[1,2048]{1,0:T(1,128)S(1)} %get-tuple-element.26.term_ref, bf16[128,2048]{1,0:T(8,128)(2,1)S(1)} %copy-done.2), custom_call_target="tpu_custom_call" | custom-call | tf_op jit(solution)/shard_map/unpack/pallas_call | solution.py:457
  58.7 0.7 %collective-permute-done.8.recv_ref = f32[16,512]{1,0:T(8,128)S(1)} collective-permute-done((f32[16,512]{1,0:T(8,128)S(1)}, f32[16,512]{1,0:T(8,128)S(1)}, u32[]{:S(2)}, u32[]{:S(2)}) %collective-permute-start.8) | collective-permute-done | bytes 32800 | tf_op jit(solution)/shard_map/ppermute | solution.py:447
  59.4 0.6 %add_neighbour.1 = f32[16,512]{1,0:T(8,128)} custom-call(f32[16,512]{1,0:T(8,128)S(1)} %get-tuple-element.28.own_ref, f32[16,512]{1,0:T(8,128)S(1)} %collective-permute-done.8.recv_ref), custom_call_target="tpu_custom_call" | custom-call | tf_op jit(solution)/shard_map/add_neighbour/pallas_call | solution.py:448
  (26 shorter events, 1.2 us)
Async XLA Ops:
  1.4 15.8 %copy-start = (bf16[6144,128]{1,0:T(8,128)(2,1)S(1)}, bf16[6144,128]{1,0:T(8,128)(2,1)}, u32[]{:S(2)}) copy-start(bf16[6144,128]{1,0:T(8,128)(2,1)} %p_ref.1) | copy-start | bytes 4718596
  1.4 15.8 %copy-start.3 = (s32[6144]{0:T(1024)S(1)}, s32[6144]{0:T(1024)}, u32[]{:S(2)}) copy-start(s32[6144]{0:T(1024)} %param.8) | copy-start | bytes 73732
  1.4 15.8 %copy-start.4 = (s32[1,32]{1,0:T(1,128)S(1)}, s32[1,32]{1,0:T(1,128)}, u32[]{:S(2)}) copy-start(s32[1,32]{1,0:T(1,128)} %len_ref.5) | copy-start | bytes 388
  1.4 3.9 %collective-permute-start = (bf16[16,640]{1,0:T(8,128)(2,1)S(1)}, bf16[16,640]{1,0:T(8,128)(2,1)S(1)}, u32[]{:S(2)}, u32[]{:S(2)}) collective-permute-start(bf16[16,640]{1,0:T(8,128)(2,1)S(1)} %negative_rows.1.row_ref), channel_id=1, source_target_pairs={{0,16},{16,0},{1,17},{17,1},{2,18},{18,2},{3,19},{19,3},{4,20},{20... | collective-permute-start | bytes 61448 | tf_op jit(solution)/shard_map/ppermute | solution.py:318
  5.3 15.3 %collective-permute-start.1 = (bf16[2048,128]{1,0:T(8,128)(2,1)S(1)}, bf16[2048,128]{1,0:T(8,128)(2,1)}, u32[]{:S(2)}, u32[]{:S(2)}) collective-permute-start(bf16[2048,128]{1,0:T(8,128)(2,1)S(1)} %after.4.qp_ref.value_ref), channel_id=1, source_target_pairs={{0,2},{1,3},{2,0},{3,1},{4,6},{5,7},{6,4},{7,5},{8,10},{9,11},{10,... | collective-permute-start | bytes 1572872 | tf_op jit(solution)/shard_map/ppermute | solution.py:295
  10.2 19.0 %all-to-all-start = ((bf16[16,32,640]{2,1,0:T(8,128)(2,1)}), bf16[16,32,640]{2,1,0:T(8,128)(2,1)S(1)}, u32[]{:S(2)}, u32[]{:S(2)}) async-start(bf16[16,32,640]{2,1,0:T(8,128)(2,1)} %bitcast.1), calls=%async_computation | async-start | bytes 1310720 | tf_op jit(solution)/shard_map/all_to_all | solution.py:358
  19.1 3.4 %copy-start.1 = (bf16[128,2048]{1,0:T(8,128)(2,1)}, bf16[128,2048]{1,0:T(8,128)(2,1)S(1)}, u32[]{:S(2)}) copy-start(bf16[128,2048]{1,0:T(8,128)(2,1)S(1)} %get-tuple-element.27.pt_ref) | copy-start | bytes 1572868
  20.6 2.6 %collective-permute-start.2 = (bf16[2048,128]{1,0:T(8,128)(2,1)S(1)}, bf16[2048,128]{1,0:T(8,128)(2,1)S(1)}, u32[]{:S(2)}, u32[]{:S(2)}) collective-permute-start(bf16[2048,128]{1,0:T(8,128)(2,1)S(1)} %after.6.refs_0_), channel_id=1, source_target_pairs={{0,1},{1,0},{2,3},{3,2},{4,5},{5,4},{6,7},{7,6},{8,9},{9,8},{10,11... | collective-permute-start | bytes 1572872 | tf_op jit(solution)/shard_map/ppermute | solution.py:295
  20.6 2.9 %collective-permute-start.3 = (bf16[2048,128]{1,0:T(8,128)(2,1)}, bf16[2048,128]{1,0:T(8,128)(2,1)S(1)}, u32[]{:S(2)}, u32[]{:S(2)}) collective-permute-start(bf16[2048,128]{1,0:T(8,128)(2,1)} %after.5.after_ref.refs_1_), channel_id=1, source_target_pairs={{0,1},{1,0},{2,3},{3,2},{4,5},{5,4},{6,7},{7,6},{8,9},{9,8},{10,11... | collective-permute-start | bytes 1572872 | tf_op jit(solution)/shard_map/ppermute | solution.py:295
  31.1 1.3 %collective-permute-start.4 = (f32[4,2048]{1,0:T(4,128)S(1)}, f32[4,2048]{1,0:T(4,128)S(1)}, u32[]{:S(2)}, u32[]{:S(2)}) collective-permute-start(f32[4,2048]{1,0:T(4,128)S(1)} %get-tuple-element.18.own_ref.s0), channel_id=1, source_target_pairs={{0,1},{1,0},{2,3},{3,2},{4,5},{5,4},{6,7},{7,6},{8,9},{9,8},{10,11... | collective-permute-start | bytes 98312 | tf_op jit(solution)/shard_map/ppermute | solution.py:295
  32.4 5.5 %collective-permute-start.5 = (f32[4,2048]{1,0:T(4,128)S(1)}, f32[4,2048]{1,0:T(4,128)S(1)}, u32[]{:S(2)}, u32[]{:S(2)}) collective-permute-start(f32[4,2048]{1,0:T(4,128)S(1)} %merge_stats.1.near), channel_id=1, source_target_pairs={{0,2},{1,3},{2,0},{3,1},{4,6},{5,7},{6,4},{7,5},{8,10},{9,11},{10,... | collective-permute-start | bytes 98312 | tf_op jit(solution)/shard_map/ppermute | solution.py:295
  34.1 5.1 %collective-permute-start.6 = (bf16[256,2048]{1,0:T(8,128)(2,1)S(1)}, bf16[256,2048]{1,0:T(8,128)(2,1)S(1)}, u32[]{:S(2)}, u32[]{:S(2)}) collective-permute-start(bf16[256,2048]{1,0:T(8,128)(2,1)S(1)} %get-tuple-element.23), channel_id=1, source_target_pairs={{0,1},{1,0},{2,3},{3,2},{4,5},{5,4},{6,7},{7,6},{8,9},{9,8},{10,11... | collective-permute-start | bytes 3145736 | tf_op jit(solution)/shard_map/ppermute | solution.py:295
  39.2 16.7 %copy-start.2 = (bf16[128,2048]{1,0:T(8,128)(2,1)S(1)}, bf16[128,2048]{1,0:T(8,128)(2,1)}, u32[]{:S(2)}) copy-start(bf16[128,2048]{1,0:T(8,128)(2,1)} %copy-done.1) | copy-start | bytes 1572868
  39.5 15.8 %collective-permute-start.7 = (bf16[128,2048]{1,0:T(8,128)(2,1)S(1)}, bf16[128,2048]{1,0:T(8,128)(2,1)S(1)}, u32[]{:S(2)}, u32[]{:S(2)}) collective-permute-start(bf16[128,2048]{1,0:T(8,128)(2,1)S(1)} %get-tuple-element.25), channel_id=1, source_target_pairs={{0,2},{1,3},{2,0},{3,1},{4,6},{5,7},{6,4},{7,5},{8,10},{9,11},{10,... | collective-permute-start | bytes 1572872 | tf_op jit(solution)/shard_map/ppermute | solution.py:295
  55.4 4.0 %collective-permute-start.8 = (f32[16,512]{1,0:T(8,128)S(1)}, f32[16,512]{1,0:T(8,128)S(1)}, u32[]{:S(2)}, u32[]{:S(2)}) collective-permute-start(f32[16,512]{1,0:T(8,128)S(1)} %after.7), channel_id=1, source_target_pairs={{0,16},{16,0},{1,17},{17,1},{2,18},{18,2},{3,19},{19,3},{4,20},{20... | collective-permute-start | bytes 98312 | tf_op jit(solution)/shard_map/ppermute | solution.py:447

commit v6 on v5

--- a/solution.py
+++ b/solution.py
@@ -23,10 +23,6 @@
 
 def params():
     return pltpu.CompilerParams(vmem_limit_bytes=VMEM_BYTES)
-
-
-def weight(micros):
-    return pl.CostEstimate(flops=int(micros * 1e9), transcendentals=0, bytes_accessed=0)
 
 
 def whole():
@@ -201,28 +197,32 @@
         send_ref[:, at] = out[half:, :].astype(BF16)
 
 
-def merge_kernel(own_ref, other_ref, out_ref):
+def merge_kernel(own_ref, other_ref, out_ref, own_scale, other_scale):
     top = jnp.maximum(own_ref[0:1, :], other_ref[0:1, :])
-    total = own_ref[1:2, :] * jnp.exp(own_ref[0:1, :] - top) + other_ref[1:2, :] * jnp.exp(other_ref[0:1, :] - top)
+    mine, other = jnp.exp(own_ref[0:1, :] - top), jnp.exp(other_ref[0:1, :] - top)
+    total = own_ref[1:2, :] * mine + other_ref[1:2, :] * other
     out_ref[0:1, :] = top
     out_ref[1:2, :] = total
     out_ref[2:3, :] = own_ref[2:3, :] + other_ref[2:3, :]
     out_ref[3:4, :] = total
-
-
-def norm_kernel(s0, s1, near, far, after_ref, scale_ref, other_ref, term_ref):
+    own_scale[...] = mine
+    other_scale[...] = other
+
+
+def norm_kernel(own, near, far, after_ref, own_scale, near_scale, far_scale, term_ref):
     positive = near[2:3, :] + far[2:3, :]
     top = jnp.maximum(jnp.maximum(near[0:1, :], far[0:1, :]), positive)
     total = jnp.exp(positive - top)
     for ref in (near, far):
         total = total + ref[1:2, :] * jnp.exp(ref[0:1, :] - top)
     log_total = top + jnp.log(total)
-    scale_ref[...] = jnp.exp(s0[0:1, :] - log_total)
-    other_ref[...] = jnp.exp(s1[0:1, :] - log_total)
+    own_scale[...] = jnp.exp(own[0:1, :] - log_total)
+    near_scale[...] = jnp.exp(near[0:1, :] - log_total)
+    far_scale[...] = jnp.exp(far[0:1, :] - log_total)
     term_ref[...] = jnp.exp(positive - log_total) - 1.0
 
 
-def combine_kernel(scale_ref, other_ref, keep_ref, recv_ref, after_ref, own_ref, send_ref):
+def combine_kernel(scale_ref, other_ref, keep_ref, recv_ref, own_ref, send_ref):
     mine, other = scale_ref[...], other_ref[...]
     send_ref[...] = (keep_ref[LANES:, :] * mine + recv_ref[LANES:, :].astype(F32) * other).astype(BF16)
     own_ref[...] = keep_ref[:LANES, :] * mine + recv_ref[:LANES, :].astype(F32) * other
@@ -238,11 +238,12 @@
     out_ref[...] = total.astype(BF16)
 
 
-def unpack_kernel(len_ref, own_ref, recv_ref, term_ref, pt_ref, out_ref, packed, staged, sems):
+def unpack_kernel(len_ref, own_ref, recv_ref, near, far, term_ref, pt_ref, out_ref, packed, staged, sems):
     rows = own_ref.shape[1]
     for k in range(rows // LANES):
         at = slice(k * LANES, (k + 1) * LANES)
-        packed[at, :] = (own_ref[:, at] + recv_ref[:, at].astype(F32) + term_ref[:, at] * pt_ref[:, at].astype(F32)).T
+        negatives = own_ref[:, at] * near[:, at] + recv_ref[:, at].astype(F32) * far[:, at]
+        packed[at, :] = (negatives + term_ref[:, at] * pt_ref[:, at].astype(F32)).T
     index = lax.broadcasted_iota(jnp.int32, (CHUNK, LANES), 0)
     start = jnp.int32(0)
     parts = sems.shape[0]
@@ -298,7 +299,7 @@
 def shards(live, query, pos_emb, pos_ids, lengths, negatives, neg_ids):
     groups = lax.axis_size("grp")
     seqs = lax.axis_size(SEQ)
-    near = lax.axis_size("zl")
+    pair = lax.axis_size("zl")
     own_neg, width = negatives.shape
     slots = query.shape[0]
     negs = own_neg * seqs
@@ -315,7 +316,7 @@
         name="negative_rows",
     )(in_hbm(negatives), in_hbm(neg_ids.reshape(1, own_neg)))
 
-    other = lax.ppermute(row, "zl", [(i, near - 1 - i) for i in range(near)])
+    other = lax.ppermute(row, "zl", [(i, pair - 1 - i) for i in range(pair)])
     qp = pl.pallas_call(
         pack_query,
         out_shape=vmem((live, LANES), BF16),
@@ -386,15 +387,15 @@
         name="scores",
     )(pool, qfull, held(idp), held(part))
     stat, stat1 = held(stat), held(swap(stat, 1, groups))
-    near_stat = pl.pallas_call(
+    near, own_part, other_part = pl.pallas_call(
         merge_kernel,
-        out_shape=vmem((4, live), F32),
+        out_shape=(vmem((4, live), F32), vmem((1, live), F32), vmem((1, live), F32)),
         in_specs=[whole()] * 2,
-        out_specs=whole(),
+        out_specs=(whole(),) * 3,
         compiler_params=params(),
         name="merge_stats",
     )(stat, stat1)
-    stats = (stat, stat1, held(near_stat), held(swap(near_stat, 2, groups)))
+    far = swap(near, 2, groups)
 
     keep, send = pl.pallas_call(
         rows_kernel,
@@ -405,35 +406,33 @@
         compiler_params=params(),
         name="row_products",
     )(pool, held(e))
-    recv = swap(send, 1, groups)
-
-    scale, other_scale, term = pl.pallas_call(
+    recv = swap(after(send, stat1), 1, groups)
+    own, onward = pl.pallas_call(
+        combine_kernel,
+        out_shape=(vmem((LANES, live), F32), vmem((LANES, live), BF16)),
+        in_specs=[whole()] * 4,
+        out_specs=(whole(), whole()),
+        compiler_params=params(),
+        name="combine",
+    )(held(own_part), held(other_part), held(keep), held(recv))
+    recv2 = swap(onward, 2, groups)
+
+    own_scale, near_scale, far_scale, term = pl.pallas_call(
         norm_kernel,
-        out_shape=(vmem((1, live), F32),) * 3,
-        in_specs=[whole()] * 4 + [anywhere()],
-        out_specs=(whole(),) * 3,
+        out_shape=(vmem((1, live), F32),) * 4,
+        in_specs=[whole()] * 3 + [anywhere()],
+        out_specs=(whole(),) * 4,
         compiler_params=params(),
         name="norm",
-    )(*stats, keep)
+    )(stat, held(near), held(far), onward)
     items = pl.pallas_call(
         items_kernel,
         out_shape=vmem((negs, width), BF16),
         in_specs=[whole()] * 3,
         out_specs=whole(),
-        cost_estimate=weight(50),
         compiler_params=params(),
         name="item_products",
-    )(held(scale), held(e), qfull)
-    own, onward = pl.pallas_call(
-        combine_kernel,
-        out_shape=(vmem((LANES, live), F32), vmem((LANES, live), BF16)),
-        in_specs=[whole()] * 4 + [anywhere()],
-        out_specs=(whole(), whole()),
-        compiler_params=params(),
-        name="combine",
-    )(held(scale), held(other_scale), held(keep), held(recv), items)
-    recv2 = swap(onward, 2, groups)
-
+    )(held(own_scale), held(e), qfull)
     shares = lax.all_to_all(items, ("x", "y"), split_axis=0, concat_axis=0, tiled=True)
     own_sum, other_sum = pl.pallas_call(
         sum_kernel,
@@ -444,7 +443,7 @@
         name="sum_shares",
     )(held(shares))
     other_sum = after(other_sum, recv2)
-    recv_sum = lax.ppermute(other_sum, "zl", [(i, near - 1 - i) for i in range(near)])
+    recv_sum = lax.ppermute(other_sum, "zl", [(i, pair - 1 - i) for i in range(pair)])
     grad_items = pl.pallas_call(
         add_kernel,
         out_shape=jax.ShapeDtypeStruct((own_neg, width), F32),
@@ -457,7 +456,7 @@
     grad_query = pl.pallas_call(
         unpack_kernel,
         out_shape=jax.ShapeDtypeStruct((slots, LANES), BF16),
-        in_specs=[small()] + [whole()] * 4,
+        in_specs=[small()] + [whole()] * 6,
         out_specs=anywhere(),
         scratch_shapes=[
             vmem((live + MAXLEN, LANES), F32),
@@ -466,7 +465,7 @@
         ],
         compiler_params=params(),
         name="unpack",
-    )(lengths, held(own), held(recv2), held(term), held(pt))
+    )(lengths, *[held(v) for v in (own, recv2, near_scale, far_scale, term, pt)])
     return grad_query, grad_items
 
 

time: 60.3 us -> 59 us (0.978)
  waiting for transfers between devices: 13.8 us -> 12.3 us
  starting transfers between devices: 15.6 us -> 16.6 us
  blocking collectives: 14.8 us -> 14 us
    ppermute x7, waiting for transfers between devices: 7.55 us -> 6.04 us  [swap(): return lax.ppermute(value, 'grp', [(g, g ^ step) for g in range(groups)])]
    ppermute x7, starting transfers between devices: 5.95 us -> 6.94 us  [swap(): return lax.ppermute(value, 'grp', [(g, g ^ step) for g in range(groups)])]
    all_to_all x1, blocking collectives: 14.8 us -> 14 us  [shards(): lax.all_to_all(items, ('x', 'y'), split_axis=0, concat_axis=0, tiled=True)]
  transfers between devices with their start and end apart: 10 -> 10, of which waited for: 8 -> 8; matrix products, arithmetic and copies ran while one was open for 0% -> 0% of each run, Pallas kernels for 19% -> 20%
where the time goes in v6:
time: 59 us; the launch traced here: 58.6 us
  starting transfers between devices  16.6 us (28%)
  Pallas kernels  14.9 us (25%)
  blocking collectives  14 us (24%)
  waiting for transfers between devices  12.3 us (21%)
  between operations  0.82 us (1%)
    all_to_all x1, blocking collectives, shards(): lax.all_to_all(items, ('x', 'y'), split_axis=0, concat_axis=0, tiled=True)  14 us
    all_to_all x1, starting transfers between devices, shards(): lax.all_to_all(copies, ('x', 'y'), split_axis=0, concat_axis=0, tiled=True)  7.03 us
    ppermute x7, starting transfers between devices, swap(): return lax.ppermute(value, 'grp', [(g, g ^ step) for g in range(groups)])  6.94 us
    ppermute x7, waiting for transfers between devices, swap(): return lax.ppermute(value, 'grp', [(g, g ^ step) for g in range(groups)])  6.04 us
    all_to_all x1, waiting for transfers between devices, shards(): lax.all_to_all(copies, ('x', 'y'), split_axis=0, concat_axis=0, tiled=True)  5.45 us
    pallas_call x1, Pallas kernels, shards(): pl.pallas_call(unpack_kernel, out_shape=jax.ShapeDtypeStruct((slots, LANE...  2.71 us
    ppermute x1, starting transfers between devices, shards(): other = lax.ppermute(row, 'zl', [(i, pair - 1 - i) for i in range(pair)])  2.08 us
    pallas_call x1, Pallas kernels, shards(): pl.pallas_call(scores_kernel, out_shape=(vmem((negs, live), F32), vmem((4...  1.95 us
  transfers between devices with their start and end apart: 10, of which 8 were waited for; matrix products, arithmetic and copies ran while one was open for 0% of the time, Pallas kernels for 20%

profile of v6, /device:TPU:0, one launch (start us, length us, event | category | flops | bytes accessed | tf_op | source)
XLA Modules:
  0.0 58.6 jit_solution(4979770906676124394)
XLA Ops:
  0.6 0.8 %negative_rows.1.row_ref = bf16[16,640]{1,0:T(8,128)(2,1)S(1)} custom-call(bf16[16,512]{1,0:T(8,128)(2,1)} %neg_ref.1, s32[1,16]{1,0:T(1,128)} %bitcast.11), custom_call_target="tpu_custom_call" | custom-call | tf_op jit(solution)/shard_map/negative_rows/pallas_call | solution.py:309
  1.4 2.1 %collective-permute-start = (bf16[16,640]{1,0:T(8,128)(2,1)S(1)}, bf16[16,640]{1,0:T(8,128)(2,1)S(1)}, u32[]{:S(2)}, u32[]{:S(2)}) collective-permute-start(bf16[16,640]{1,0:T(8,128)(2,1)S(1)} %negative_rows.1.row_ref), channel_id=1, source_target_pairs={{0,16},{16,0},{1,17},{17,1},{2,18},{18,2},{3,19},{19,3},{4,20},{20... | collective-permute-start | bytes 61448 | tf_op jit(solution)/shard_map/ppermute | solution.py:319
  3.5 1.7 %pack_query.1.value_ref = bf16[2048,128]{1,0:T(8,128)(2,1)S(1)} custom-call(s32[1,32]{1,0:T(1,128)} %len_ref.5, bf16[6144,128]{1,0:T(8,128)(2,1)} %q_ref.1), custom_call_target="tpu_custom_call" | custom-call | tf_op jit(solution)/shard_map/pack_query/pallas_call | solution.py:320
  5.3 4.0 %collective-permute-start.1 = (bf16[2048,128]{1,0:T(8,128)(2,1)S(1)}, bf16[2048,128]{1,0:T(8,128)(2,1)}, u32[]{:S(2)}, u32[]{:S(2)}) collective-permute-start(bf16[2048,128]{1,0:T(8,128)(2,1)S(1)} %after.5.qp_ref.value_ref), channel_id=1, source_target_pairs={{0,2},{1,3},{2,0},{3,1},{4,6},{5,7},{6,4},{7,5},{8,10},{9,11},{10,... | collective-permute-start | bytes 1572872 | tf_op jit(solution)/shard_map/ppermute | solution.py:296
  9.3 0.9 %copies.1 = bf16[512,640]{1,0:T(8,128)(2,1)} custom-call(bf16[16,640]{1,0:T(8,128)(2,1)S(1)} %negative_rows.1.row_ref, bf16[16,640]{1,0:T(8,128)(2,1)S(1)} %collective-permute-done.other_ref.after_ref), custom_call_target="tpu_custom_call" | custom-call | tf_op jit(solution)/shard_map/copies/pallas_call | solution.py:351
  10.2 7.0 %all-to-all-start = ((bf16[16,32,640]{2,1,0:T(8,128)(2,1)}), bf16[16,32,640]{2,1,0:T(8,128)(2,1)S(1)}, u32[]{:S(2)}, u32[]{:S(2)}) async-start(bf16[16,32,640]{2,1,0:T(8,128)(2,1)} %bitcast.1), calls=%async_computation | async-start | bytes 1310720 | tf_op jit(solution)/shard_map/all_to_all | solution.py:359
  17.2 1.8 %pack_positive.1 = (bf16[128,2048]{1,0:T(8,128)(2,1)S(1)}, f32[1,2048]{1,0:T(1,128)S(1)}, f32[1,2048]{1,0:T(1,128)S(1)}) custom-call(s32[1,32]{1,0:T(1,128)S(1)} %copy-done.4, bf16[6144,128]{1,0:T(8,128)(2,1)S(1)} %copy-done, s32[48,128]{1,0:T(8,128)S(1)} %bitcast.10, bf16[2048,128]{1,0:T(8,128)(2,1)S(1)} %after.5.qp_ref.value_ref), custom_call_target="tpu_custom_call" | custom-call | tf_op jit(solution)/shard_map/pack_positive/pallas_call | solution.py:336
  19.1 1.6 %collective-permute-done.1.value_ref = bf16[2048,128]{1,0:T(8,128)(2,1)} collective-permute-done((bf16[2048,128]{1,0:T(8,128)(2,1)S(1)}, bf16[2048,128]{1,0:T(8,128)(2,1)}, u32[]{:S(2)}, u32[]{:S(2)}) %collective-permute-start.1) | collective-permute-done | bytes 524320 | tf_op jit(solution)/shard_map/ppermute | solution.py:296
  20.6 0.5 collective-permute-start.3
  21.2 1.3 %place_own.1.refs_2_ = bf16[2048,512]{1,0:T(8,128)(2,1)S(1)} custom-call(bf16[2048,128]{1,0:T(8,128)(2,1)S(1)} %after.7.refs_0_, bf16[2048,128]{1,0:T(8,128)(2,1)} %after.6.after_ref.refs_1_), custom_call_target="tpu_custom_call" | custom-call | tf_op jit(solution)/shard_map/place_own/pallas_call | solution.py:362
  22.4 0.8 %collective-permute-done.2.refs_0_ = bf16[2048,128]{1,0:T(8,128)(2,1)S(1)} collective-permute-done((bf16[2048,128]{1,0:T(8,128)(2,1)S(1)}, bf16[2048,128]{1,0:T(8,128)(2,1)S(1)}, u32[]{:S(2)}, u32[]{:S(2)}) %collective-permute-start.2) | collective-permute-done | bytes 524320 | tf_op jit(solution)/shard_map/ppermute | solution.py:296
  23.7 5.5 %all-to-all-done = bf16[16,32,640]{2,1,0:T(8,128)(2,1)S(1)} async-done(((bf16[16,32,640]{2,1,0:T(8,128)(2,1)}), bf16[16,32,640]{2,1,0:T(8,128)(2,1)S(1)}, u32[]{:S(2)}, u32[]{:S(2)}) %all-to-all-start) | async-done | bytes 655392 | tf_op jit(solution)/shard_map/all_to_all | solution.py:359
  29.2 2.0 %scores.1 = (f32[512,2048]{1,0:T(8,128)S(1)}, f32[4,2048]{1,0:T(4,128)S(1)}) custom-call(bf16[512,640]{1,0:T(8,128)(2,1)S(1)} %bitcast.6, bf16[2048,512]{1,0:T(8,128)(2,1)S(1)} %place_near.1.qfull_ref.q_ref, f32[1,2048]{1,0:T(1,128)S(1)} %get-tuple-element.21.idp_ref, f32[1,2048]{1,0:T(1,128)S(1)} %get-tuple-element.20.after_ref.part_ref), custom_call_target="tpu_custom_call" | custom-call | tf_op jit(solution)/shard_map/scores/pallas_call | solution.py:380
  31.2 1.3 %row_products.1 = (f32[256,2048]{1,0:T(8,128)S(1)}, bf16[256,2048]{1,0:T(8,128)(2,1)S(1)}) custom-call(bf16[512,640]{1,0:T(8,128)(2,1)S(1)} %bitcast.7, f32[512,2048]{1,0:T(8,128)S(1)} %get-tuple-element.25.e_ref), custom_call_target="tpu_custom_call" | custom-call | tf_op jit(solution)/shard_map/row_products/pallas_call | solution.py:400
  32.5 0.6 collective-permute-start.5
  33.5 1.9 %collective-permute-done.5.recv_ref = bf16[256,2048]{1,0:T(8,128)(2,1)S(1)} collective-permute-done((bf16[256,2048]{1,0:T(8,128)(2,1)S(1)}, bf16[256,2048]{1,0:T(8,128)(2,1)S(1)}, u32[]{:S(2)}, u32[]{:S(2)}) %collective-permute-start.5) | collective-permute-done | bytes 1048608 | tf_op jit(solution)/shard_map/ppermute | solution.py:296
  35.7 1.4 %collective-permute-start.6 = (bf16[128,2048]{1,0:T(8,128)(2,1)S(1)}, bf16[128,2048]{1,0:T(8,128)(2,1)S(1)}, u32[]{:S(2)}, u32[]{:S(2)}) collective-permute-start(bf16[128,2048]{1,0:T(8,128)(2,1)S(1)} %get-tuple-element.29.after_ref), channel_id=1, source_target_pairs={{0,2},{1,3},{2,0},{3,1},{4,6},{5,7},{6,4},{7,5},{8,10},{9,11},{10,... | collective-permute-start | bytes 1572872 | tf_op jit(solution)/shard_map/ppermute | solution.py:296
  37.1 1.5 %collective-permute-done.7.far = f32[4,2048]{1,0:T(4,128)S(1)} collective-permute-done((f32[4,2048]{1,0:T(4,128)S(1)}, f32[4,2048]{1,0:T(4,128)S(1)}, u32[]{:S(2)}, u32[]{:S(2)}) %collective-permute-start.7) | collective-permute-done | bytes 32800 | tf_op jit(solution)/shard_map/ppermute | solution.py:296
  38.7 1.2 %item_products.1 = bf16[512,512]{1,0:T(8,128)(2,1)S(1)} custom-call(f32[1,2048]{1,0:T(1,128)S(1)} %get-tuple-element.35.scale_ref, f32[512,2048]{1,0:T(8,128)S(1)} %get-tuple-element.25.e_ref, bf16[2048,512]{1,0:T(8,128)(2,1)S(1)} %place_near.1.qfull_ref.q_ref), custom_call_target="tpu_custom_call" | custom-call | tf_op jit(solution)/shard_map/item_products/pallas_call | solution.py:428
  39.9 14.0 %all_to_all.22 = bf16[16,32,512]{2,1,0:T(8,128)(2,1)S(1)} all-to-all(bf16[16,32,512]{2,1,0:T(8,128)(2,1)S(1)} %bitcast.9), channel_id=1, replica_groups=mesh['x'=4,'zl'=2,'y'=4,'grp'=4] {'x','y'}, dimensions={0} | all-to-all | bytes 1048576 | tf_op jit(solution)/shard_map/all_to_all | solution.py:436
  54.0 0.6 collective-permute-start.8
  54.5 2.7 %unpack.1 = bf16[6144,128]{1,0:T(8,128)(2,1)} custom-call(s32[1,32]{1,0:T(1,128)S(1)} %copy-done.4, f32[128,2048]{1,0:T(8,128)S(1)} %get-tuple-element.28.own_ref, bf16[128,2048]{1,0:T(8,128)(2,1)S(1)} %collective-permute-done.6.recv_ref.after_ref, f32[1,2048]{1,0:T(1,128)S(1)} %get-tuple-element.31.near, f32[1,2048]{1,0:T(1,128)S(1)} %get-tuple-element.32.far, ...), custom_call_target="tpu_custom_call" | custom-call | tf_op jit(solution)/shard_map/unpack/pallas_call | solution.py:456
  57.3 0.7 %collective-permute-done.8.recv_ref = f32[16,512]{1,0:T(8,128)S(1)} collective-permute-done((f32[16,512]{1,0:T(8,128)S(1)}, f32[16,512]{1,0:T(8,128)S(1)}, u32[]{:S(2)}, u32[]{:S(2)}) %collective-permute-start.8) | collective-permute-done | bytes 32800 | tf_op jit(solution)/shard_map/ppermute | solution.py:446
  58.0 0.6 %add_neighbour.1 = f32[16,512]{1,0:T(8,128)} custom-call(f32[16,512]{1,0:T(8,128)S(1)} %get-tuple-element.36.own_ref, f32[16,512]{1,0:T(8,128)S(1)} %collective-permute-done.8.recv_ref), custom_call_target="tpu_custom_call" | custom-call | tf_op jit(solution)/shard_map/add_neighbour/pallas_call | solution.py:447
  (27 shorter events, 1.5 us)
Async XLA Ops:
  1.4 15.8 %copy-start = (bf16[6144,128]{1,0:T(8,128)(2,1)S(1)}, bf16[6144,128]{1,0:T(8,128)(2,1)}, u32[]{:S(2)}) copy-start(bf16[6144,128]{1,0:T(8,128)(2,1)} %p_ref.1) | copy-start | bytes 4718596
  1.4 15.8 %copy-start.3 = (s32[6144]{0:T(1024)S(1)}, s32[6144]{0:T(1024)}, u32[]{:S(2)}) copy-start(s32[6144]{0:T(1024)} %param.8) | copy-start | bytes 73732
  1.4 15.8 %copy-start.4 = (s32[1,32]{1,0:T(1,128)S(1)}, s32[1,32]{1,0:T(1,128)}, u32[]{:S(2)}) copy-start(s32[1,32]{1,0:T(1,128)} %len_ref.5) | copy-start | bytes 388
  1.4 3.9 %collective-permute-start = (bf16[16,640]{1,0:T(8,128)(2,1)S(1)}, bf16[16,640]{1,0:T(8,128)(2,1)S(1)}, u32[]{:S(2)}, u32[]{:S(2)}) collective-permute-start(bf16[16,640]{1,0:T(8,128)(2,1)S(1)} %negative_rows.1.row_ref), channel_id=1, source_target_pairs={{0,16},{16,0},{1,17},{17,1},{2,18},{18,2},{3,19},{19,3},{4,20},{20... | collective-permute-start | bytes 61448 | tf_op jit(solution)/shard_map/ppermute | solution.py:319
  5.3 15.3 %collective-permute-start.1 = (bf16[2048,128]{1,0:T(8,128)(2,1)S(1)}, bf16[2048,128]{1,0:T(8,128)(2,1)}, u32[]{:S(2)}, u32[]{:S(2)}) collective-permute-start(bf16[2048,128]{1,0:T(8,128)(2,1)S(1)} %after.5.qp_ref.value_ref), channel_id=1, source_target_pairs={{0,2},{1,3},{2,0},{3,1},{4,6},{5,7},{6,4},{7,5},{8,10},{9,11},{10,... | collective-permute-start | bytes 1572872 | tf_op jit(solution)/shard_map/ppermute | solution.py:296
  10.2 19.0 %all-to-all-start = ((bf16[16,32,640]{2,1,0:T(8,128)(2,1)}), bf16[16,32,640]{2,1,0:T(8,128)(2,1)S(1)}, u32[]{:S(2)}, u32[]{:S(2)}) async-start(bf16[16,32,640]{2,1,0:T(8,128)(2,1)} %bitcast.1), calls=%async_computation | async-start | bytes 1310720 | tf_op jit(solution)/shard_map/all_to_all | solution.py:359
  19.1 3.4 %copy-start.1 = (bf16[128,2048]{1,0:T(8,128)(2,1)}, bf16[128,2048]{1,0:T(8,128)(2,1)S(1)}, u32[]{:S(2)}) copy-start(bf16[128,2048]{1,0:T(8,128)(2,1)S(1)} %get-tuple-element.34.pt_ref) | copy-start | bytes 1572868
  20.6 2.6 %collective-permute-start.2 = (bf16[2048,128]{1,0:T(8,128)(2,1)S(1)}, bf16[2048,128]{1,0:T(8,128)(2,1)S(1)}, u32[]{:S(2)}, u32[]{:S(2)}) collective-permute-start(bf16[2048,128]{1,0:T(8,128)(2,1)S(1)} %after.7.refs_0_), channel_id=1, source_target_pairs={{0,1},{1,0},{2,3},{3,2},{4,5},{5,4},{6,7},{7,6},{8,9},{9,8},{10,11... | collective-permute-start | bytes 1572872 | tf_op jit(solution)/shard_map/ppermute | solution.py:296
  20.6 2.9 %collective-permute-start.3 = (bf16[2048,128]{1,0:T(8,128)(2,1)}, bf16[2048,128]{1,0:T(8,128)(2,1)S(1)}, u32[]{:S(2)}, u32[]{:S(2)}) collective-permute-start(bf16[2048,128]{1,0:T(8,128)(2,1)} %after.6.after_ref.refs_1_), channel_id=1, source_target_pairs={{0,1},{1,0},{2,3},{3,2},{4,5},{5,4},{6,7},{7,6},{8,9},{9,8},{10,11... | collective-permute-start | bytes 1572872 | tf_op jit(solution)/shard_map/ppermute | solution.py:296
  31.1 1.4 %collective-permute-start.4 = (f32[4,2048]{1,0:T(4,128)S(1)}, f32[4,2048]{1,0:T(4,128)S(1)}, u32[]{:S(2)}, u32[]{:S(2)}) collective-permute-start(f32[4,2048]{1,0:T(4,128)S(1)} %get-tuple-element.22.own_ref.own), channel_id=1, source_target_pairs={{0,1},{1,0},{2,3},{3,2},{4,5},{5,4},{6,7},{7,6},{8,9},{9,8},{10,11... | collective-permute-start | bytes 98312 | tf_op jit(solution)/shard_map/ppermute | solution.py:296
  32.5 2.9 %collective-permute-start.5 = (bf16[256,2048]{1,0:T(8,128)(2,1)S(1)}, bf16[256,2048]{1,0:T(8,128)(2,1)S(1)}, u32[]{:S(2)}, u32[]{:S(2)}) collective-permute-start(bf16[256,2048]{1,0:T(8,128)(2,1)S(1)} %after.8), channel_id=1, source_target_pairs={{0,1},{1,0},{2,3},{3,2},{4,5},{5,4},{6,7},{7,6},{8,9},{9,8},{10,11... | collective-permute-start | bytes 3145736 | tf_op jit(solution)/shard_map/ppermute | solution.py:296
  33.1 5.5 %collective-permute-start.7 = (f32[4,2048]{1,0:T(4,128)S(1)}, f32[4,2048]{1,0:T(4,128)S(1)}, u32[]{:S(2)}, u32[]{:S(2)}) collective-permute-start(f32[4,2048]{1,0:T(4,128)S(1)} %get-tuple-element.30.near), channel_id=1, source_target_pairs={{0,2},{1,3},{2,0},{3,1},{4,6},{5,7},{6,4},{7,5},{8,10},{9,11},{10,... | collective-permute-start | bytes 98312 | tf_op jit(solution)/shard_map/ppermute | solution.py:296
  35.7 18.3 %collective-permute-start.6 = (bf16[128,2048]{1,0:T(8,128)(2,1)S(1)}, bf16[128,2048]{1,0:T(8,128)(2,1)S(1)}, u32[]{:S(2)}, u32[]{:S(2)}) collective-permute-start(bf16[128,2048]{1,0:T(8,128)(2,1)S(1)} %get-tuple-element.29.after_ref), channel_id=1, source_target_pairs={{0,2},{1,3},{2,0},{3,1},{4,6},{5,7},{6,4},{7,5},{8,10},{9,11},{10,... | collective-permute-start | bytes 1572872 | tf_op jit(solution)/shard_map/ppermute | solution.py:296
  39.9 14.6 %copy-start.2 = (bf16[128,2048]{1,0:T(8,128)(2,1)S(1)}, bf16[128,2048]{1,0:T(8,128)(2,1)}, u32[]{:S(2)}) copy-start(bf16[128,2048]{1,0:T(8,128)(2,1)} %copy-done.1) | copy-start | bytes 1572868
  54.0 4.0 %collective-permute-start.8 = (f32[16,512]{1,0:T(8,128)S(1)}, f32[16,512]{1,0:T(8,128)S(1)}, u32[]{:S(2)}, u32[]{:S(2)}) collective-permute-start(f32[16,512]{1,0:T(8,128)S(1)} %after.9), channel_id=1, source_target_pairs={{0,16},{16,0},{1,17},{17,1},{2,18},{18,2},{3,19},{19,3},{4,20},{20... | collective-permute-start | bytes 98312 | tf_op jit(solution)/shard_map/ppermute | solution.py:446

commit v7 on v6

--- a/solution.py
+++ b/solution.py
@@ -12,6 +12,7 @@
 LANES = 128
 CHUNK = 64
 TILE = 512
+SUB = 16
 PARTS = 4
 FLOOR = -1e30
 MASKED = -3e38
@@ -25,6 +26,10 @@
     return pltpu.CompilerParams(vmem_limit_bytes=VMEM_BYTES)
 
 
+def weight(micros):
+    return pl.CostEstimate(flops=int(micros * 1e9), transcendentals=0, bytes_accessed=0)
+
+
 def whole():
     return pl.BlockSpec(memory_space=pltpu.VMEM)
 
@@ -59,12 +64,16 @@
 
 
 def copies_kernel(row_ref, other_ref, out_ref):
-    first = lax.axis_index("zl") == 0
-    size = row_ref.shape[0]
+    second = lax.axis_index("zl") == 1
     row, other = row_ref[...], other_ref[...]
-    pair = (jnp.where(first, row, other), jnp.where(first, other, row))
+    low, high = jnp.where(second, other, row), jnp.where(second, row, other)
+    size = SUB
+    parts = []
+    for k in range(row_ref.shape[0] // size - 1):
+        parts += [low[k * size : (k + 1) * size], high[k * size : (k + 1) * size]]
+    parts.append((low[-size:].astype(F32) + pltpu.roll(high[-size:].astype(F32), 3, 1)).astype(BF16))
     for i in range(out_ref.shape[0] // size):
-        out_ref[i * size : (i + 1) * size, :] = pair[i % 2]
+        out_ref[i * size : (i + 1) * size, :] = parts[i % len(parts)]
 
 
 def sum_kernel(share_ref, own_ref, other_ref):
@@ -89,11 +98,14 @@
 
 def row_kernel(neg_ref, id_ref, out_ref, held_id, sems):
     rows, width = neg_ref.shape
-    load_id = pltpu.make_async_copy(id_ref, held_id, sems.at[0])
-    load = pltpu.make_async_copy(neg_ref, out_ref.at[:, pl.ds(0, width)], sems.at[1])
-    load_id.start()
-    load.start()
-    load_id.wait()
+    blocks = width // LANES
+    loads = [pltpu.make_async_copy(id_ref, held_id, sems.at[blocks])]
+    for k in range(blocks):
+        src, dst = neg_ref.at[:, pl.ds(k * LANES, LANES)], out_ref.at[pl.ds(k * rows, rows)]
+        loads.append(pltpu.make_async_copy(src, dst, sems.at[k]))
+    for load in loads:
+        load.start()
+    loads[0].wait()
     shape = (rows, LANES)
     lane = lax.broadcasted_iota(jnp.int32, shape, 1)
     ids = jnp.concatenate([held_id[...], jnp.zeros((1, LANES - rows), jnp.int32)], axis=1)
@@ -101,8 +113,9 @@
     value = jnp.sum(jnp.where(own, jnp.broadcast_to(ids, shape), 0), axis=1, keepdims=True)
     value = jnp.broadcast_to(value, shape)
     digit = jnp.where(lane == 0, value >> 16, jnp.where(lane == 1, (value >> 8) & 255, value & 255))
-    out_ref[:, width:] = jnp.where(lane < 3, digit, 0).astype(F32).astype(BF16)
-    load.wait()
+    out_ref[blocks * rows :, :] = jnp.where(lane < 3, digit, 0).astype(F32).astype(BF16)
+    for load in loads[1:]:
+        load.wait()
 
 
 def pack_query(len_ref, q_ref, qp_ref, held_q, held_len, packed, sems):
@@ -166,13 +179,28 @@
         refs[-1][:, block_of(member, step)] = ref[...]
 
 
-def scores_kernel(neg_ref, qfull_ref, idp_ref, part_ref, e_ref, stat_ref, negid):
-    width = 4 * LANES
-    lane = lax.broadcasted_iota(jnp.int32, (1, LANES), 1)
-    place = jnp.where(lane == 0, 65536.0, jnp.where(lane == 1, 256.0, jnp.where(lane == 2, 1.0, 0.0)))
-    value = jnp.sum(neg_ref[:, width : width + LANES].astype(F32) * place, axis=1, keepdims=True)
-    negid[...] = jnp.broadcast_to(value, negid.shape)
-    e_ref[...] = dot(neg_ref[:, :width], qfull_ref[...], 1, 1)
+def pool_kernel(msg_ref, neg_ref, negid, tiles):
+    blocks, pair = neg_ref.shape[1] // LANES, 2 * SUB
+    pairs = neg_ref.shape[0] // pair
+    for p in range(pairs):
+        base = p * (2 * blocks + 1) * SUB
+        for k in range(blocks):
+            block = msg_ref[base + k * pair : base + (k + 1) * pair, :]
+            neg_ref[p * pair : (p + 1) * pair, k * LANES : (k + 1) * LANES] = block
+        tiles[p * SUB : (p + 1) * SUB, :] = msg_ref[base + blocks * pair : base + blocks * pair + SUB, :]
+    lane = lax.broadcasted_iota(jnp.int32, (2 * LANES, LANES), 1)
+    place = lane - 3 * (lax.broadcasted_iota(jnp.int32, (2 * LANES, LANES), 0) // LANES)
+    place = jnp.where(place == 0, 65536.0, jnp.where(place == 1, 256.0, jnp.where(place == 2, 1.0, 0.0)))
+    value = dot(tiles[...], place.astype(BF16), 1, 1)
+    for p in range(pairs):
+        for k in range(2):
+            at = p * pair + k * SUB
+            negid[at : at + SUB, :] = value[p * SUB : (p + 1) * SUB, k * LANES : (k + 1) * LANES]
+
+
+def scores_kernel(msg_ref, qfull_ref, idp_ref, part_ref, neg_ref, e_ref, stat_ref, negid, tiles):
+    pool_kernel(msg_ref, neg_ref, negid, tiles)
+    e_ref[...] = dot(neg_ref[...], qfull_ref[...], 1, 1)
     for k in range(e_ref.shape[1] // LANES):
         at = slice(k * LANES, (k + 1) * LANES)
         part = jnp.where(negid[...] == idp_ref[:, at], MASKED, e_ref[:, at])
@@ -303,15 +331,15 @@
     own_neg, width = negatives.shape
     slots = query.shape[0]
     negs = own_neg * seqs
-    half = 2 * LANES
+    half, blocks = 2 * LANES, width // LANES
     vmem = pltpu.VMEM
 
     row = pl.pallas_call(
         row_kernel,
-        out_shape=vmem((own_neg, width + LANES), BF16),
+        out_shape=vmem((own_neg * (blocks + 1), LANES), BF16),
         in_specs=[anywhere()] * 2,
         out_specs=whole(),
-        scratch_shapes=[vmem((1, own_neg), jnp.int32), pltpu.SemaphoreType.DMA((2,))],
+        scratch_shapes=[vmem((1, own_neg), jnp.int32), pltpu.SemaphoreType.DMA((blocks + 1,))],
         compiler_params=params(),
         name="negative_rows",
     )(in_hbm(negatives), in_hbm(neg_ids.reshape(1, own_neg)))
@@ -339,18 +367,18 @@
         in_specs=[small(), whole(), whole(), whole()],
         out_specs=(whole(), whole(), whole()),
         scratch_shapes=[vmem((live + MAXLEN, LANES), F32), vmem((live // LANES + 8, LANES), jnp.int32)],
+        cost_estimate=weight(10),
         compiler_params=params(),
         name="pack_positive",
     )(lengths, pos_emb, pos_ids.reshape(slots // LANES, LANES), held(qp))
 
-    q2 = after(q2, part)
     qp = after(qp, q2)
     q1 = swap(qp, 1, groups)
     q3 = swap(q2, 1, groups)
 
     copies = pl.pallas_call(
         copies_kernel,
-        out_shape=vmem((negs, width + LANES), BF16),
+        out_shape=vmem((negs // 2 * (2 * blocks + 1), LANES), BF16),
         in_specs=[whole()] * 2,
         out_specs=whole(),
         compiler_params=params(),
@@ -377,12 +405,12 @@
         name="place_near",
     )(held(q1), held(q3), held(qfull))
     qfull = held(qfull)
-    e, stat = pl.pallas_call(
+    pool, e, stat = pl.pallas_call(
         scores_kernel,
-        out_shape=(vmem((negs, live), F32), vmem((4, live), F32)),
+        out_shape=(vmem((negs, width), BF16), vmem((negs, live), F32), vmem((4, live), F32)),
         in_specs=[whole()] * 4,
-        out_specs=(whole(), whole()),
-        scratch_shapes=[vmem((negs, LANES), F32)],
+        out_specs=(whole(),) * 3,
+        scratch_shapes=[vmem((negs, LANES), F32), vmem((negs // 2, LANES), BF16)],
         compiler_params=params(),
         name="scores",
     )(pool, qfull, held(idp), held(part))
@@ -405,7 +433,7 @@
         scratch_shapes=[vmem((width, negs), BF16)],
         compiler_params=params(),
         name="row_products",
-    )(pool, held(e))
+    )(held(pool), held(e))
     recv = swap(after(send, stat1), 1, groups)
     own, onward = pl.pallas_call(
         combine_kernel,

time: 59 us -> 58.6 us (level)
  waiting for transfers between devices: 12.3 us -> 10.8 us
  local copies, waits for them, and re-layouts: 0.03 us -> 0.83 us
    ppermute x7, waiting for transfers between devices: 6.04 us -> 5.23 us  [swap(): return lax.ppermute(value, 'grp', [(g, g ^ step) for g in range(groups)])]
    unnamed x10, local copies, waits for them, and re-layouts: 0.03 us -> 0.83 us
    all_to_all x1, waiting for transfers between devices: 5.45 us -> 4.78 us  [shards(): lax.all_to_all(copies, ('x', 'y'), split_axis=0, concat_axis=0, tiled=True)]
where the time goes in v7:
time: 58.6 us; the launch traced here: 58.3 us
  starting transfers between devices  16.6 us (28%)
  Pallas kernels  14.8 us (25%)
  blocking collectives  14.4 us (25%)
  waiting for transfers between devices  10.8 us (18%)
  local copies, waits for them, and re-layouts  0.83 us (1%)
  between operations  0.81 us (1%)
    all_to_all x1, blocking collectives, shards(): lax.all_to_all(items, ('x', 'y'), split_axis=0, concat_axis=0, tiled=True)  14.4 us
    all_to_all x1, starting transfers between devices, shards(): lax.all_to_all(copies, ('x', 'y'), split_axis=0, concat_axis=0, tiled=True)  7.03 us
    ppermute x7, starting transfers between devices, swap(): return lax.ppermute(value, 'grp', [(g, g ^ step) for g in range(groups)])  6.92 us
    ppermute x7, waiting for transfers between devices, swap(): return lax.ppermute(value, 'grp', [(g, g ^ step) for g in range(groups)])  5.23 us
    all_to_all x1, waiting for transfers between devices, shards(): lax.all_to_all(copies, ('x', 'y'), split_axis=0, concat_axis=0, tiled=True)  4.78 us
    pallas_call x1, Pallas kernels, shards(): pl.pallas_call(unpack_kernel, out_shape=jax.ShapeDtypeStruct((slots, LANE...  2.71 us
    ppermute x1, starting transfers between devices, shards(): other = lax.ppermute(row, 'zl', [(i, pair - 1 - i) for i in range(pair)])  2.08 us
    pallas_call x1, Pallas kernels, shards(): pl.pallas_call(scores_kernel, out_shape=(vmem((negs, width), BF16), vmem(...  1.87 us
  transfers between devices with their start and end apart: 10, of which 8 were waited for; matrix products, arithmetic and copies ran while one was open for 0% of the time, Pallas kernels for 20%

profile of v7, /device:TPU:0, one launch (start us, length us, event | category | flops | bytes accessed | tf_op | source)
XLA Modules:
  0.0 58.3 jit_solution(11492843901078938227)
XLA Ops:
  0.6 0.8 %negative_rows.1.row_ref = bf16[80,128]{1,0:T(8,128)(2,1)S(1)} custom-call(bf16[16,512]{1,0:T(8,128)(2,1)} %neg_ref.1, s32[1,16]{1,0:T(1,128)} %bitcast.10), custom_call_target="tpu_custom_call" | custom-call | tf_op jit(solution)/shard_map/negative_rows/pallas_call | solution.py:337
  1.5 2.1 %collective-permute-start = (bf16[80,128]{1,0:T(8,128)(2,1)S(1)}, bf16[80,128]{1,0:T(8,128)(2,1)S(1)}, u32[]{:S(2)}, u32[]{:S(2)}) collective-permute-start(bf16[80,128]{1,0:T(8,128)(2,1)S(1)} %negative_rows.1.row_ref), channel_id=1, source_target_pairs={{0,16},{16,0},{1,17},{17,1},{2,18},{18,2},{3,19},{19,3},{4,20},{20... | collective-permute-start | bytes 61448 | tf_op jit(solution)/shard_map/ppermute | solution.py:347
  3.6 1.7 %pack_query.1.value_ref = bf16[2048,128]{1,0:T(8,128)(2,1)S(1)} custom-call(s32[1,32]{1,0:T(1,128)} %len_ref.5, bf16[6144,128]{1,0:T(8,128)(2,1)} %q_ref.1), custom_call_target="tpu_custom_call" | custom-call | tf_op jit(solution)/shard_map/pack_query/pallas_call | solution.py:348
  5.3 4.0 %collective-permute-start.1 = (bf16[2048,128]{1,0:T(8,128)(2,1)S(1)}, bf16[2048,128]{1,0:T(8,128)(2,1)}, u32[]{:S(2)}, u32[]{:S(2)}) collective-permute-start(bf16[2048,128]{1,0:T(8,128)(2,1)S(1)} %after.4.value_ref.qp_ref), channel_id=1, source_target_pairs={{0,2},{1,3},{2,0},{3,1},{4,6},{5,7},{6,4},{7,5},{8,10},{9,11},{10,... | collective-permute-start | bytes 1572872 | tf_op jit(solution)/shard_map/ppermute | solution.py:324
  9.3 0.9 %copies.1 = bf16[2304,128]{1,0:T(8,128)(2,1)} custom-call(bf16[80,128]{1,0:T(8,128)(2,1)S(1)} %negative_rows.1.row_ref, bf16[80,128]{1,0:T(8,128)(2,1)S(1)} %collective-permute-done.other_ref.after_ref), custom_call_target="tpu_custom_call" | custom-call | tf_op jit(solution)/shard_map/copies/pallas_call | solution.py:379
  10.2 7.0 %all-to-all-start = ((bf16[16,144,128]{2,1,0:T(8,128)(2,1)}), bf16[16,144,128]{2,1,0:T(8,128)(2,1)S(1)}, u32[]{:S(2)}, u32[]{:S(2)}) async-start(bf16[16,144,128]{2,1,0:T(8,128)(2,1)} %bitcast.1), calls=%async_computation | async-start | bytes 1179648 | tf_op jit(solution)/shard_map/all_to_all | solution.py:387
  17.3 1.8 %pack_positive.1 = (bf16[128,2048]{1,0:T(8,128)(2,1)S(1)}, f32[1,2048]{1,0:T(1,128)S(1)}, f32[1,2048]{1,0:T(1,128)S(1)}) custom-call(s32[1,32]{1,0:T(1,128)S(1)} %copy-done.2, bf16[6144,128]{1,0:T(8,128)(2,1)S(1)} %copy-done.3, s32[48,128]{1,0:T(8,128)S(1)} %bitcast.9, bf16[2048,128]{1,0:T(8,128)(2,1)S(1)} %after.4.value_ref.qp_ref), custom_call_target="tpu_custom_call" | custom-call | flops 10000000000 | tf_op jit(solution)/shard_map/pack_positive/pallas_call | solution.py:364
  19.1 0.8 %copy-done = bf16[128,2048]{1,0:T(8,128)(2,1)} copy-done((bf16[128,2048]{1,0:T(8,128)(2,1)}, bf16[128,2048]{1,0:T(8,128)(2,1)S(1)}, u32[]{:S(2)}) %copy-start) | copy-done | bytes 524312
  19.9 0.7 %collective-permute-done.1.after_ref.refs_1_ = bf16[2048,128]{1,0:T(8,128)(2,1)} collective-permute-done((bf16[2048,128]{1,0:T(8,128)(2,1)S(1)}, bf16[2048,128]{1,0:T(8,128)(2,1)}, u32[]{:S(2)}, u32[]{:S(2)}) %collective-permute-start.1) | collective-permute-done | bytes 524320 | tf_op jit(solution)/shard_map/ppermute | solution.py:324
  21.2 1.3 %place_own.1.refs_2_ = bf16[2048,512]{1,0:T(8,128)(2,1)S(1)} custom-call(bf16[2048,128]{1,0:T(8,128)(2,1)S(1)} %after.5.refs_0_, bf16[2048,128]{1,0:T(8,128)(2,1)} %collective-permute-done.1.after_ref.refs_1_), custom_call_target="tpu_custom_call" | custom-call | tf_op jit(solution)/shard_map/place_own/pallas_call | solution.py:390
  22.4 0.8 %collective-permute-done.2.refs_0_ = bf16[2048,128]{1,0:T(8,128)(2,1)S(1)} collective-permute-done((bf16[2048,128]{1,0:T(8,128)(2,1)S(1)}, bf16[2048,128]{1,0:T(8,128)(2,1)S(1)}, u32[]{:S(2)}, u32[]{:S(2)}) %collective-permute-start.2) | collective-permute-done | bytes 524320 | tf_op jit(solution)/shard_map/ppermute | solution.py:324
  23.7 4.8 %all-to-all-done = bf16[16,144,128]{2,1,0:T(8,128)(2,1)S(1)} async-done(((bf16[16,144,128]{2,1,0:T(8,128)(2,1)}), bf16[16,144,128]{2,1,0:T(8,128)(2,1)S(1)}, u32[]{:S(2)}, u32[]{:S(2)}) %all-to-all-start) | async-done | bytes 589856 | tf_op jit(solution)/shard_map/all_to_all | solution.py:387
  28.5 1.9 %scores.1 = (bf16[512,512]{1,0:T(8,128)(2,1)S(1)}, f32[512,2048]{1,0:T(8,128)S(1)}, f32[4,2048]{1,0:T(4,128)S(1)}) custom-call(bf16[2304,128]{1,0:T(8,128)(2,1)S(1)} %bitcast.6, bf16[2048,512]{1,0:T(8,128)(2,1)S(1)} %place_near.1.qfull_ref.q_ref, f32[1,2048]{1,0:T(1,128)S(1)} %get-tuple-element.21.idp_ref, f32[1,2048]{1,0:T(1,128)S(1)} %get-tuple-element.22.part_ref), custom_call_target="tpu_custom_call" | custom-call | tf_op jit(solution)/shard_map/scores/pallas_call | solution.py:408
  30.5 1.3 %row_products.1 = (f32[256,2048]{1,0:T(8,128)S(1)}, bf16[256,2048]{1,0:T(8,128)(2,1)S(1)}) custom-call(bf16[512,512]{1,0:T(8,128)(2,1)S(1)} %get-tuple-element.26.neg_ref, f32[512,2048]{1,0:T(8,128)S(1)} %get-tuple-element.27.e_ref), custom_call_target="tpu_custom_call" | custom-call | tf_op jit(solution)/shard_map/row_products/pallas_call | solution.py:428
  31.8 0.6 collective-permute-start.5
  32.7 1.9 %collective-permute-done.5.recv_ref = bf16[256,2048]{1,0:T(8,128)(2,1)S(1)} collective-permute-done((bf16[256,2048]{1,0:T(8,128)(2,1)S(1)}, bf16[256,2048]{1,0:T(8,128)(2,1)S(1)}, u32[]{:S(2)}, u32[]{:S(2)}) %collective-permute-start.5) | collective-permute-done | bytes 1048608 | tf_op jit(solution)/shard_map/ppermute | solution.py:324
  34.9 1.4 %collective-permute-start.6 = (bf16[128,2048]{1,0:T(8,128)(2,1)S(1)}, bf16[128,2048]{1,0:T(8,128)(2,1)S(1)}, u32[]{:S(2)}, u32[]{:S(2)}) collective-permute-start(bf16[128,2048]{1,0:T(8,128)(2,1)S(1)} %get-tuple-element.31.after_ref), channel_id=1, source_target_pairs={{0,2},{1,3},{2,0},{3,1},{4,6},{5,7},{6,4},{7,5},{8,10},{9,11},{10,... | collective-permute-start | bytes 1572872 | tf_op jit(solution)/shard_map/ppermute | solution.py:324
  36.4 1.5 %collective-permute-done.7.far = f32[4,2048]{1,0:T(4,128)S(1)} collective-permute-done((f32[4,2048]{1,0:T(4,128)S(1)}, f32[4,2048]{1,0:T(4,128)S(1)}, u32[]{:S(2)}, u32[]{:S(2)}) %collective-permute-start.7) | collective-permute-done | bytes 32800 | tf_op jit(solution)/shard_map/ppermute | solution.py:324
  37.9 1.2 %item_products.1 = bf16[512,512]{1,0:T(8,128)(2,1)S(1)} custom-call(f32[1,2048]{1,0:T(1,128)S(1)} %get-tuple-element.37.scale_ref, f32[512,2048]{1,0:T(8,128)S(1)} %get-tuple-element.27.e_ref, bf16[2048,512]{1,0:T(8,128)(2,1)S(1)} %place_near.1.qfull_ref.q_ref), custom_call_target="tpu_custom_call" | custom-call | tf_op jit(solution)/shard_map/item_products/pallas_call | solution.py:456
  39.2 14.4 %all_to_all.22 = bf16[16,32,512]{2,1,0:T(8,128)(2,1)S(1)} all-to-all(bf16[16,32,512]{2,1,0:T(8,128)(2,1)S(1)} %bitcast.8), channel_id=1, replica_groups=mesh['x'=4,'zl'=2,'y'=4,'grp'=4] {'x','y'}, dimensions={0} | all-to-all | bytes 1048576 | tf_op jit(solution)/shard_map/all_to_all | solution.py:464
  53.6 0.6 %collective-permute-start.8 = (f32[16,512]{1,0:T(8,128)S(1)}, f32[16,512]{1,0:T(8,128)S(1)}, u32[]{:S(2)}, u32[]{:S(2)}) collective-permute-start(f32[16,512]{1,0:T(8,128)S(1)} %after.7), channel_id=1, source_target_pairs={{0,16},{16,0},{1,17},{17,1},{2,18},{18,2},{3,19},{19,3},{4,20},{20... | collective-permute-start | bytes 98312 | tf_op jit(solution)/shard_map/ppermute | solution.py:474
  54.2 2.7 %unpack.1 = bf16[6144,128]{1,0:T(8,128)(2,1)} custom-call(s32[1,32]{1,0:T(1,128)S(1)} %copy-done.2, f32[128,2048]{1,0:T(8,128)S(1)} %get-tuple-element.30.own_ref, bf16[128,2048]{1,0:T(8,128)(2,1)S(1)} %collective-permute-done.6.recv_ref.after_ref, f32[1,2048]{1,0:T(1,128)S(1)} %get-tuple-element.33.near, f32[1,2048]{1,0:T(1,128)S(1)} %get-tuple-element.34.far, ...), custom_call_target="tpu_custom_call" | custom-call | tf_op jit(solution)/shard_map/unpack/pallas_call | solution.py:484
  57.0 0.7 %collective-permute-done.8.recv_ref = f32[16,512]{1,0:T(8,128)S(1)} collective-permute-done((f32[16,512]{1,0:T(8,128)S(1)}, f32[16,512]{1,0:T(8,128)S(1)}, u32[]{:S(2)}, u32[]{:S(2)}) %collective-permute-start.8) | collective-permute-done | bytes 32800 | tf_op jit(solution)/shard_map/ppermute | solution.py:474
  57.6 0.6 %add_neighbour.1 = f32[16,512]{1,0:T(8,128)} custom-call(f32[16,512]{1,0:T(8,128)S(1)} %get-tuple-element.38.own_ref, f32[16,512]{1,0:T(8,128)S(1)} %collective-permute-done.8.recv_ref), custom_call_target="tpu_custom_call" | custom-call | tf_op jit(solution)/shard_map/add_neighbour/pallas_call | solution.py:475
  (26 shorter events, 2.0 us)
Async XLA Ops:
  1.4 15.8 %copy-start.2 = (s32[1,32]{1,0:T(1,128)S(1)}, s32[1,32]{1,0:T(1,128)}, u32[]{:S(2)}) copy-start(s32[1,32]{1,0:T(1,128)} %len_ref.5) | copy-start | bytes 388
  1.4 15.8 %copy-start.3 = (bf16[6144,128]{1,0:T(8,128)(2,1)S(1)}, bf16[6144,128]{1,0:T(8,128)(2,1)}, u32[]{:S(2)}) copy-start(bf16[6144,128]{1,0:T(8,128)(2,1)} %p_ref.1) | copy-start | bytes 4718596
  1.5 15.8 %copy-start.4 = (s32[6144]{0:T(1024)S(1)}, s32[6144]{0:T(1024)}, u32[]{:S(2)}) copy-start(s32[6144]{0:T(1024)} %param.8) | copy-start | bytes 73732
  1.5 3.9 %collective-permute-start = (bf16[80,128]{1,0:T(8,128)(2,1)S(1)}, bf16[80,128]{1,0:T(8,128)(2,1)S(1)}, u32[]{:S(2)}, u32[]{:S(2)}) collective-permute-start(bf16[80,128]{1,0:T(8,128)(2,1)S(1)} %negative_rows.1.row_ref), channel_id=1, source_target_pairs={{0,16},{16,0},{1,17},{17,1},{2,18},{18,2},{3,19},{19,3},{4,20},{20... | collective-permute-start | bytes 61448 | tf_op jit(solution)/shard_map/ppermute | solution.py:347
  5.3 15.3 %collective-permute-start.1 = (bf16[2048,128]{1,0:T(8,128)(2,1)S(1)}, bf16[2048,128]{1,0:T(8,128)(2,1)}, u32[]{:S(2)}, u32[]{:S(2)}) collective-permute-start(bf16[2048,128]{1,0:T(8,128)(2,1)S(1)} %after.4.value_ref.qp_ref), channel_id=1, source_target_pairs={{0,2},{1,3},{2,0},{3,1},{4,6},{5,7},{6,4},{7,5},{8,10},{9,11},{10,... | collective-permute-start | bytes 1572872 | tf_op jit(solution)/shard_map/ppermute | solution.py:324
  10.2 18.3 %all-to-all-start = ((bf16[16,144,128]{2,1,0:T(8,128)(2,1)}), bf16[16,144,128]{2,1,0:T(8,128)(2,1)S(1)}, u32[]{:S(2)}, u32[]{:S(2)}) async-start(bf16[16,144,128]{2,1,0:T(8,128)(2,1)} %bitcast.1), calls=%async_computation | async-start | bytes 1179648 | tf_op jit(solution)/shard_map/all_to_all | solution.py:387
  19.1 0.8 %copy-start = (bf16[128,2048]{1,0:T(8,128)(2,1)}, bf16[128,2048]{1,0:T(8,128)(2,1)S(1)}, u32[]{:S(2)}) copy-start(bf16[128,2048]{1,0:T(8,128)(2,1)S(1)} %get-tuple-element.36.pt_ref) | copy-start | bytes 1572868
  20.7 2.6 %collective-permute-start.2 = (bf16[2048,128]{1,0:T(8,128)(2,1)S(1)}, bf16[2048,128]{1,0:T(8,128)(2,1)S(1)}, u32[]{:S(2)}, u32[]{:S(2)}) collective-permute-start(bf16[2048,128]{1,0:T(8,128)(2,1)S(1)} %after.5.refs_0_), channel_id=1, source_target_pairs={{0,1},{1,0},{2,3},{3,2},{4,5},{5,4},{6,7},{7,6},{8,9},{9,8},{10,11... | collective-permute-start | bytes 1572872 | tf_op jit(solution)/shard_map/ppermute | solution.py:324
  20.7 2.9 %collective-permute-start.3 = (bf16[2048,128]{1,0:T(8,128)(2,1)}, bf16[2048,128]{1,0:T(8,128)(2,1)S(1)}, u32[]{:S(2)}, u32[]{:S(2)}) collective-permute-start(bf16[2048,128]{1,0:T(8,128)(2,1)} %collective-permute-done.1.after_ref.refs_1_), channel_id=1, source_target_pairs={{0,1},{1,0},{2,3},{3,2},{4,5},{5,4},{6,7},{7,6},{8,9},{9,8},{10,11... | collective-permute-start | bytes 1572872 | tf_op jit(solution)/shard_map/ppermute | solution.py:324
  30.4 1.4 %collective-permute-start.4 = (f32[4,2048]{1,0:T(4,128)S(1)}, f32[4,2048]{1,0:T(4,128)S(1)}, u32[]{:S(2)}, u32[]{:S(2)}) collective-permute-start(f32[4,2048]{1,0:T(4,128)S(1)} %get-tuple-element.23.own_ref.own), channel_id=1, source_target_pairs={{0,1},{1,0},{2,3},{3,2},{4,5},{5,4},{6,7},{7,6},{8,9},{9,8},{10,11... | collective-permute-start | bytes 98312 | tf_op jit(solution)/shard_map/ppermute | solution.py:324
  31.8 2.9 %collective-permute-start.5 = (bf16[256,2048]{1,0:T(8,128)(2,1)S(1)}, bf16[256,2048]{1,0:T(8,128)(2,1)S(1)}, u32[]{:S(2)}, u32[]{:S(2)}) collective-permute-start(bf16[256,2048]{1,0:T(8,128)(2,1)S(1)} %after.6), channel_id=1, source_target_pairs={{0,1},{1,0},{2,3},{3,2},{4,5},{5,4},{6,7},{7,6},{8,9},{9,8},{10,11... | collective-permute-start | bytes 3145736 | tf_op jit(solution)/shard_map/ppermute | solution.py:324
  32.4 5.5 %collective-permute-start.7 = (f32[4,2048]{1,0:T(4,128)S(1)}, f32[4,2048]{1,0:T(4,128)S(1)}, u32[]{:S(2)}, u32[]{:S(2)}) collective-permute-start(f32[4,2048]{1,0:T(4,128)S(1)} %get-tuple-element.32.near), channel_id=1, source_target_pairs={{0,2},{1,3},{2,0},{3,1},{4,6},{5,7},{6,4},{7,5},{8,10},{9,11},{10,... | collective-permute-start | bytes 98312 | tf_op jit(solution)/shard_map/ppermute | solution.py:324
  34.9 18.7 %collective-permute-start.6 = (bf16[128,2048]{1,0:T(8,128)(2,1)S(1)}, bf16[128,2048]{1,0:T(8,128)(2,1)S(1)}, u32[]{:S(2)}, u32[]{:S(2)}) collective-permute-start(bf16[128,2048]{1,0:T(8,128)(2,1)S(1)} %get-tuple-element.31.after_ref), channel_id=1, source_target_pairs={{0,2},{1,3},{2,0},{3,1},{4,6},{5,7},{6,4},{7,5},{8,10},{9,11},{10,... | collective-permute-start | bytes 1572872 | tf_op jit(solution)/shard_map/ppermute | solution.py:324
  39.2 15.1 %copy-start.1 = (bf16[128,2048]{1,0:T(8,128)(2,1)S(1)}, bf16[128,2048]{1,0:T(8,128)(2,1)}, u32[]{:S(2)}) copy-start(bf16[128,2048]{1,0:T(8,128)(2,1)} %copy-done) | copy-start | bytes 1572868
  53.6 4.0 %collective-permute-start.8 = (f32[16,512]{1,0:T(8,128)S(1)}, f32[16,512]{1,0:T(8,128)S(1)}, u32[]{:S(2)}, u32[]{:S(2)}) collective-permute-start(f32[16,512]{1,0:T(8,128)S(1)} %after.7), channel_id=1, source_target_pairs={{0,16},{16,0},{1,17},{17,1},{2,18},{18,2},{3,19},{19,3},{4,20},{20... | collective-permute-start | bytes 98312 | tf_op jit(solution)/shard_map/ppermute | solution.py:474

commit v8 on v7

--- a/solution.py
+++ b/solution.py
@@ -10,7 +10,7 @@
 
 MAXLEN = 192
 LANES = 128
-CHUNK = 64
+CHUNK = 192
 TILE = 512
 SUB = 16
 PARTS = 4

time: 58.6 us -> 58.5 us (level)
  Pallas kernels: 14.8 us -> 14 us
  transfers between devices with their start and end apart: 10 -> 10, of which waited for: 8 -> 8; matrix products, arithmetic and copies ran while one was open for 0% -> 0% of each run, Pallas kernels for 20% -> 18%
where the time goes in v8:
time: 58.5 us; the launch traced here: 58.1 us
  starting transfers between devices  16.8 us (29%)
  blocking collectives  14.4 us (25%)
  Pallas kernels  14 us (24%)
  waiting for transfers between devices  11.3 us (19%)
  local copies, waits for them, and re-layouts  0.83 us (1%)
  between operations  0.81 us (1%)
    all_to_all x1, blocking collectives, shards(): lax.all_to_all(items, ('x', 'y'), split_axis=0, concat_axis=0, tiled=True)  14.4 us
    all_to_all x1, starting transfers between devices, shards(): lax.all_to_all(copies, ('x', 'y'), split_axis=0, concat_axis=0, tiled=True)  7.03 us
    ppermute x7, starting transfers between devices, swap(): return lax.ppermute(value, 'grp', [(g, g ^ step) for g in range(groups)])  6.92 us
    ppermute x7, waiting for transfers between devices, swap(): return lax.ppermute(value, 'grp', [(g, g ^ step) for g in range(groups)])  5.32 us
    all_to_all x1, waiting for transfers between devices, shards(): lax.all_to_all(copies, ('x', 'y'), split_axis=0, concat_axis=0, tiled=True)  4.76 us
    pallas_call x1, Pallas kernels, shards(): pl.pallas_call(unpack_kernel, out_shape=jax.ShapeDtypeStruct((slots, LANE...  2.27 us
    ppermute x1, starting transfers between devices, shards(): other = lax.ppermute(row, 'zl', [(i, pair - 1 - i) for i in range(pair)])  2.08 us
    pallas_call x1, Pallas kernels, shards(): pl.pallas_call(scores_kernel, out_shape=(vmem((negs, width), BF16), vmem(...  1.87 us
  transfers between devices with their start and end apart: 10, of which 8 were waited for; matrix products, arithmetic and copies ran while one was open for 0% of the time, Pallas kernels for 18%

profile of v8, /device:TPU:0, one launch (start us, length us, event | category | flops | bytes accessed | tf_op | source)
XLA Modules:
  0.0 58.1 jit_solution(6216847133553961036)
XLA Ops:
  0.6 0.8 %negative_rows.1.row_ref = bf16[80,128]{1,0:T(8,128)(2,1)S(1)} custom-call(bf16[16,512]{1,0:T(8,128)(2,1)} %neg_ref.1, s32[1,16]{1,0:T(1,128)} %bitcast.10), custom_call_target="tpu_custom_call" | custom-call | tf_op jit(solution)/shard_map/negative_rows/pallas_call | solution.py:337
  1.5 2.1 %collective-permute-start = (bf16[80,128]{1,0:T(8,128)(2,1)S(1)}, bf16[80,128]{1,0:T(8,128)(2,1)S(1)}, u32[]{:S(2)}, u32[]{:S(2)}) collective-permute-start(bf16[80,128]{1,0:T(8,128)(2,1)S(1)} %negative_rows.1.row_ref), channel_id=1, source_target_pairs={{0,16},{16,0},{1,17},{17,1},{2,18},{18,2},{3,19},{19,3},{4,20},{20... | collective-permute-start | bytes 61448 | tf_op jit(solution)/shard_map/ppermute | solution.py:347
  3.6 1.5 %pack_query.1.value_ref = bf16[2048,128]{1,0:T(8,128)(2,1)S(1)} custom-call(s32[1,32]{1,0:T(1,128)} %len_ref.5, bf16[6144,128]{1,0:T(8,128)(2,1)} %q_ref.1), custom_call_target="tpu_custom_call" | custom-call | tf_op jit(solution)/shard_map/pack_query/pallas_call | solution.py:348
  5.3 4.0 %collective-permute-start.1 = (bf16[2048,128]{1,0:T(8,128)(2,1)S(1)}, bf16[2048,128]{1,0:T(8,128)(2,1)}, u32[]{:S(2)}, u32[]{:S(2)}) collective-permute-start(bf16[2048,128]{1,0:T(8,128)(2,1)S(1)} %after.4.value_ref.qp_ref), channel_id=1, source_target_pairs={{0,2},{1,3},{2,0},{3,1},{4,6},{5,7},{6,4},{7,5},{8,10},{9,11},{10,... | collective-permute-start | bytes 1572872 | tf_op jit(solution)/shard_map/ppermute | solution.py:324
  9.3 0.9 %copies.1 = bf16[2304,128]{1,0:T(8,128)(2,1)} custom-call(bf16[80,128]{1,0:T(8,128)(2,1)S(1)} %negative_rows.1.row_ref, bf16[80,128]{1,0:T(8,128)(2,1)S(1)} %collective-permute-done.other_ref.after_ref), custom_call_target="tpu_custom_call" | custom-call | tf_op jit(solution)/shard_map/copies/pallas_call | solution.py:379
  10.2 7.0 %all-to-all-start = ((bf16[16,144,128]{2,1,0:T(8,128)(2,1)}), bf16[16,144,128]{2,1,0:T(8,128)(2,1)S(1)}, u32[]{:S(2)}, u32[]{:S(2)}) async-start(bf16[16,144,128]{2,1,0:T(8,128)(2,1)} %bitcast.1), calls=%async_computation | async-start | bytes 1179648 | tf_op jit(solution)/shard_map/all_to_all | solution.py:387
  17.3 1.6 %pack_positive.1 = (bf16[128,2048]{1,0:T(8,128)(2,1)S(1)}, f32[1,2048]{1,0:T(1,128)S(1)}, f32[1,2048]{1,0:T(1,128)S(1)}) custom-call(s32[1,32]{1,0:T(1,128)S(1)} %copy-done.2, bf16[6144,128]{1,0:T(8,128)(2,1)S(1)} %copy-done.3, s32[48,128]{1,0:T(8,128)S(1)} %bitcast.9, bf16[2048,128]{1,0:T(8,128)(2,1)S(1)} %after.4.value_ref.qp_ref), custom_call_target="tpu_custom_call" | custom-call | flops 10000000000 | tf_op jit(solution)/shard_map/pack_positive/pallas_call | solution.py:364
  18.9 0.8 %copy-done = bf16[128,2048]{1,0:T(8,128)(2,1)} copy-done((bf16[128,2048]{1,0:T(8,128)(2,1)}, bf16[128,2048]{1,0:T(8,128)(2,1)S(1)}, u32[]{:S(2)}) %copy-start) | copy-done | bytes 524312
  19.7 0.8 %collective-permute-done.1.after_ref.refs_1_ = bf16[2048,128]{1,0:T(8,128)(2,1)} collective-permute-done((bf16[2048,128]{1,0:T(8,128)(2,1)S(1)}, bf16[2048,128]{1,0:T(8,128)(2,1)}, u32[]{:S(2)}, u32[]{:S(2)}) %collective-permute-start.1) | collective-permute-done | bytes 524320 | tf_op jit(solution)/shard_map/ppermute | solution.py:324
  21.0 1.3 %place_own.1.refs_2_ = bf16[2048,512]{1,0:T(8,128)(2,1)S(1)} custom-call(bf16[2048,128]{1,0:T(8,128)(2,1)S(1)} %after.5.refs_0_, bf16[2048,128]{1,0:T(8,128)(2,1)} %collective-permute-done.1.after_ref.refs_1_), custom_call_target="tpu_custom_call" | custom-call | tf_op jit(solution)/shard_map/place_own/pallas_call | solution.py:390
  22.3 0.8 %collective-permute-done.2.refs_0_ = bf16[2048,128]{1,0:T(8,128)(2,1)S(1)} collective-permute-done((bf16[2048,128]{1,0:T(8,128)(2,1)S(1)}, bf16[2048,128]{1,0:T(8,128)(2,1)S(1)}, u32[]{:S(2)}, u32[]{:S(2)}) %collective-permute-start.2) | collective-permute-done | bytes 524320 | tf_op jit(solution)/shard_map/ppermute | solution.py:324
  23.6 4.8 %all-to-all-done = bf16[16,144,128]{2,1,0:T(8,128)(2,1)S(1)} async-done(((bf16[16,144,128]{2,1,0:T(8,128)(2,1)}), bf16[16,144,128]{2,1,0:T(8,128)(2,1)S(1)}, u32[]{:S(2)}, u32[]{:S(2)}) %all-to-all-start) | async-done | bytes 589856 | tf_op jit(solution)/shard_map/all_to_all | solution.py:387
  28.3 1.9 %scores.1 = (bf16[512,512]{1,0:T(8,128)(2,1)S(1)}, f32[512,2048]{1,0:T(8,128)S(1)}, f32[4,2048]{1,0:T(4,128)S(1)}) custom-call(bf16[2304,128]{1,0:T(8,128)(2,1)S(1)} %bitcast.6, bf16[2048,512]{1,0:T(8,128)(2,1)S(1)} %place_near.1.qfull_ref.q_ref, f32[1,2048]{1,0:T(1,128)S(1)} %get-tuple-element.21.idp_ref, f32[1,2048]{1,0:T(1,128)S(1)} %get-tuple-element.22.part_ref), custom_call_target="tpu_custom_call" | custom-call | tf_op jit(solution)/shard_map/scores/pallas_call | solution.py:408
  30.3 1.3 %row_products.1 = (f32[256,2048]{1,0:T(8,128)S(1)}, bf16[256,2048]{1,0:T(8,128)(2,1)S(1)}) custom-call(bf16[512,512]{1,0:T(8,128)(2,1)S(1)} %get-tuple-element.26.neg_ref, f32[512,2048]{1,0:T(8,128)S(1)} %get-tuple-element.27.e_ref), custom_call_target="tpu_custom_call" | custom-call | tf_op jit(solution)/shard_map/row_products/pallas_call | solution.py:428
  31.6 0.6 collective-permute-start.5
  32.6 1.9 %collective-permute-done.5.recv_ref = bf16[256,2048]{1,0:T(8,128)(2,1)S(1)} collective-permute-done((bf16[256,2048]{1,0:T(8,128)(2,1)S(1)}, bf16[256,2048]{1,0:T(8,128)(2,1)S(1)}, u32[]{:S(2)}, u32[]{:S(2)}) %collective-permute-start.5) | collective-permute-done | bytes 1048608 | tf_op jit(solution)/shard_map/ppermute | solution.py:324
  34.8 1.4 %collective-permute-start.6 = (bf16[128,2048]{1,0:T(8,128)(2,1)S(1)}, bf16[128,2048]{1,0:T(8,128)(2,1)S(1)}, u32[]{:S(2)}, u32[]{:S(2)}) collective-permute-start(bf16[128,2048]{1,0:T(8,128)(2,1)S(1)} %get-tuple-element.31.after_ref), channel_id=1, source_target_pairs={{0,2},{1,3},{2,0},{3,1},{4,6},{5,7},{6,4},{7,5},{8,10},{9,11},{10,... | collective-permute-start | bytes 1572872 | tf_op jit(solution)/shard_map/ppermute | solution.py:324
  36.2 1.5 %collective-permute-done.7.far = f32[4,2048]{1,0:T(4,128)S(1)} collective-permute-done((f32[4,2048]{1,0:T(4,128)S(1)}, f32[4,2048]{1,0:T(4,128)S(1)}, u32[]{:S(2)}, u32[]{:S(2)}) %collective-permute-start.7) | collective-permute-done | bytes 32800 | tf_op jit(solution)/shard_map/ppermute | solution.py:324
  37.8 1.2 %item_products.1 = bf16[512,512]{1,0:T(8,128)(2,1)S(1)} custom-call(f32[1,2048]{1,0:T(1,128)S(1)} %get-tuple-element.37.scale_ref, f32[512,2048]{1,0:T(8,128)S(1)} %get-tuple-element.27.e_ref, bf16[2048,512]{1,0:T(8,128)(2,1)S(1)} %place_near.1.qfull_ref.q_ref), custom_call_target="tpu_custom_call" | custom-call | tf_op jit(solution)/shard_map/item_products/pallas_call | solution.py:456
  39.0 14.4 %all_to_all.22 = bf16[16,32,512]{2,1,0:T(8,128)(2,1)S(1)} all-to-all(bf16[16,32,512]{2,1,0:T(8,128)(2,1)S(1)} %bitcast.8), channel_id=1, replica_groups=mesh['x'=4,'zl'=2,'y'=4,'grp'=4] {'x','y'}, dimensions={0} | all-to-all | bytes 1048576 | tf_op jit(solution)/shard_map/all_to_all | solution.py:464
  53.5 0.7 %collective-permute-start.8 = (f32[16,512]{1,0:T(8,128)S(1)}, f32[16,512]{1,0:T(8,128)S(1)}, u32[]{:S(2)}, u32[]{:S(2)}) collective-permute-start(f32[16,512]{1,0:T(8,128)S(1)} %after.7), channel_id=1, source_target_pairs={{0,16},{16,0},{1,17},{17,1},{2,18},{18,2},{3,19},{19,3},{4,20},{20... | collective-permute-start | bytes 98312 | tf_op jit(solution)/shard_map/ppermute | solution.py:474
  54.2 2.3 %unpack.1 = bf16[6144,128]{1,0:T(8,128)(2,1)} custom-call(s32[1,32]{1,0:T(1,128)S(1)} %copy-done.2, f32[128,2048]{1,0:T(8,128)S(1)} %get-tuple-element.30.own_ref, bf16[128,2048]{1,0:T(8,128)(2,1)S(1)} %collective-permute-done.6.recv_ref.after_ref, f32[1,2048]{1,0:T(1,128)S(1)} %get-tuple-element.33.near, f32[1,2048]{1,0:T(1,128)S(1)} %get-tuple-element.34.far, ...), custom_call_target="tpu_custom_call" | custom-call | tf_op jit(solution)/shard_map/unpack/pallas_call | solution.py:484
  56.5 1.0 %collective-permute-done.8.recv_ref = f32[16,512]{1,0:T(8,128)S(1)} collective-permute-done((f32[16,512]{1,0:T(8,128)S(1)}, f32[16,512]{1,0:T(8,128)S(1)}, u32[]{:S(2)}, u32[]{:S(2)}) %collective-permute-start.8) | collective-permute-done | bytes 32800 | tf_op jit(solution)/shard_map/ppermute | solution.py:474
  57.5 0.6 %add_neighbour.1 = f32[16,512]{1,0:T(8,128)} custom-call(f32[16,512]{1,0:T(8,128)S(1)} %get-tuple-element.38.own_ref, f32[16,512]{1,0:T(8,128)S(1)} %collective-permute-done.8.recv_ref), custom_call_target="tpu_custom_call" | custom-call | tf_op jit(solution)/shard_map/add_neighbour/pallas_call | solution.py:475
  (26 shorter events, 2.1 us)
Async XLA Ops:
  1.4 15.8 %copy-start.2 = (s32[1,32]{1,0:T(1,128)S(1)}, s32[1,32]{1,0:T(1,128)}, u32[]{:S(2)}) copy-start(s32[1,32]{1,0:T(1,128)} %len_ref.5) | copy-start | bytes 388
  1.4 15.8 %copy-start.3 = (bf16[6144,128]{1,0:T(8,128)(2,1)S(1)}, bf16[6144,128]{1,0:T(8,128)(2,1)}, u32[]{:S(2)}) copy-start(bf16[6144,128]{1,0:T(8,128)(2,1)} %p_ref.1) | copy-start | bytes 4718596
  1.5 15.8 %copy-start.4 = (s32[6144]{0:T(1024)S(1)}, s32[6144]{0:T(1024)}, u32[]{:S(2)}) copy-start(s32[6144]{0:T(1024)} %param.8) | copy-start | bytes 73732
  1.5 3.9 %collective-permute-start = (bf16[80,128]{1,0:T(8,128)(2,1)S(1)}, bf16[80,128]{1,0:T(8,128)(2,1)S(1)}, u32[]{:S(2)}, u32[]{:S(2)}) collective-permute-start(bf16[80,128]{1,0:T(8,128)(2,1)S(1)} %negative_rows.1.row_ref), channel_id=1, source_target_pairs={{0,16},{16,0},{1,17},{17,1},{2,18},{18,2},{3,19},{19,3},{4,20},{20... | collective-permute-start | bytes 61448 | tf_op jit(solution)/shard_map/ppermute | solution.py:347
  5.3 15.2 %collective-permute-start.1 = (bf16[2048,128]{1,0:T(8,128)(2,1)S(1)}, bf16[2048,128]{1,0:T(8,128)(2,1)}, u32[]{:S(2)}, u32[]{:S(2)}) collective-permute-start(bf16[2048,128]{1,0:T(8,128)(2,1)S(1)} %after.4.value_ref.qp_ref), channel_id=1, source_target_pairs={{0,2},{1,3},{2,0},{3,1},{4,6},{5,7},{6,4},{7,5},{8,10},{9,11},{10,... | collective-permute-start | bytes 1572872 | tf_op jit(solution)/shard_map/ppermute | solution.py:324
  10.2 18.2 %all-to-all-start = ((bf16[16,144,128]{2,1,0:T(8,128)(2,1)}), bf16[16,144,128]{2,1,0:T(8,128)(2,1)S(1)}, u32[]{:S(2)}, u32[]{:S(2)}) async-start(bf16[16,144,128]{2,1,0:T(8,128)(2,1)} %bitcast.1), calls=%async_computation | async-start | bytes 1179648 | tf_op jit(solution)/shard_map/all_to_all | solution.py:387
  18.9 0.8 %copy-start = (bf16[128,2048]{1,0:T(8,128)(2,1)}, bf16[128,2048]{1,0:T(8,128)(2,1)S(1)}, u32[]{:S(2)}) copy-start(bf16[128,2048]{1,0:T(8,128)(2,1)S(1)} %get-tuple-element.36.pt_ref) | copy-start | bytes 1572868
  20.5 2.6 %collective-permute-start.2 = (bf16[2048,128]{1,0:T(8,128)(2,1)S(1)}, bf16[2048,128]{1,0:T(8,128)(2,1)S(1)}, u32[]{:S(2)}, u32[]{:S(2)}) collective-permute-start(bf16[2048,128]{1,0:T(8,128)(2,1)S(1)} %after.5.refs_0_), channel_id=1, source_target_pairs={{0,1},{1,0},{2,3},{3,2},{4,5},{5,4},{6,7},{7,6},{8,9},{9,8},{10,11... | collective-permute-start | bytes 1572872 | tf_op jit(solution)/shard_map/ppermute | solution.py:324
  20.5 2.9 %collective-permute-start.3 = (bf16[2048,128]{1,0:T(8,128)(2,1)}, bf16[2048,128]{1,0:T(8,128)(2,1)S(1)}, u32[]{:S(2)}, u32[]{:S(2)}) collective-permute-start(bf16[2048,128]{1,0:T(8,128)(2,1)} %collective-permute-done.1.after_ref.refs_1_), channel_id=1, source_target_pairs={{0,1},{1,0},{2,3},{3,2},{4,5},{5,4},{6,7},{7,6},{8,9},{9,8},{10,11... | collective-permute-start | bytes 1572872 | tf_op jit(solution)/shard_map/ppermute | solution.py:324
  30.2 1.4 %collective-permute-start.4 = (f32[4,2048]{1,0:T(4,128)S(1)}, f32[4,2048]{1,0:T(4,128)S(1)}, u32[]{:S(2)}, u32[]{:S(2)}) collective-permute-start(f32[4,2048]{1,0:T(4,128)S(1)} %get-tuple-element.23.own_ref.own), channel_id=1, source_target_pairs={{0,1},{1,0},{2,3},{3,2},{4,5},{5,4},{6,7},{7,6},{8,9},{9,8},{10,11... | collective-permute-start | bytes 98312 | tf_op jit(solution)/shard_map/ppermute | solution.py:324
  31.6 2.9 %collective-permute-start.5 = (bf16[256,2048]{1,0:T(8,128)(2,1)S(1)}, bf16[256,2048]{1,0:T(8,128)(2,1)S(1)}, u32[]{:S(2)}, u32[]{:S(2)}) collective-permute-start(bf16[256,2048]{1,0:T(8,128)(2,1)S(1)} %after.6), channel_id=1, source_target_pairs={{0,1},{1,0},{2,3},{3,2},{4,5},{5,4},{6,7},{7,6},{8,9},{9,8},{10,11... | collective-permute-start | bytes 3145736 | tf_op jit(solution)/shard_map/ppermute | solution.py:324
  32.2 5.5 %collective-permute-start.7 = (f32[4,2048]{1,0:T(4,128)S(1)}, f32[4,2048]{1,0:T(4,128)S(1)}, u32[]{:S(2)}, u32[]{:S(2)}) collective-permute-start(f32[4,2048]{1,0:T(4,128)S(1)} %get-tuple-element.32.near), channel_id=1, source_target_pairs={{0,2},{1,3},{2,0},{3,1},{4,6},{5,7},{6,4},{7,5},{8,10},{9,11},{10,... | collective-permute-start | bytes 98312 | tf_op jit(solution)/shard_map/ppermute | solution.py:324
  34.8 18.7 %collective-permute-start.6 = (bf16[128,2048]{1,0:T(8,128)(2,1)S(1)}, bf16[128,2048]{1,0:T(8,128)(2,1)S(1)}, u32[]{:S(2)}, u32[]{:S(2)}) collective-permute-start(bf16[128,2048]{1,0:T(8,128)(2,1)S(1)} %get-tuple-element.31.after_ref), channel_id=1, source_target_pairs={{0,2},{1,3},{2,0},{3,1},{4,6},{5,7},{6,4},{7,5},{8,10},{9,11},{10,... | collective-permute-start | bytes 1572872 | tf_op jit(solution)/shard_map/ppermute | solution.py:324
  39.0 15.2 %copy-start.1 = (bf16[128,2048]{1,0:T(8,128)(2,1)S(1)}, bf16[128,2048]{1,0:T(8,128)(2,1)}, u32[]{:S(2)}) copy-start(bf16[128,2048]{1,0:T(8,128)(2,1)} %copy-done) | copy-start | bytes 1572868
  53.5 4.0 %collective-permute-start.8 = (f32[16,512]{1,0:T(8,128)S(1)}, f32[16,512]{1,0:T(8,128)S(1)}, u32[]{:S(2)}, u32[]{:S(2)}) collective-permute-start(f32[16,512]{1,0:T(8,128)S(1)} %after.7), channel_id=1, source_target_pairs={{0,16},{16,0},{1,17},{17,1},{2,18},{18,2},{3,19},{19,3},{4,20},{20... | collective-permute-start | bytes 98312 | tf_op jit(solution)/shard_map/ppermute | solution.py:474

commit v9 on v8

--- a/solution.py
+++ b/solution.py
@@ -89,11 +89,11 @@
             parts = [a + b for a, b in zip(parts[::2], parts[1::2])]
         totals.append(parts[0])
     own_ref[...] = jnp.where(first, totals[0], totals[1])
-    other_ref[...] = jnp.where(first, totals[1], totals[0])
+    other_ref[...] = jnp.where(first, totals[1], totals[0]).astype(BF16)
 
 
 def add_kernel(own_ref, recv_ref, out_ref):
-    out_ref[...] = own_ref[...] + recv_ref[...]
+    out_ref[...] = own_ref[...] + recv_ref[...].astype(F32)
 
 
 def row_kernel(neg_ref, id_ref, out_ref, held_id, sems):
@@ -464,7 +464,7 @@
     shares = lax.all_to_all(items, ("x", "y"), split_axis=0, concat_axis=0, tiled=True)
     own_sum, other_sum = pl.pallas_call(
         sum_kernel,
-        out_shape=(vmem((own_neg, width), F32), vmem((own_neg, width), F32)),
+        out_shape=(vmem((own_neg, width), F32), vmem((own_neg, width), BF16)),
         in_specs=[whole()],
         out_specs=(whole(), whole()),
         compiler_params=params(),

time: 58.5 us -> 58.3 us (level)
  transfers between devices with their start and end apart: 10 -> 10, of which waited for: 8 -> 8; matrix products, arithmetic and copies ran while one was open for 0% -> 0% of each run, Pallas kernels for 18% -> 19%
where the time goes in v9:
time: 58.3 us; the launch traced here: 57.9 us
  starting transfers between devices  16.8 us (29%)
  blocking collectives  14.4 us (25%)
  Pallas kernels  14 us (24%)
  waiting for transfers between devices  11.1 us (19%)
  local copies, waits for them, and re-layouts  0.83 us (1%)
  between operations  0.81 us (1%)
    all_to_all x1, blocking collectives, shards(): lax.all_to_all(items, ('x', 'y'), split_axis=0, concat_axis=0, tiled=True)  14.4 us
    all_to_all x1, starting transfers between devices, shards(): lax.all_to_all(copies, ('x', 'y'), split_axis=0, concat_axis=0, tiled=True)  7.03 us
    ppermute x7, starting transfers between devices, swap(): return lax.ppermute(value, 'grp', [(g, g ^ step) for g in range(groups)])  6.92 us
    ppermute x7, waiting for transfers between devices, swap(): return lax.ppermute(value, 'grp', [(g, g ^ step) for g in range(groups)])  5.32 us
    all_to_all x1, waiting for transfers between devices, shards(): lax.all_to_all(copies, ('x', 'y'), split_axis=0, concat_axis=0, tiled=True)  4.76 us
    pallas_call x1, Pallas kernels, shards(): pl.pallas_call(unpack_kernel, out_shape=jax.ShapeDtypeStruct((slots, LANE...  2.27 us
    ppermute x1, starting transfers between devices, shards(): other = lax.ppermute(row, 'zl', [(i, pair - 1 - i) for i in range(pair)])  2.08 us
    pallas_call x1, Pallas kernels, shards(): pl.pallas_call(scores_kernel, out_shape=(vmem((negs, width), BF16), vmem(...  1.87 us
  transfers between devices with their start and end apart: 10, of which 8 were waited for; matrix products, arithmetic and copies ran while one was open for 0% of the time, Pallas kernels for 19%

profile of v9, /device:TPU:0, one launch (start us, length us, event | category | flops | bytes accessed | tf_op | source)
XLA Modules:
  0.0 57.9 jit_solution(2849174190079747523)
XLA Ops:
  0.6 0.8 %negative_rows.1.row_ref = bf16[80,128]{1,0:T(8,128)(2,1)S(1)} custom-call(bf16[16,512]{1,0:T(8,128)(2,1)} %neg_ref.1, s32[1,16]{1,0:T(1,128)} %bitcast.10), custom_call_target="tpu_custom_call" | custom-call | tf_op jit(solution)/shard_map/negative_rows/pallas_call | solution.py:337
  1.5 2.1 %collective-permute-start = (bf16[80,128]{1,0:T(8,128)(2,1)S(1)}, bf16[80,128]{1,0:T(8,128)(2,1)S(1)}, u32[]{:S(2)}, u32[]{:S(2)}) collective-permute-start(bf16[80,128]{1,0:T(8,128)(2,1)S(1)} %negative_rows.1.row_ref), channel_id=1, source_target_pairs={{0,16},{16,0},{1,17},{17,1},{2,18},{18,2},{3,19},{19,3},{4,20},{20... | collective-permute-start | bytes 61448 | tf_op jit(solution)/shard_map/ppermute | solution.py:347
  3.6 1.5 %pack_query.1.value_ref = bf16[2048,128]{1,0:T(8,128)(2,1)S(1)} custom-call(s32[1,32]{1,0:T(1,128)} %len_ref.5, bf16[6144,128]{1,0:T(8,128)(2,1)} %q_ref.1), custom_call_target="tpu_custom_call" | custom-call | tf_op jit(solution)/shard_map/pack_query/pallas_call | solution.py:348
  5.3 4.0 %collective-permute-start.1 = (bf16[2048,128]{1,0:T(8,128)(2,1)S(1)}, bf16[2048,128]{1,0:T(8,128)(2,1)}, u32[]{:S(2)}, u32[]{:S(2)}) collective-permute-start(bf16[2048,128]{1,0:T(8,128)(2,1)S(1)} %after.4.value_ref.qp_ref), channel_id=1, source_target_pairs={{0,2},{1,3},{2,0},{3,1},{4,6},{5,7},{6,4},{7,5},{8,10},{9,11},{10,... | collective-permute-start | bytes 1572872 | tf_op jit(solution)/shard_map/ppermute | solution.py:324
  9.3 0.9 %copies.1 = bf16[2304,128]{1,0:T(8,128)(2,1)} custom-call(bf16[80,128]{1,0:T(8,128)(2,1)S(1)} %negative_rows.1.row_ref, bf16[80,128]{1,0:T(8,128)(2,1)S(1)} %collective-permute-done.other_ref.after_ref), custom_call_target="tpu_custom_call" | custom-call | tf_op jit(solution)/shard_map/copies/pallas_call | solution.py:379
  10.2 7.0 %all-to-all-start = ((bf16[16,144,128]{2,1,0:T(8,128)(2,1)}), bf16[16,144,128]{2,1,0:T(8,128)(2,1)S(1)}, u32[]{:S(2)}, u32[]{:S(2)}) async-start(bf16[16,144,128]{2,1,0:T(8,128)(2,1)} %bitcast.1), calls=%async_computation | async-start | bytes 1179648 | tf_op jit(solution)/shard_map/all_to_all | solution.py:387
  17.3 1.6 %pack_positive.1 = (bf16[128,2048]{1,0:T(8,128)(2,1)S(1)}, f32[1,2048]{1,0:T(1,128)S(1)}, f32[1,2048]{1,0:T(1,128)S(1)}) custom-call(s32[1,32]{1,0:T(1,128)S(1)} %copy-done.2, bf16[6144,128]{1,0:T(8,128)(2,1)S(1)} %copy-done.3, s32[48,128]{1,0:T(8,128)S(1)} %bitcast.9, bf16[2048,128]{1,0:T(8,128)(2,1)S(1)} %after.4.value_ref.qp_ref), custom_call_target="tpu_custom_call" | custom-call | flops 10000000000 | tf_op jit(solution)/shard_map/pack_positive/pallas_call | solution.py:364
  18.9 0.8 %copy-done = bf16[128,2048]{1,0:T(8,128)(2,1)} copy-done((bf16[128,2048]{1,0:T(8,128)(2,1)}, bf16[128,2048]{1,0:T(8,128)(2,1)S(1)}, u32[]{:S(2)}) %copy-start) | copy-done | bytes 524312
  19.7 0.8 %collective-permute-done.1.after_ref.refs_1_ = bf16[2048,128]{1,0:T(8,128)(2,1)} collective-permute-done((bf16[2048,128]{1,0:T(8,128)(2,1)S(1)}, bf16[2048,128]{1,0:T(8,128)(2,1)}, u32[]{:S(2)}, u32[]{:S(2)}) %collective-permute-start.1) | collective-permute-done | bytes 524320 | tf_op jit(solution)/shard_map/ppermute | solution.py:324
  21.0 1.3 %place_own.1.refs_2_ = bf16[2048,512]{1,0:T(8,128)(2,1)S(1)} custom-call(bf16[2048,128]{1,0:T(8,128)(2,1)S(1)} %after.5.refs_0_, bf16[2048,128]{1,0:T(8,128)(2,1)} %collective-permute-done.1.after_ref.refs_1_), custom_call_target="tpu_custom_call" | custom-call | tf_op jit(solution)/shard_map/place_own/pallas_call | solution.py:390
  22.3 0.8 %collective-permute-done.2.refs_0_ = bf16[2048,128]{1,0:T(8,128)(2,1)S(1)} collective-permute-done((bf16[2048,128]{1,0:T(8,128)(2,1)S(1)}, bf16[2048,128]{1,0:T(8,128)(2,1)S(1)}, u32[]{:S(2)}, u32[]{:S(2)}) %collective-permute-start.2) | collective-permute-done | bytes 524320 | tf_op jit(solution)/shard_map/ppermute | solution.py:324
  23.6 4.8 %all-to-all-done = bf16[16,144,128]{2,1,0:T(8,128)(2,1)S(1)} async-done(((bf16[16,144,128]{2,1,0:T(8,128)(2,1)}), bf16[16,144,128]{2,1,0:T(8,128)(2,1)S(1)}, u32[]{:S(2)}, u32[]{:S(2)}) %all-to-all-start) | async-done | bytes 589856 | tf_op jit(solution)/shard_map/all_to_all | solution.py:387
  28.3 1.9 %scores.1 = (bf16[512,512]{1,0:T(8,128)(2,1)S(1)}, f32[512,2048]{1,0:T(8,128)S(1)}, f32[4,2048]{1,0:T(4,128)S(1)}) custom-call(bf16[2304,128]{1,0:T(8,128)(2,1)S(1)} %bitcast.6, bf16[2048,512]{1,0:T(8,128)(2,1)S(1)} %place_near.1.qfull_ref.q_ref, f32[1,2048]{1,0:T(1,128)S(1)} %get-tuple-element.21.idp_ref, f32[1,2048]{1,0:T(1,128)S(1)} %get-tuple-element.22.part_ref), custom_call_target="tpu_custom_call" | custom-call | tf_op jit(solution)/shard_map/scores/pallas_call | solution.py:408
  30.3 1.3 %row_products.1 = (f32[256,2048]{1,0:T(8,128)S(1)}, bf16[256,2048]{1,0:T(8,128)(2,1)S(1)}) custom-call(bf16[512,512]{1,0:T(8,128)(2,1)S(1)} %get-tuple-element.26.neg_ref, f32[512,2048]{1,0:T(8,128)S(1)} %get-tuple-element.27.e_ref), custom_call_target="tpu_custom_call" | custom-call | tf_op jit(solution)/shard_map/row_products/pallas_call | solution.py:428
  31.6 0.6 collective-permute-start.5
  32.6 1.9 %collective-permute-done.5.recv_ref = bf16[256,2048]{1,0:T(8,128)(2,1)S(1)} collective-permute-done((bf16[256,2048]{1,0:T(8,128)(2,1)S(1)}, bf16[256,2048]{1,0:T(8,128)(2,1)S(1)}, u32[]{:S(2)}, u32[]{:S(2)}) %collective-permute-start.5) | collective-permute-done | bytes 1048608 | tf_op jit(solution)/shard_map/ppermute | solution.py:324
  34.8 1.4 %collective-permute-start.6 = (bf16[128,2048]{1,0:T(8,128)(2,1)S(1)}, bf16[128,2048]{1,0:T(8,128)(2,1)S(1)}, u32[]{:S(2)}, u32[]{:S(2)}) collective-permute-start(bf16[128,2048]{1,0:T(8,128)(2,1)S(1)} %get-tuple-element.31.after_ref), channel_id=1, source_target_pairs={{0,2},{1,3},{2,0},{3,1},{4,6},{5,7},{6,4},{7,5},{8,10},{9,11},{10,... | collective-permute-start | bytes 1572872 | tf_op jit(solution)/shard_map/ppermute | solution.py:324
  36.2 1.5 %collective-permute-done.7.far = f32[4,2048]{1,0:T(4,128)S(1)} collective-permute-done((f32[4,2048]{1,0:T(4,128)S(1)}, f32[4,2048]{1,0:T(4,128)S(1)}, u32[]{:S(2)}, u32[]{:S(2)}) %collective-permute-start.7) | collective-permute-done | bytes 32800 | tf_op jit(solution)/shard_map/ppermute | solution.py:324
  37.8 1.2 %item_products.1 = bf16[512,512]{1,0:T(8,128)(2,1)S(1)} custom-call(f32[1,2048]{1,0:T(1,128)S(1)} %get-tuple-element.37.scale_ref, f32[512,2048]{1,0:T(8,128)S(1)} %get-tuple-element.27.e_ref, bf16[2048,512]{1,0:T(8,128)(2,1)S(1)} %place_near.1.qfull_ref.q_ref), custom_call_target="tpu_custom_call" | custom-call | tf_op jit(solution)/shard_map/item_products/pallas_call | solution.py:456
  39.0 14.4 %all_to_all.22 = bf16[16,32,512]{2,1,0:T(8,128)(2,1)S(1)} all-to-all(bf16[16,32,512]{2,1,0:T(8,128)(2,1)S(1)} %bitcast.8), channel_id=1, replica_groups=mesh['x'=4,'zl'=2,'y'=4,'grp'=4] {'x','y'}, dimensions={0} | all-to-all | bytes 1048576 | tf_op jit(solution)/shard_map/all_to_all | solution.py:464
  53.5 0.7 %collective-permute-start.8 = (bf16[16,512]{1,0:T(8,128)(2,1)S(1)}, bf16[16,512]{1,0:T(8,128)(2,1)S(1)}, u32[]{:S(2)}, u32[]{:S(2)}) collective-permute-start(bf16[16,512]{1,0:T(8,128)(2,1)S(1)} %after.7), channel_id=1, source_target_pairs={{0,16},{16,0},{1,17},{17,1},{2,18},{18,2},{3,19},{19,3},{4,20},{20... | collective-permute-start | bytes 49160 | tf_op jit(solution)/shard_map/ppermute | solution.py:474
  54.2 2.3 %unpack.1 = bf16[6144,128]{1,0:T(8,128)(2,1)} custom-call(s32[1,32]{1,0:T(1,128)S(1)} %copy-done.2, f32[128,2048]{1,0:T(8,128)S(1)} %get-tuple-element.30.own_ref, bf16[128,2048]{1,0:T(8,128)(2,1)S(1)} %collective-permute-done.6.recv_ref.after_ref, f32[1,2048]{1,0:T(1,128)S(1)} %get-tuple-element.33.near, f32[1,2048]{1,0:T(1,128)S(1)} %get-tuple-element.34.far, ...), custom_call_target="tpu_custom_call" | custom-call | tf_op jit(solution)/shard_map/unpack/pallas_call | solution.py:484
  56.5 0.8 %collective-permute-done.8.recv_ref = bf16[16,512]{1,0:T(8,128)(2,1)S(1)} collective-permute-done((bf16[16,512]{1,0:T(8,128)(2,1)S(1)}, bf16[16,512]{1,0:T(8,128)(2,1)S(1)}, u32[]{:S(2)}, u32[]{:S(2)}) %collective-permute-start.8) | collective-permute-done | bytes 16416 | tf_op jit(solution)/shard_map/ppermute | solution.py:474
  57.3 0.6 %add_neighbour.1 = f32[16,512]{1,0:T(8,128)} custom-call(f32[16,512]{1,0:T(8,128)S(1)} %get-tuple-element.38.own_ref, bf16[16,512]{1,0:T(8,128)(2,1)S(1)} %collective-permute-done.8.recv_ref), custom_call_target="tpu_custom_call" | custom-call | tf_op jit(solution)/shard_map/add_neighbour/pallas_call | solution.py:475
  (26 shorter events, 2.1 us)
Async XLA Ops:
  1.4 15.8 %copy-start.2 = (s32[1,32]{1,0:T(1,128)S(1)}, s32[1,32]{1,0:T(1,128)}, u32[]{:S(2)}) copy-start(s32[1,32]{1,0:T(1,128)} %len_ref.5) | copy-start | bytes 388
  1.4 15.8 %copy-start.3 = (bf16[6144,128]{1,0:T(8,128)(2,1)S(1)}, bf16[6144,128]{1,0:T(8,128)(2,1)}, u32[]{:S(2)}) copy-start(bf16[6144,128]{1,0:T(8,128)(2,1)} %p_ref.1) | copy-start | bytes 4718596
  1.5 15.8 %copy-start.4 = (s32[6144]{0:T(1024)S(1)}, s32[6144]{0:T(1024)}, u32[]{:S(2)}) copy-start(s32[6144]{0:T(1024)} %param.8) | copy-start | bytes 73732
  1.5 3.9 %collective-permute-start = (bf16[80,128]{1,0:T(8,128)(2,1)S(1)}, bf16[80,128]{1,0:T(8,128)(2,1)S(1)}, u32[]{:S(2)}, u32[]{:S(2)}) collective-permute-start(bf16[80,128]{1,0:T(8,128)(2,1)S(1)} %negative_rows.1.row_ref), channel_id=1, source_target_pairs={{0,16},{16,0},{1,17},{17,1},{2,18},{18,2},{3,19},{19,3},{4,20},{20... | collective-permute-start | bytes 61448 | tf_op jit(solution)/shard_map/ppermute | solution.py:347
  5.3 15.2 %collective-permute-start.1 = (bf16[2048,128]{1,0:T(8,128)(2,1)S(1)}, bf16[2048,128]{1,0:T(8,128)(2,1)}, u32[]{:S(2)}, u32[]{:S(2)}) collective-permute-start(bf16[2048,128]{1,0:T(8,128)(2,1)S(1)} %after.4.value_ref.qp_ref), channel_id=1, source_target_pairs={{0,2},{1,3},{2,0},{3,1},{4,6},{5,7},{6,4},{7,5},{8,10},{9,11},{10,... | collective-permute-start | bytes 1572872 | tf_op jit(solution)/shard_map/ppermute | solution.py:324
  10.2 18.2 %all-to-all-start = ((bf16[16,144,128]{2,1,0:T(8,128)(2,1)}), bf16[16,144,128]{2,1,0:T(8,128)(2,1)S(1)}, u32[]{:S(2)}, u32[]{:S(2)}) async-start(bf16[16,144,128]{2,1,0:T(8,128)(2,1)} %bitcast.1), calls=%async_computation | async-start | bytes 1179648 | tf_op jit(solution)/shard_map/all_to_all | solution.py:387
  18.9 0.8 %copy-start = (bf16[128,2048]{1,0:T(8,128)(2,1)}, bf16[128,2048]{1,0:T(8,128)(2,1)S(1)}, u32[]{:S(2)}) copy-start(bf16[128,2048]{1,0:T(8,128)(2,1)S(1)} %get-tuple-element.36.pt_ref) | copy-start | bytes 1572868
  20.5 2.6 %collective-permute-start.2 = (bf16[2048,128]{1,0:T(8,128)(2,1)S(1)}, bf16[2048,128]{1,0:T(8,128)(2,1)S(1)}, u32[]{:S(2)}, u32[]{:S(2)}) collective-permute-start(bf16[2048,128]{1,0:T(8,128)(2,1)S(1)} %after.5.refs_0_), channel_id=1, source_target_pairs={{0,1},{1,0},{2,3},{3,2},{4,5},{5,4},{6,7},{7,6},{8,9},{9,8},{10,11... | collective-permute-start | bytes 1572872 | tf_op jit(solution)/shard_map/ppermute | solution.py:324
  20.5 2.9 %collective-permute-start.3 = (bf16[2048,128]{1,0:T(8,128)(2,1)}, bf16[2048,128]{1,0:T(8,128)(2,1)S(1)}, u32[]{:S(2)}, u32[]{:S(2)}) collective-permute-start(bf16[2048,128]{1,0:T(8,128)(2,1)} %collective-permute-done.1.after_ref.refs_1_), channel_id=1, source_target_pairs={{0,1},{1,0},{2,3},{3,2},{4,5},{5,4},{6,7},{7,6},{8,9},{9,8},{10,11... | collective-permute-start | bytes 1572872 | tf_op jit(solution)/shard_map/ppermute | solution.py:324
  30.2 1.4 %collective-permute-start.4 = (f32[4,2048]{1,0:T(4,128)S(1)}, f32[4,2048]{1,0:T(4,128)S(1)}, u32[]{:S(2)}, u32[]{:S(2)}) collective-permute-start(f32[4,2048]{1,0:T(4,128)S(1)} %get-tuple-element.23.own_ref.own), channel_id=1, source_target_pairs={{0,1},{1,0},{2,3},{3,2},{4,5},{5,4},{6,7},{7,6},{8,9},{9,8},{10,11... | collective-permute-start | bytes 98312 | tf_op jit(solution)/shard_map/ppermute | solution.py:324
  31.6 2.9 %collective-permute-start.5 = (bf16[256,2048]{1,0:T(8,128)(2,1)S(1)}, bf16[256,2048]{1,0:T(8,128)(2,1)S(1)}, u32[]{:S(2)}, u32[]{:S(2)}) collective-permute-start(bf16[256,2048]{1,0:T(8,128)(2,1)S(1)} %after.6), channel_id=1, source_target_pairs={{0,1},{1,0},{2,3},{3,2},{4,5},{5,4},{6,7},{7,6},{8,9},{9,8},{10,11... | collective-permute-start | bytes 3145736 | tf_op jit(solution)/shard_map/ppermute | solution.py:324
  32.2 5.5 %collective-permute-start.7 = (f32[4,2048]{1,0:T(4,128)S(1)}, f32[4,2048]{1,0:T(4,128)S(1)}, u32[]{:S(2)}, u32[]{:S(2)}) collective-permute-start(f32[4,2048]{1,0:T(4,128)S(1)} %get-tuple-element.32.near), channel_id=1, source_target_pairs={{0,2},{1,3},{2,0},{3,1},{4,6},{5,7},{6,4},{7,5},{8,10},{9,11},{10,... | collective-permute-start | bytes 98312 | tf_op jit(solution)/shard_map/ppermute | solution.py:324
  34.8 18.7 %collective-permute-start.6 = (bf16[128,2048]{1,0:T(8,128)(2,1)S(1)}, bf16[128,2048]{1,0:T(8,128)(2,1)S(1)}, u32[]{:S(2)}, u32[]{:S(2)}) collective-permute-start(bf16[128,2048]{1,0:T(8,128)(2,1)S(1)} %get-tuple-element.31.after_ref), channel_id=1, source_target_pairs={{0,2},{1,3},{2,0},{3,1},{4,6},{5,7},{6,4},{7,5},{8,10},{9,11},{10,... | collective-permute-start | bytes 1572872 | tf_op jit(solution)/shard_map/ppermute | solution.py:324
  39.0 15.2 %copy-start.1 = (bf16[128,2048]{1,0:T(8,128)(2,1)S(1)}, bf16[128,2048]{1,0:T(8,128)(2,1)}, u32[]{:S(2)}) copy-start(bf16[128,2048]{1,0:T(8,128)(2,1)} %copy-done) | copy-start | bytes 1572868
  53.5 3.8 %collective-permute-start.8 = (bf16[16,512]{1,0:T(8,128)(2,1)S(1)}, bf16[16,512]{1,0:T(8,128)(2,1)S(1)}, u32[]{:S(2)}, u32[]{:S(2)}) collective-permute-start(bf16[16,512]{1,0:T(8,128)(2,1)S(1)} %after.7), channel_id=1, source_target_pairs={{0,16},{16,0},{1,17},{17,1},{2,18},{18,2},{3,19},{19,3},{4,20},{20... | collective-permute-start | bytes 49160 | tf_op jit(solution)/shard_map/ppermute | solution.py:474
